TPU v7x, 32 devices: a whole 2x2x4 slice. The times are simulated.
32 devices in a mesh: dp: 4 (over x, core), fsdp: 8 (over z, y).
Axes of the slice: x: 2, y: 2, z: 4, core: 2. Of those that a mesh axis runs over, the one named last changes fastest.
Arguments:
- hidden: bfloat16 [4096, 8192], P(('dp', 'fsdp')), may hold values from -6 to 6
- d_attn: bfloat16 [4096, 1024], P(('dp', 'fsdp')), may hold values from -24 to 24
- w_query: bfloat16 [8192, 1024], P('fsdp'), may hold values from -0.0625 to 0.0625
- w_key: bfloat16 [8192, 128], P('fsdp'), may hold values from -0.0625 to 0.0625
- w_value: bfloat16 [8192, 128], P('fsdp'), may hold values from -0.0625 to 0.0625
- cache_keys: bfloat16 [2048, 128], P('fsdp'), may hold values from -700 to 700
- cache_values: bfloat16 [2048, 128], P('fsdp'), may hold values from -6 to 6
- lengths: int32 [4, 4], P('dp'), may hold values from 1 to 768, 1024 in all within a row
Outputs:
- grad_keys: float32 [2048, 128], P('fsdp')
- grad_values: float32 [2048, 128], P('fsdp')
Inputs may be any that keep to these rules, and one draw needn't show every extreme that they name: `lengths`: each row sums to 1024 and its longest conversation has exactly 768 tokens.
All inputs are finite; a program needn't handle non-finite values.
Results may differ from a plain program's by a relative error of at most 0.0075.
The roundings to bfloat16 on the way count: a program that leaves them out, or rounds other values in their place, can miss the bound.
Values may be sent and summed in bfloat16 or wider, within the bound.
No kernel may reach another device: no remote copies, remote signals or barrier semaphores. Data moves between devices by JAX's collectives and lax.ppermute only.
A program may use at most 128 MiB of HBM per device.

v0:
```python
import functools
import math

import jax
import jax.numpy as jnp
from jax import lax
from jax.experimental import pallas as pl
from jax.experimental.pallas import tpu as pltpu
from jax.sharding import PartitionSpec as P

F32 = jnp.float32
BF16 = jnp.bfloat16
VMEM_LIMIT = 56 * 1024 * 1024


def swap(value, axis, size, bit):
    return lax.ppermute(value, axis, [(i, i ^ bit) for i in range(size)])


def bits_down(size):
    bits = []
    bit = size // 2
    while bit:
        bits.append(bit)
        bit //= 2
    return bits


def double(block, order, axis, size, bit):
    return jnp.concatenate([block, swap(block, axis, size, bit)]), order + [o ^ bit for o in order]


def finish(block, order, axis, size, bits):
    for bit in bits[:-1]:
        block, order = double(block, order, axis, size, bit)
    return [block, swap(block, axis, size, bits[-1])], order + [o ^ bits[-1] for o in order]


def together(*values):
    return lax.optimization_barrier(values)


def params():
    return pltpu.CompilerParams(vmem_limit_bytes=VMEM_LIMIT)


def run_copies(copies):
    for copy in copies:
        copy.start()
    for copy in copies:
        copy.wait()


def prepare(hidden, w_query, w_key, w_value, n_dp, n_fsdp):
    inner = n_fsdp // 2
    tokens = hidden.shape[0]
    rows_w, q_width = w_query.shape
    head_dim = w_key.shape[1]
    share = rows_w // n_dp
    cols = q_width // 2

    def body(hidden_ref, wq_ref, wk_ref, wv_ref, *rest):
        sent, part, sems = rest[: inner - 1], rest[-2], rest[-1]
        me, dp = lax.axis_index("fsdp"), lax.axis_index("dp")
        first = pl.multiple_of(dp * share, 16)
        rows = pl.ds(first, share)
        pairs = []
        for i in range(2):
            to = part.at[pl.ds(i * (share + share // 2), share)]
            pairs.append((wq_ref.at[rows, pl.ds(i * cols, cols)], to))
            for j, ref in enumerate((wk_ref, wv_ref)):
                to = part.at[pl.ds(share, share // 2), pl.ds((2 * i + j) * head_dim, head_dim)]
                pairs.append((ref.at[pl.ds(first + i * (share // 2), share // 2)], to))
        for k in range(1, inner):
            for side, bit in enumerate((0, inner)):
                start = pl.multiple_of((me ^ k ^ bit) * rows_w, 128)
                pairs.append(
                    (hidden_ref.at[:, pl.ds(start, rows_w)], sent[k - 1].at[:, pl.ds(side * rows_w, rows_w)])
                )
        run_copies([pltpu.make_async_copy(a, b, sems.at[i]) for i, (a, b) in enumerate(pairs)])

    moved = 2 * (tokens * 2 * rows_w * 2 * (inner - 1) + share * (q_width + 2 * head_dim) * 2)
    out = pl.pallas_call(
        body,
        in_specs=[pl.BlockSpec(memory_space=pl.ANY)] * 4,
        out_specs=[pl.BlockSpec(memory_space=pltpu.VMEM)] * inner,
        out_shape=[jax.ShapeDtypeStruct((tokens, 2 * rows_w), BF16)] * (inner - 1)
        + [jax.ShapeDtypeStruct((2 * share + share // 2, cols), BF16)],
        scratch_shapes=[pltpu.SemaphoreType.DMA((6 + 2 * (inner - 1),))],
        compiler_params=params(),
        cost_estimate=pl.CostEstimate(flops=0, bytes_accessed=moved, transcendentals=0),
        name="prepare",
    )(hidden, w_query, w_key, w_value)
    return out[:-1], out[-1]


def multiply(hidden, received, near, far, layout, order, n_fsdp, groups):
    inner = n_fsdp // 2
    tokens = hidden.shape[0]
    cols = sum(wide for _, _, wide in near)
    slots = far[0].shape[0]
    n_dp = slots * len(far)
    rows_w = near[0][0].shape[0]
    share = rows_w // n_dp
    step = 256 if all(g % 256 == 0 for g in groups) else 128
    n_in = inner - 1 + len(near) + len(far)

    def body(hidden_ref, *rest):
        blocks, rest = rest[: inner - 1], rest[inner - 1 :]
        near_refs, rest = rest[: len(near)], rest[len(near) :]
        far_refs, rest = rest[: len(far)], rest[len(far) :]
        outs = rest[:-3]
        x_all, w_all, sems = rest[-3:]
        me, dp = lax.axis_index("fsdp"), lax.axis_index("dp")
        pairs = []
        for side, bit in enumerate((0, inner)):
            start = pl.multiple_of((me ^ bit) * rows_w, 128)
            pairs.append(
                (
                    hidden_ref.at[:, pl.ds(start, rows_w)],
                    x_all.at[pl.ds(0, tokens), pl.ds(side * rows_w, rows_w)],
                )
            )
        for k in range(1, inner):
            pairs.append((blocks[k - 1], x_all.at[pl.ds(k * tokens, tokens)]))
        to = 0
        for ref, (_, start, wide) in zip(near_refs, near):
            pairs.append((ref.at[:, pl.ds(start, wide)], w_all.at[pl.ds(0, rows_w), pl.ds(to, wide)]))
            to += wide
        for slot, o in enumerate(order):
            block = far_refs[slot // slots].at[slot % slots]
            for row, col, rows, wide, to_row, to_col in layout:
                to = pl.multiple_of(rows_w + (dp ^ o) * share + to_row, 16)
                piece = block.at[pl.ds(row, rows), pl.ds(col, wide)]
                pairs.append((piece, w_all.at[pl.ds(to, rows), pl.ds(to_col, wide)]))
        run_copies([pltpu.make_async_copy(a, b, sems.at[i]) for i, (a, b) in enumerate(pairs)])

        base = 0
        for g, wide in enumerate(groups):

            @pl.loop(0, wide // step)
            def _(n, g=g, base=base):
                at = pl.multiple_of(n * step, 128)
                product = jnp.dot(
                    x_all[...], w_all[:, pl.ds(base + at, step)], preferred_element_type=F32
                )
                for k in range(inner):
                    outs[g * inner + k][:, pl.ds(at, step)] = product[k * tokens : (k + 1) * tokens]

            base += wide

    copies = 2 + (inner - 1) + len(near) + n_dp * len(layout)
    moved = inner * tokens * 2 * rows_w * 2 + 2 * rows_w * cols * 2 + inner * tokens * cols * 4
    out = pl.pallas_call(
        body,
        in_specs=[pl.BlockSpec(memory_space=pl.ANY)] * (1 + n_in),
        out_specs=[pl.BlockSpec(memory_space=pltpu.VMEM)] * (inner * len(groups)),
        out_shape=[jax.ShapeDtypeStruct((tokens, g), F32) for g in groups for _ in range(inner)],
        scratch_shapes=[
            pltpu.VMEM((inner * tokens, 2 * rows_w), BF16),
            pltpu.VMEM((2 * rows_w, cols), BF16),
            pltpu.SemaphoreType.DMA((copies,)),
        ],
        compiler_params=params(),
        cost_estimate=pl.CostEstimate(
            flops=2 * inner * tokens * 2 * rows_w * cols, bytes_accessed=moved, transcendentals=0
        ),
        name="multiply",
    )(hidden, *received, *[array for array, _, _ in near], *far)
    return [list(out[g * inner : (g + 1) * inner]) for g in range(len(groups))]


def attend(lengths, terms, d_attn, first_head, cache, group, g_order, sums):
    tokens = d_attn.shape[0]
    n_blocks, block, head_dim = cache[0].shape
    slots = n_blocks // len(group)
    n_convs = lengths.shape[1]
    scale = head_dim ** (-0.5)
    to_log2 = scale * math.log2(math.e)
    n_heads = terms[0].shape[1] // head_dim
    pair = 2 if n_heads % 2 == 0 else 1
    lanes = pair * tokens
    n_cache = n_blocks * block
    n_group = n_blocks * tokens
    chunk = 512
    n_part, n_sum = len(terms), len(sums)

    def body(len_ref, d_ref, *rest):
        cache_refs, rest = rest[:2], rest[2:]
        group_refs, rest = rest[: len(group)], rest[len(group) :]
        part_refs, rest = rest[:n_part], rest[n_part:]
        sum_refs, rest = rest[:n_sum], rest[n_sum:]
        keep_ref, give_ref, gk, gv, s_ref, p_ref, q_ref, ck_ref, cv_ref, sems = rest
        me, dp = lax.axis_index("fsdp"), lax.axis_index("dp")
        even = dp % 2 == 0

        @pl.when(even)
        def _():
            pltpu.make_async_copy(cache_refs[0], ck_ref, sems.at[0]).start()
            pltpu.make_async_copy(cache_refs[1], cv_ref, sems.at[1]).start()

        @pl.when(jnp.logical_not(even))
        def _():
            pltpu.make_async_copy(cache_refs[1], ck_ref, sems.at[0]).start()
            pltpu.make_async_copy(cache_refs[0], cv_ref, sems.at[1]).start()

        for h in range(n_heads):
            at = slice(h * head_dim, (h + 1) * head_dim)
            q = part_refs[0][:, at]
            for ref in part_refs[1:]:
                q = q + ref[:, at]
            q_ref[h, 0] = q.astype(BF16)
            at = (first_head + h) * head_dim
            q_ref[h, 1] = d_ref[:, at : at + head_dim]

        q_pos = me * tokens + lax.broadcasted_iota(jnp.int32, (1, lanes), 1) % tokens
        begin = jnp.zeros((1, lanes), jnp.int32)
        end = jnp.int32(0)
        for i in range(n_convs):
            end = end + len_ref[0, i]
            begin = jnp.where(end <= q_pos, end, begin)

        pltpu.make_async_copy(cache_refs[0], ck_ref, sems.at[0]).wait()
        pltpu.make_async_copy(cache_refs[1], cv_ref, sems.at[1]).wait()

        @pl.loop(0, n_heads // pair)
        def _(step):
            rows_q = jnp.concatenate([q_ref[step * pair + i, 0] for i in range(pair)], axis=0)
            rows_d = jnp.concatenate([q_ref[step * pair + i, 1] for i in range(pair)], axis=0)
            dims = (((1,), (1,)), ((), ()))
            top = jnp.full((1, lanes), -jnp.inf, F32)
            cache_spans = [
                (b, r, min(chunk, block)) for b in range(n_blocks) for r in range(0, block, min(chunk, block))
            ]
            for b, r, size in cache_spans:
                s = lax.dot_general(
                    ck_ref[b, r : r + size], rows_q, dims, preferred_element_type=F32
                )
                s_ref[pl.ds(b * block + r, size)] = s
                top = jnp.maximum(top, jnp.max(s, axis=0, keepdims=True))
            for b in range(n_blocks):
                s = lax.dot_general(group_refs[b // slots][b % slots, :, :head_dim], rows_q, dims, preferred_element_type=F32)
                pos = (me ^ g_order[b]) * tokens + lax.broadcasted_iota(jnp.int32, (tokens, lanes), 0)
                s = jnp.where((pos <= q_pos) & (pos >= begin), s, -jnp.inf)
                s_ref[pl.ds(n_cache + b * tokens, tokens)] = s
                top = jnp.maximum(top, jnp.max(s, axis=0, keepdims=True))
            total = jnp.zeros((1, lanes), F32)
            for r in range(0, n_cache + n_group, chunk):
                e = jnp.exp2((s_ref[pl.ds(r, chunk)] - top) * to_log2)
                s_ref[pl.ds(r, chunk)] = e
                total = total + jnp.sum(e, axis=0, keepdims=True)
            inv = 1.0 / total
            delta = jnp.zeros((1, lanes), F32)
            for b in range(n_blocks):
                p = s_ref[pl.ds(n_cache + b * tokens, tokens)] * inv
                dp_ = lax.dot_general(group_refs[b // slots][b % slots, :, head_dim:], rows_d, dims, preferred_element_type=F32)
                delta = delta + jnp.sum(p.astype(BF16).astype(F32) * dp_, axis=0, keepdims=True)
            for b, r, size in cache_spans:
                at = pl.ds(b * block + r, size)
                p = s_ref[at] * inv
                pb = p.astype(BF16)
                dp_ = lax.dot_general(
                    cv_ref[b, r : r + size], rows_d, dims, preferred_element_type=F32
                )
                s_ref[at] = p
                p_ref[at] = dp_
                delta = delta + jnp.sum(pb.astype(F32) * dp_, axis=0, keepdims=True)
                g = jnp.dot(pb, rows_d, preferred_element_type=F32)
                gv[at] = jnp.where(step == 0, 0.0, gv[at]) + g
            for b, r, size in cache_spans:
                at = pl.ds(b * block + r, size)
                ds = (s_ref[at] * (p_ref[at] - delta)).astype(BF16)
                g = jnp.dot(ds, rows_q, preferred_element_type=F32)
                gk[at] = jnp.where(step == 0, 0.0, gk[at]) + g

        keep_in, give_in = (sum_refs[0][...], sum_refs[1][...]) if n_sum else (0.0, 0.0)

        @pl.when(even)
        def _():
            keep_ref[...] = keep_in + gk[...] * scale
            give_ref[...] = give_in + gv[...]

        @pl.when(jnp.logical_not(even))
        def _():
            keep_ref[...] = keep_in + gv[...]
            give_ref[...] = give_in + gk[...] * scale

    rows = n_heads * tokens
    flops = 2 * rows * head_dim * (5 * n_cache + 2 * n_group)
    return pl.pallas_call(
        body,
        in_specs=[pl.BlockSpec(memory_space=pltpu.SMEM)]
        + [pl.BlockSpec(memory_space=pltpu.VMEM)]
        + [pl.BlockSpec(memory_space=pl.ANY)] * 2
        + [pl.BlockSpec(memory_space=pltpu.VMEM)] * (len(group) + n_part + n_sum),
        out_specs=[pl.BlockSpec(memory_space=pltpu.VMEM)] * 2,
        out_shape=[jax.ShapeDtypeStruct((n_cache, head_dim), F32)] * 2,
        scratch_shapes=[
            pltpu.VMEM((n_cache, head_dim), F32),
            pltpu.VMEM((n_cache, head_dim), F32),
            pltpu.VMEM((n_cache + n_group, lanes), F32),
            pltpu.VMEM((n_cache, lanes), F32),
            pltpu.VMEM((n_heads, 2, tokens, head_dim), BF16),
            pltpu.VMEM((n_blocks, block, head_dim), BF16),
            pltpu.VMEM((n_blocks, block, head_dim), BF16),
            pltpu.SemaphoreType.DMA((2,)),
        ],
        compiler_params=params(),
        cost_estimate=pl.CostEstimate(
            flops=flops,
            bytes_accessed=12 * n_cache * head_dim,
            transcendentals=rows * (n_cache + n_group),
        ),
        name="attend",
    )(lengths, d_attn, *cache, *group, *terms, *sums)


def make_on_device(n_dp, n_fsdp):
    inner = n_fsdp // 2

    def on_device(hidden, d_attn, w_query, w_key, w_value, cache_keys, cache_values, lengths):
        dp = lax.axis_index("dp")
        head_dim = w_key.shape[1]
        q_width = w_query.shape[1]
        even = dp % 2 == 0
        f_bits, d_bits = bits_down(n_fsdp), bits_down(n_dp)

        def from_owners(products):
            return [products[0]] + [swap(x, "fsdp", n_fsdp, k + 1) for k, x in enumerate(products[1:])]

        cuts = [(0, q_width // 2), (q_width // 2, q_width // 2)]
        cuts = [(0, q_width // 2), (q_width // 2, q_width // 2)]
        sent, part = prepare(hidden, w_query, w_key, w_value, n_dp, n_fsdp)
        received = [swap(block, "fsdp", n_fsdp, k + 1) for k, block in enumerate(sent)]
        part = swap(part, "fsdp", n_fsdp, inner)
        share = w_query.shape[0] // n_dp
        cut = share + share // 2
        part_a, part_b = part[:cut], part[cut:]
        far_a, order = double(part_a[None], [0], "dp", n_dp, d_bits[0])
        cache = jnp.where(even, cache_keys, cache_values)[None]
        cache, f_order = double(cache, [0], "fsdp", n_fsdp, f_bits[0])
        cache, far_a, *received = together(cache, far_a, *received)
        far_b, _ = double(part_b[None], [0], "dp", n_dp, d_bits[0])
        far_a, d_order = finish(far_a, order, "dp", n_dp, d_bits[1:])
        kv, (at_a, wide_a), (at_b, wide_b) = 2 * head_dim, *cuts
        near_a = [(w_key, 0, head_dim), (w_value, 0, head_dim), (w_query, at_a, wide_a)]
        layout_a = [(0, 0, share, wide_a, 0, kv)]
        layout_a += [(share, i * kv, share // 2, kv, i * (share // 2), 0) for i in range(2)]
        out_kv, out_a = multiply(
            hidden, received, near_a, far_a, layout_a, d_order, n_fsdp, (kv, wide_a)
        )
        cache, f_order = double(cache, f_order, "fsdp", n_fsdp, f_bits[1])
        far_b, cache, out_kv[0] = together(far_b, cache, out_kv[0])
        far_b, _ = finish(far_b, order, "dp", n_dp, d_bits[1:])
        for bit in f_bits[2:]:
            cache, f_order = double(cache, f_order, "fsdp", n_fsdp, bit)
        parts_kv = from_owners(out_kv)
        parts_a = from_owners(out_a)
        near_b, layout_b = [(w_query, at_b, wide_b)], [(0, 0, share, wide_b, 0, 0)]
        (out_b,) = multiply(
            hidden, received, near_b, far_b, layout_b, d_order, n_fsdp, (wide_b,)
        )
        out_b[0], cache, *parts_kv = together(out_b[0], cache, *parts_kv)
        own = functools.reduce(lambda a, b: a + b, parts_kv).astype(BF16)
        group = [own] + [swap(own, "fsdp", n_fsdp, k) for k in range(1, inner)]
        cache, *tied = together(cache, *out_b, *group, *parts_a)
        out_b, group, parts_a = tied[:inner], tied[inner : 2 * inner], tied[2 * inner :]
        g_order = [o for o in f_order if o < inner]
        group = jnp.stack([group[o] for o in g_order])
        group, g_order = finish(group, g_order, "fsdp", n_fsdp, [inner])
        parts_b = from_owners(out_b)
        cache = (cache, swap(cache, "dp", n_dp, 1))
        first = cuts[0][1] // head_dim
        sums = attend(lengths, parts_a, d_attn, 0, cache, group, g_order, ())
        keep, give = attend(lengths, parts_b, d_attn, first, cache, group, g_order, sums)

        half = keep + swap(give, "dp", n_dp, 1)
        size = half.shape[0] // n_fsdp
        mine = half[:size]
        for slot in range(1, n_fsdp):
            out = half[slot * size : (slot + 1) * size].astype(BF16)
            mine = mine + swap(out, "fsdp", n_fsdp, f_order[slot]).astype(F32)
        for bit in bits_down(n_dp)[:-2]:
            mine = mine + swap(mine, "dp", n_dp, bit)
        beside, other, across = (swap(mine, "dp", n_dp, bit) for bit in (2, 1, 3))
        mine = mine + beside
        other = other + across
        return jnp.where(even, mine, other), jnp.where(even, other, mine)

    return on_device


def solution(mesh):
    placed = (
        P(("dp", "fsdp"), None),
        P(("dp", "fsdp"), None),
        P("fsdp", None),
        P("fsdp", None),
        P("fsdp", None),
        P("fsdp", None),
        P("fsdp", None),
        P("dp", None),
    )
    return jax.shard_map(
        make_on_device(mesh.shape["dp"], mesh.shape["fsdp"]),
        mesh=mesh,
        in_specs=placed,
        out_specs=(P("fsdp", None), P("fsdp", None)),
        check_vma=False,
    )
```

profile of v0, /device:TPU:0, one launch (start us, length us, event | category | flops | bytes accessed | tf_op | source)
XLA Modules:
  0.0 160.5 jit_solution(5334998724897140670)
XLA Ops:
  0.6 3.1 %prepare.1 = (bf16[128,2048]{1,0:T(8,128)(2,1)}, bf16[128,2048]{1,0:T(8,128)(2,1)}, bf16[128,2048]{1,0:T(8,128)(2,1)}, bf16[640,512]{1,0:T(8,128)(2,1)}) custom-call(bf16[128,8192]{1,0:T(8,128)(2,1)} %hidden_ref.5, bf16[1024,1024]{1,0:T(8,128)(2,1)} %rest_3_.3, bf16[1024,128]{1,0:T(8,128)(2,1)} %rest_3_.2, bf16[1024,128]{1,0:T(8,128)(2,1)} %rest_4_.1), custom_call_target="tpu_custom_call" | custom-call | bytes 4456448 | tf_op jit(solution)/shard_map/prepare/pallas_call | solution.py:83
  3.8 4.1 %collective-permute-start.1 = (bf16[640,512]{1,0:T(8,128)(2,1)}, bf16[640,512]{1,0:T(8,128)(2,1)S(1)}, u32[]{:S(2)}, u32[]{:S(2)}) collective-permute-start(bf16[640,512]{1,0:T(8,128)(2,1)} %get-tuple-element.49), channel_id=1, source_target_pairs={{0,4},{1,5},{2,6},{3,7},{4,0},{5,1},{6,2},{7,3},{8,12},{9,13},{10,... | collective-permute-start | bytes 1966088 | tf_op jit(solution)/shard_map/ppermute | solution.py:17
  11.3 25.6 %collective-permute-done.1 = bf16[640,512]{1,0:T(8,128)(2,1)S(1)} collective-permute-done((bf16[640,512]{1,0:T(8,128)(2,1)}, bf16[640,512]{1,0:T(8,128)(2,1)S(1)}, u32[]{:S(2)}, u32[]{:S(2)}) %collective-permute-start.1) | collective-permute-done | bytes 655392 | tf_op jit(solution)/shard_map/ppermute | solution.py:17
  37.0 1.6 %collective-permute-start.2 = (bf16[1,384,512]{2,1,0:T(8,128)(2,1)S(1)}, bf16[1,384,512]{2,1,0:T(8,128)(2,1)S(1)}, u32[]{:S(2)}, u32[]{:S(2)}) collective-permute-start(bf16[1,384,512]{2,1,0:T(8,128)(2,1)S(1)} %slice_bitcast_fusion), channel_id=1, source_target_pairs={{0,16},{8,24},{16,0},{24,8},{1,17},{9,25},{17,1},{25,9},{2,18},{10... | collective-permute-start | bytes 1179656 | tf_op jit(solution)/shard_map/ppermute | solution.py:17
  38.7 7.3 %collective-permute-done = bf16[1,256,128]{2,1,0:T(8,128)(2,1)S(1)} collective-permute-done((bf16[1,256,128]{2,1,0:T(8,128)(2,1)S(1)}, bf16[1,256,128]{2,1,0:T(8,128)(2,1)S(1)}, u32[]{:S(2)}, u32[]{:S(2)}) %collective-permute-start) | collective-permute-done | bytes 65568 | tf_op jit(solution)/shard_map/ppermute | solution.py:17
  50.7 6.4 %collective-permute-done.6 = bf16[1,256,512]{2,1,0:T(8,128)(2,1)S(1)} collective-permute-done((bf16[1,256,512]{2,1,0:T(8,128)(2,1)S(1)}, bf16[1,256,512]{2,1,0:T(8,128)(2,1)S(1)}, u32[]{:S(2)}, u32[]{:S(2)}) %collective-permute-start.6) | collective-permute-done | bytes 262176 | tf_op jit(solution)/shard_map/ppermute | solution.py:17
  58.1 5.7 %multiply.2 = (f32[128,256]{1,0:T(8,128)}, f32[128,256]{1,0:T(8,128)}, f32[128,256]{1,0:T(8,128)}, f32[128,256]{1,0:T(8,128)}, f32[128,512]{1,0:T(8,128)}, /*ind...) custom-call(bf16[128,8192]{1,0:T(8,128)(2,1)} %hidden_ref.5, bf16[128,2048]{1,0:T(8,128)(2,1)} %copy-done.2, ...), custom_call_target="tpu_custom_call" | custom-call | flops 1610612736 | bytes 6815744 | tf_op jit(solution)/shard_map/multiply/pallas_call | solution.py:154
  66.9 2.0 %collective-permute-start.13 = (f32[128,256]{1,0:T(8,128)}, f32[128,256]{1,0:T(8,128)S(1)}, u32[]{:S(2)}, u32[]{:S(2)}) collective-permute-start(f32[128,256]{1,0:T(8,128)} %get-tuple-element.65), channel_id=1, source_target_pairs={{0,3},{1,2},{2,1},{3,0},{4,7},{5,6},{6,5},{7,4},{8,11},{9,10},{10,... | collective-permute-start | bytes 393224 | tf_op jit(solution)/shard_map/ppermute | solution.py:17
  68.9 7.0 %collective-permute-done.10 = bf16[4,256,128]{2,1,0:T(8,128)(2,1)S(1)} collective-permute-done((bf16[4,256,128]{2,1,0:T(8,128)(2,1)S(1)}, bf16[4,256,128]{2,1,0:T(8,128)(2,1)S(1)}, u32[]{:S(2)}, u32[]{:S(2)}) %collective-permute-start.10) | collective-permute-done | bytes 262176 | tf_op jit(solution)/shard_map/ppermute | solution.py:17
  78.4 4.5 %multiply.3 = (f32[128,512]{1,0:T(8,128)}, f32[128,512]{1,0:T(8,128)}, f32[128,512]{1,0:T(8,128)}, f32[128,512]{1,0:T(8,128)}) custom-call(bf16[128,8192]{1,0:T(8,128)(2,1)} %hidden_ref.5, bf16[128,2048]{1,0:T(8,128)(2,1)} %copy-done.2, bf16[128,2048]{1,0:T(8,128)(2,1)} %copy-done.3, bf16[128,2048]{1,0:T(8,128)(2,1)} %copy-done.4, ...), custom_call_target="tpu_custom_call" | custom-call | flops 1073741824 | bytes 5242880 | tf_op jit(solution)/shard_map/multiply/pallas_call | solution.py:154
  84.2 1.9 %collective-permute-start.16 = (bf16[128,256]{1,0:T(8,128)(2,1)S(1)}, bf16[128,256]{1,0:T(8,128)(2,1)S(1)}, u32[]{:S(2)}, u32[]{:S(2)}) collective-permute-start(bf16[128,256]{1,0:T(8,128)(2,1)S(1)} %add_convert_fusion), channel_id=1, source_target_pairs={{0,3},{1,2},{2,1},{3,0},{4,7},{5,6},{6,5},{7,4},{8,11},{9,10},{10,... | collective-permute-start | bytes 196616 | tf_op jit(solution)/shard_map/ppermute | solution.py:17
  87.8 4.6 %collective-permute-done.19.rest_7_ = f32[128,512]{1,0:T(8,128)S(1)} collective-permute-done((f32[128,512]{1,0:T(8,128)S(1)}, f32[128,512]{1,0:T(8,128)S(1)}, u32[]{:S(2)}, u32[]{:S(2)}) %collective-permute-start.19) | collective-permute-done | bytes 262176 | tf_op jit(solution)/shard_map/ppermute | solution.py:17
  93.8 3.2 %collective-permute-start.21 = (bf16[4,128,256]{2,1,0:T(8,128)(2,1)S(1)}, bf16[4,128,256]{2,1,0:T(8,128)(2,1)S(1)}, u32[]{:S(2)}, u32[]{:S(2)}) collective-permute-start(bf16[4,128,256]{2,1,0:T(8,128)(2,1)S(1)} %pad_maximum_fusion.4.rest_2_), channel_id=1, source_target_pairs={{0,4},{1,5},{2,6},{3,7},{4,0},{5,1},{6,2},{7,3},{8,12},{9,13},{10,... | collective-permute-start | bytes 786440 | tf_op jit(solution)/shard_map/ppermute | solution.py:17
  100.5 9.2 %collective-permute-done.21.rest_3_ = bf16[4,128,256]{2,1,0:T(8,128)(2,1)S(1)} collective-permute-done((bf16[4,128,256]{2,1,0:T(8,128)(2,1)S(1)}, bf16[4,128,256]{2,1,0:T(8,128)(2,1)S(1)}, u32[]{:S(2)}, u32[]{:S(2)}) %collective-permute-start.21) | collective-permute-done | bytes 262176 | tf_op jit(solution)/shard_map/ppermute | solution.py:17
  111.2 9.2 %attend.2 = (f32[2048,128]{1,0:T(8,128)}, f32[2048,128]{1,0:T(8,128)}) custom-call(s32[1,4]{1,0:T(1,128)} %len_ref.3, bf16[128,1024]{1,0:T(8,128)(2,1)} %d_ref.3, bf16[8,256,128]{2,1,0:T(8,128)(2,1)} %copy-done.6, bf16[8,256,128]{2,1,0:T(8,128)(2,1)} %copy-done.12, bf16[4,128,256]{2,1,0:T(8,128)(2,1)} %copy-done.8, bf16[4,128,256]{2,1,0:T(8,128)(2,1)} %copy-done.17, ...), custom_call_target="tpu_custom_call" | custom-call | flops 1610612736 | bytes 3145728 | tf_op jit(solution)/shard_map/attend/pallas_call | solution.py:290
  121.4 10.1 %attend.3 = (f32[2048,128]{1,0:T(8,128)}, f32[2048,128]{1,0:T(8,128)}) custom-call(s32[1,4]{1,0:T(1,128)} %len_ref.3, bf16[128,1024]{1,0:T(8,128)(2,1)} %d_ref.3, bf16[8,256,128]{2,1,0:T(8,128)(2,1)} %copy-done.6, bf16[8,256,128]{2,1,0:T(8,128)(2,1)} %copy-done.12, bf16[4,128,256]{2,1,0:T(8,128)(2,1)} %copy-done.8, bf16[4,128,256]{2,1,0:T(8,128)(2,1)} %copy-done.17, ...), custom_call_target="tpu_custom_call" | custom-call | flops 1610612736 | bytes 3145728 | tf_op jit(solution)/shard_map/attend/pallas_call | solution.py:290
  131.6 2.9 %collective-permute-done.25 = f32[2048,128]{1,0:T(8,128)S(1)} collective-permute-done((f32[2048,128]{1,0:T(8,128)}, f32[2048,128]{1,0:T(8,128)S(1)}, u32[]{:S(2)}, u32[]{:S(2)}) %collective-permute-start.25) | collective-permute-done | bytes 1048608 | tf_op jit(solution)/shard_map/ppermute | solution.py:17
  135.9 3.6 %collective-permute-start.32 = (bf16[256,128]{1,0:T(8,128)(2,1)S(1)}, bf16[256,128]{1,0:T(8,128)(2,1)S(1)}, u32[]{:S(2)}, u32[]{:S(2)}) collective-permute-start(bf16[256,128]{1,0:T(8,128)(2,1)S(1)} %get-tuple-element.101), channel_id=1, source_target_pairs={{0,7},{1,6},{2,5},{3,4},{4,3},{5,2},{6,1},{7,0},{8,15},{9,14},{10,... | collective-permute-start | bytes 196616 | tf_op jit(solution)/shard_map/ppermute | solution.py:17
  140.3 1.6 %collective-permute-start.30 = (bf16[256,128]{1,0:T(8,128)(2,1)S(1)}, bf16[256,128]{1,0:T(8,128)(2,1)S(1)}, u32[]{:S(2)}, u32[]{:S(2)}) collective-permute-start(bf16[256,128]{1,0:T(8,128)(2,1)S(1)} %get-tuple-element.103), channel_id=1, source_target_pairs={{0,5},{1,4},{2,7},{3,6},{4,1},{5,0},{6,3},{7,2},{8,13},{9,12},{10,... | collective-permute-start | bytes 196616 | tf_op jit(solution)/shard_map/ppermute | solution.py:17
  144.3 1.8 %collective-permute-start.28 = (bf16[256,128]{1,0:T(8,128)(2,1)S(1)}, bf16[256,128]{1,0:T(8,128)(2,1)S(1)}, u32[]{:S(2)}, u32[]{:S(2)}) collective-permute-start(bf16[256,128]{1,0:T(8,128)(2,1)S(1)} %get-tuple-element.105), channel_id=1, source_target_pairs={{0,6},{1,7},{2,4},{3,5},{4,2},{5,3},{6,0},{7,1},{8,14},{9,15},{10,... | collective-permute-start | bytes 196616 | tf_op jit(solution)/shard_map/ppermute | solution.py:17
  147.1 2.3 %collective-permute-done.30 = bf16[256,128]{1,0:T(8,128)(2,1)S(1)} collective-permute-done((bf16[256,128]{1,0:T(8,128)(2,1)S(1)}, bf16[256,128]{1,0:T(8,128)(2,1)S(1)}, u32[]{:S(2)}, u32[]{:S(2)}) %collective-permute-start.30) | collective-permute-done | bytes 65568 | tf_op jit(solution)/shard_map/ppermute | solution.py:17
  151.1 1.6 collective-permute-start.34
  153.3 3.6 %collective-permute-done.35 = f32[256,128]{1,0:T(8,128)S(1)} collective-permute-done((f32[256,128]{1,0:T(8,128)S(1)}, f32[256,128]{1,0:T(8,128)S(1)}, u32[]{:S(2)}, u32[]{:S(2)}) %collective-permute-start.35) | collective-permute-done | bytes 131104 | tf_op jit(solution)/shard_map/ppermute | solution.py:17
  156.9 2.8 %collective-permute-done.33 = f32[256,128]{1,0:T(8,128)S(1)} collective-permute-done((f32[256,128]{1,0:T(8,128)S(1)}, f32[256,128]{1,0:T(8,128)S(1)}, u32[]{:S(2)}, u32[]{:S(2)}) %collective-permute-start.33) | collective-permute-done | bytes 131104 | tf_op jit(solution)/shard_map/ppermute | solution.py:17
  (109 shorter events, 33.7 us)
Async XLA Ops:
  3.8 33.2 %collective-permute-start.1 = (bf16[640,512]{1,0:T(8,128)(2,1)}, bf16[640,512]{1,0:T(8,128)(2,1)S(1)}, u32[]{:S(2)}, u32[]{:S(2)}) collective-permute-start(bf16[640,512]{1,0:T(8,128)(2,1)} %get-tuple-element.49), channel_id=1, source_target_pairs={{0,4},{1,5},{2,6},{3,7},{4,0},{5,1},{6,2},{7,3},{8,12},{9,13},{10,... | collective-permute-start | bytes 1966088 | tf_op jit(solution)/shard_map/ppermute | solution.py:17
  7.9 39.5 %collective-permute-start.3 = (bf16[128,2048]{1,0:T(8,128)(2,1)}, bf16[128,2048]{1,0:T(8,128)(2,1)S(1)}, u32[]{:S(2)}, u32[]{:S(2)}) collective-permute-start(bf16[128,2048]{1,0:T(8,128)(2,1)} %get-tuple-element.50), channel_id=1, source_target_pairs={{0,1},{1,0},{2,3},{3,2},{4,5},{5,4},{6,7},{7,6},{8,9},{9,8},{10,11... | collective-permute-start | bytes 1572872 | tf_op jit(solution)/shard_map/ppermute | solution.py:17
  9.4 38.0 %collective-permute-start.4 = (bf16[128,2048]{1,0:T(8,128)(2,1)}, bf16[128,2048]{1,0:T(8,128)(2,1)S(1)}, u32[]{:S(2)}, u32[]{:S(2)}) collective-permute-start(bf16[128,2048]{1,0:T(8,128)(2,1)} %get-tuple-element.51), channel_id=1, source_target_pairs={{0,2},{1,3},{2,0},{3,1},{4,6},{5,7},{6,4},{7,5},{8,10},{9,11},{10,... | collective-permute-start | bytes 1572872 | tf_op jit(solution)/shard_map/ppermute | solution.py:17
  11.0 37.2 %collective-permute-start.5 = (bf16[128,2048]{1,0:T(8,128)(2,1)}, bf16[128,2048]{1,0:T(8,128)(2,1)S(1)}, u32[]{:S(2)}, u32[]{:S(2)}) collective-permute-start(bf16[128,2048]{1,0:T(8,128)(2,1)} %get-tuple-element.52), channel_id=1, source_target_pairs={{0,3},{1,2},{2,1},{3,0},{4,7},{5,6},{6,5},{7,4},{8,11},{9,10},{10,... | collective-permute-start | bytes 1572872 | tf_op jit(solution)/shard_map/ppermute | solution.py:17
  37.0 10.3 %collective-permute-start.2 = (bf16[1,384,512]{2,1,0:T(8,128)(2,1)S(1)}, bf16[1,384,512]{2,1,0:T(8,128)(2,1)S(1)}, u32[]{:S(2)}, u32[]{:S(2)}) collective-permute-start(bf16[1,384,512]{2,1,0:T(8,128)(2,1)S(1)} %slice_bitcast_fusion), channel_id=1, source_target_pairs={{0,16},{8,24},{16,0},{24,8},{1,17},{9,25},{17,1},{25,9},{2,18},{10... | collective-permute-start | bytes 1179656 | tf_op jit(solution)/shard_map/ppermute | solution.py:17
  48.2 8.9 %collective-permute-start.8 = (bf16[2,384,512]{2,1,0:T(8,128)(2,1)S(1)}, bf16[2,384,512]{2,1,0:T(8,128)(2,1)S(1)}, u32[]{:S(2)}, u32[]{:S(2)}) collective-permute-start(bf16[2,384,512]{2,1,0:T(8,128)(2,1)S(1)} %pad_maximum_fusion.rest_6_), channel_id=1, source_target_pairs={{0,8},{8,0},{16,24},{24,16},{1,9},{9,1},{17,25},{25,17},{2,10},{10... | collective-permute-start | bytes 2359304 | tf_op jit(solution)/shard_map/ppermute | solution.py:17
  48.2 8.8 %collective-permute-start.6 = (bf16[1,256,512]{2,1,0:T(8,128)(2,1)S(1)}, bf16[1,256,512]{2,1,0:T(8,128)(2,1)S(1)}, u32[]{:S(2)}, u32[]{:S(2)}) collective-permute-start(bf16[1,256,512]{2,1,0:T(8,128)(2,1)S(1)} %slice_bitcast_fusion.1), channel_id=1, source_target_pairs={{0,16},{8,24},{16,0},{24,8},{1,17},{9,25},{17,1},{25,9},{2,18},{10... | collective-permute-start | bytes 786440 | tf_op jit(solution)/shard_map/ppermute | solution.py:17
  63.8 13.6 %collective-permute-start.9 = (bf16[2,256,512]{2,1,0:T(8,128)(2,1)S(1)}, bf16[2,256,512]{2,1,0:T(8,128)(2,1)S(1)}, u32[]{:S(2)}, u32[]{:S(2)}) collective-permute-start(bf16[2,256,512]{2,1,0:T(8,128)(2,1)S(1)} %pad_maximum_fusion.1.rest_4_), channel_id=1, source_target_pairs={{0,8},{8,0},{16,24},{24,16},{1,9},{9,1},{17,25},{25,17},{2,10},{10... | collective-permute-start | bytes 1572872 | tf_op jit(solution)/shard_map/ppermute | solution.py:17
  63.9 12.0 %collective-permute-start.10 = (bf16[4,256,128]{2,1,0:T(8,128)(2,1)S(1)}, bf16[4,256,128]{2,1,0:T(8,128)(2,1)S(1)}, u32[]{:S(2)}, u32[]{:S(2)}) collective-permute-start(bf16[4,256,128]{2,1,0:T(8,128)(2,1)S(1)} %pad_maximum_fusion.3), channel_id=1, source_target_pairs={{0,1},{1,0},{2,3},{3,2},{4,5},{5,4},{6,7},{7,6},{8,9},{9,8},{10,11... | collective-permute-start | bytes 786440 | tf_op jit(solution)/shard_map/ppermute | solution.py:17
  65.4 17.6 %collective-permute-start.11 = (f32[128,256]{1,0:T(8,128)}, f32[128,256]{1,0:T(8,128)S(1)}, u32[]{:S(2)}, u32[]{:S(2)}) collective-permute-start(f32[128,256]{1,0:T(8,128)} %get-tuple-element.63), channel_id=1, source_target_pairs={{0,1},{1,0},{2,3},{3,2},{4,5},{5,4},{6,7},{7,6},{8,9},{9,8},{10,11... | collective-permute-start | bytes 393224 | tf_op jit(solution)/shard_map/ppermute | solution.py:17
  66.0 18.2 %collective-permute-start.12 = (f32[128,256]{1,0:T(8,128)}, f32[128,256]{1,0:T(8,128)S(1)}, u32[]{:S(2)}, u32[]{:S(2)}) collective-permute-start(f32[128,256]{1,0:T(8,128)} %get-tuple-element.64), channel_id=1, source_target_pairs={{0,2},{1,3},{2,0},{3,1},{4,6},{5,7},{6,4},{7,5},{8,10},{9,11},{10,... | collective-permute-start | bytes 393224 | tf_op jit(solution)/shard_map/ppermute | solution.py:17
  66.9 17.3 %collective-permute-start.13 = (f32[128,256]{1,0:T(8,128)}, f32[128,256]{1,0:T(8,128)S(1)}, u32[]{:S(2)}, u32[]{:S(2)}) collective-permute-start(f32[128,256]{1,0:T(8,128)} %get-tuple-element.65), channel_id=1, source_target_pairs={{0,3},{1,2},{2,1},{3,0},{4,7},{5,6},{6,5},{7,4},{8,11},{9,10},{10,... | collective-permute-start | bytes 393224 | tf_op jit(solution)/shard_map/ppermute | solution.py:17
  75.9 11.4 %collective-permute-start.17 = (f32[128,512]{1,0:T(8,128)}, f32[128,512]{1,0:T(8,128)S(1)}, u32[]{:S(2)}, u32[]{:S(2)}) collective-permute-start(f32[128,512]{1,0:T(8,128)} %get-tuple-element.76), channel_id=1, source_target_pairs={{0,1},{1,0},{2,3},{3,2},{4,5},{5,4},{6,7},{7,6},{8,9},{9,8},{10,11... | collective-permute-start | bytes 786440 | tf_op jit(solution)/shard_map/ppermute | solution.py:17
  77.4 10.4 %collective-permute-start.18 = (f32[128,512]{1,0:T(8,128)}, f32[128,512]{1,0:T(8,128)S(1)}, u32[]{:S(2)}, u32[]{:S(2)}) collective-permute-start(f32[128,512]{1,0:T(8,128)} %get-tuple-element.77), channel_id=1, source_target_pairs={{0,2},{1,3},{2,0},{3,1},{4,6},{5,7},{6,4},{7,5},{8,10},{9,11},{10,... | collective-permute-start | bytes 786440 | tf_op jit(solution)/shard_map/ppermute | solution.py:17
  83.0 9.4 %collective-permute-start.19 = (f32[128,512]{1,0:T(8,128)S(1)}, f32[128,512]{1,0:T(8,128)S(1)}, u32[]{:S(2)}, u32[]{:S(2)}) collective-permute-start(f32[128,512]{1,0:T(8,128)S(1)} %copy-done.15), channel_id=1, source_target_pairs={{0,3},{1,2},{2,1},{3,0},{4,7},{5,6},{6,5},{7,4},{8,11},{9,10},{10,... | collective-permute-start | bytes 786440 | tf_op jit(solution)/shard_map/ppermute | solution.py:17
  84.2 8.9 %collective-permute-start.16 = (bf16[128,256]{1,0:T(8,128)(2,1)S(1)}, bf16[128,256]{1,0:T(8,128)(2,1)S(1)}, u32[]{:S(2)}, u32[]{:S(2)}) collective-permute-start(bf16[128,256]{1,0:T(8,128)(2,1)S(1)} %add_convert_fusion), channel_id=1, source_target_pairs={{0,3},{1,2},{2,1},{3,0},{4,7},{5,6},{6,5},{7,4},{8,11},{9,10},{10,... | collective-permute-start | bytes 196616 | tf_op jit(solution)/shard_map/ppermute | solution.py:17
  93.7 16.0 %collective-permute-start.20 = (bf16[8,256,128]{2,1,0:T(8,128)(2,1)S(1)}, bf16[8,256,128]{2,1,0:T(8,128)(2,1)S(1)}, u32[]{:S(2)}, u32[]{:S(2)}) collective-permute-start(bf16[8,256,128]{2,1,0:T(8,128)(2,1)S(1)} %pad_maximum_fusion.2.rest_0_), channel_id=1, source_target_pairs={{0,8},{8,0},{16,24},{24,16},{1,9},{9,1},{17,25},{25,17},{2,10},{10... | collective-permute-start | bytes 1572872 | tf_op jit(solution)/shard_map/ppermute | solution.py:17
  93.8 15.9 %collective-permute-start.21 = (bf16[4,128,256]{2,1,0:T(8,128)(2,1)S(1)}, bf16[4,128,256]{2,1,0:T(8,128)(2,1)S(1)}, u32[]{:S(2)}, u32[]{:S(2)}) collective-permute-start(bf16[4,128,256]{2,1,0:T(8,128)(2,1)S(1)} %pad_maximum_fusion.4.rest_2_), channel_id=1, source_target_pairs={{0,4},{1,5},{2,6},{3,7},{4,0},{5,1},{6,2},{7,3},{8,12},{9,13},{10,... | collective-permute-start | bytes 786440 | tf_op jit(solution)/shard_map/ppermute | solution.py:17
  97.0 23.4 %collective-permute-start.22 = (f32[128,512]{1,0:T(8,128)}, f32[128,512]{1,0:T(8,128)S(1)}, u32[]{:S(2)}, u32[]{:S(2)}) collective-permute-start(f32[128,512]{1,0:T(8,128)} %get-tuple-element.85), channel_id=1, source_target_pairs={{0,1},{1,0},{2,3},{3,2},{4,5},{5,4},{6,7},{7,6},{8,9},{9,8},{10,11... | collective-permute-start | bytes 786440 | tf_op jit(solution)/shard_map/ppermute | solution.py:17
  97.6 22.8 %collective-permute-start.23 = (f32[128,512]{1,0:T(8,128)}, f32[128,512]{1,0:T(8,128)S(1)}, u32[]{:S(2)}, u32[]{:S(2)}) collective-permute-start(f32[128,512]{1,0:T(8,128)} %get-tuple-element.86), channel_id=1, source_target_pairs={{0,2},{1,3},{2,0},{3,1},{4,6},{5,7},{6,4},{7,5},{8,10},{9,11},{10,... | collective-permute-start | bytes 786440 | tf_op jit(solution)/shard_map/ppermute | solution.py:17
  99.1 21.4 %collective-permute-start.24 = (f32[128,512]{1,0:T(8,128)}, f32[128,512]{1,0:T(8,128)S(1)}, u32[]{:S(2)}, u32[]{:S(2)}) collective-permute-start(f32[128,512]{1,0:T(8,128)} %get-tuple-element.87), channel_id=1, source_target_pairs={{0,3},{1,2},{2,1},{3,0},{4,7},{5,6},{6,5},{7,4},{8,11},{9,10},{10,... | collective-permute-start | bytes 786440 | tf_op jit(solution)/shard_map/ppermute | solution.py:17
  135.8 8.4 %collective-permute-start.26 = (bf16[256,128]{1,0:T(8,128)(2,1)S(1)}, bf16[256,128]{1,0:T(8,128)(2,1)S(1)}, u32[]{:S(2)}, u32[]{:S(2)}) collective-permute-start(bf16[256,128]{1,0:T(8,128)(2,1)S(1)} %get-tuple-element.100), channel_id=1, source_target_pairs={{0,4},{1,5},{2,6},{3,7},{4,0},{5,1},{6,2},{7,3},{8,12},{9,13},{10,... | collective-permute-start | bytes 196616 | tf_op jit(solution)/shard_map/ppermute | solution.py:17
  135.9 10.1 %collective-permute-start.32 = (bf16[256,128]{1,0:T(8,128)(2,1)S(1)}, bf16[256,128]{1,0:T(8,128)(2,1)S(1)}, u32[]{:S(2)}, u32[]{:S(2)}) collective-permute-start(bf16[256,128]{1,0:T(8,128)(2,1)S(1)} %get-tuple-element.101), channel_id=1, source_target_pairs={{0,7},{1,6},{2,5},{3,4},{4,3},{5,2},{6,1},{7,0},{8,15},{9,14},{10,... | collective-permute-start | bytes 196616 | tf_op jit(solution)/shard_map/ppermute | solution.py:17
  140.3 9.1 %collective-permute-start.30 = (bf16[256,128]{1,0:T(8,128)(2,1)S(1)}, bf16[256,128]{1,0:T(8,128)(2,1)S(1)}, u32[]{:S(2)}, u32[]{:S(2)}) collective-permute-start(bf16[256,128]{1,0:T(8,128)(2,1)S(1)} %get-tuple-element.103), channel_id=1, source_target_pairs={{0,5},{1,4},{2,7},{3,6},{4,1},{5,0},{6,3},{7,2},{8,13},{9,12},{10,... | collective-permute-start | bytes 196616 | tf_op jit(solution)/shard_map/ppermute | solution.py:17
  (33 other events, 309.4 us)
where the time goes:
time: 161 us; the launch traced here: 160 us
  waiting for transfers between devices  78 us (48%)
  starting transfers between devices  42.9 us (27%)
  Pallas kernels  32.6 us (20%)
  local copies, waits for them, and re-layouts  3.43 us (2%)
  other arithmetic  2.45 us (2%)
    ppermute x36, waiting for transfers between devices, swap(): return lax.ppermute(value, axis, [(i, i ^ bit) for i in range(size)])  78 us
    ppermute x36, starting transfers between devices, swap(): return lax.ppermute(value, axis, [(i, i ^ bit) for i in range(size)])  42.9 us
    pallas_call x2, Pallas kernels, attend(): pl.pallas_call(body, in_specs=[pl.BlockSpec(memory_space=pltpu.SMEM)] + [...  19.3 us
    pallas_call x2, Pallas kernels, multiply(): pl.pallas_call(body, in_specs=[pl.BlockSpec(memory_space=pl.ANY)] * (1 +...  10.2 us
    unnamed x42, local copies, waits for them, and re-layouts  3.35 us
  transfers between devices with their start and end apart: 36, of which 18 were waited for; matrix products, arithmetic and copies ran while one was open for 0% of the time, Pallas kernels for 9%

commit v1 on v0

--- a/solution.py
+++ b/solution.py
@@ -342,6 +342,8 @@
         cache, far_a, *received = together(cache, far_a, *received)
         far_b, _ = double(part_b[None], [0], "dp", n_dp, d_bits[0])
         far_a, d_order = finish(far_a, order, "dp", n_dp, d_bits[1:])
+        cache, f_order = double(cache, f_order, "fsdp", n_fsdp, f_bits[1])
+        cache, far_a[1] = together(cache, far_a[1])
         kv, (at_a, wide_a), (at_b, wide_b) = 2 * head_dim, *cuts
         near_a = [(w_key, 0, head_dim), (w_value, 0, head_dim), (w_query, at_a, wide_a)]
         layout_a = [(0, 0, share, wide_a, 0, kv)]
@@ -349,27 +351,25 @@
         out_kv, out_a = multiply(
             hidden, received, near_a, far_a, layout_a, d_order, n_fsdp, (kv, wide_a)
         )
-        cache, f_order = double(cache, f_order, "fsdp", n_fsdp, f_bits[1])
-        far_b, cache, out_kv[0] = together(far_b, cache, out_kv[0])
-        far_b, _ = finish(far_b, order, "dp", n_dp, d_bits[1:])
         for bit in f_bits[2:]:
             cache, f_order = double(cache, f_order, "fsdp", n_fsdp, bit)
+        far_b, cache, out_kv[0] = together(far_b, cache, out_kv[0])
+        cache = [cache, swap(cache, "dp", n_dp, 1)]
+        far_b, _ = finish(far_b, order, "dp", n_dp, d_bits[1:])
         parts_kv = from_owners(out_kv)
         parts_a = from_owners(out_a)
         near_b, layout_b = [(w_query, at_b, wide_b)], [(0, 0, share, wide_b, 0, 0)]
         (out_b,) = multiply(
             hidden, received, near_b, far_b, layout_b, d_order, n_fsdp, (wide_b,)
         )
-        out_b[0], cache, *parts_kv = together(out_b[0], cache, *parts_kv)
+        cache[1], out_b[0], *parts_kv = together(cache[1], out_b[0], *parts_kv)
         own = functools.reduce(lambda a, b: a + b, parts_kv).astype(BF16)
-        group = [own] + [swap(own, "fsdp", n_fsdp, k) for k in range(1, inner)]
-        cache, *tied = together(cache, *out_b, *group, *parts_a)
+        group, _ = double(own[None], [0], "fsdp", n_fsdp, inner)
+        group = [group] + [swap(group, "fsdp", n_fsdp, k) for k in range(1, inner)]
+        tied = together(*out_b, *group, *parts_a)
         out_b, group, parts_a = tied[:inner], tied[inner : 2 * inner], tied[2 * inner :]
-        g_order = [o for o in f_order if o < inner]
-        group = jnp.stack([group[o] for o in g_order])
-        group, g_order = finish(group, g_order, "fsdp", n_fsdp, [inner])
+        g_order = [o for k in range(inner) for o in (k, k ^ inner)]
         parts_b = from_owners(out_b)
-        cache = (cache, swap(cache, "dp", n_dp, 1))
         first = cuts[0][1] // head_dim
         sums = attend(lengths, parts_a, d_attn, 0, cache, group, g_order, ())
         keep, give = attend(lengths, parts_b, d_attn, first, cache, group, g_order, sums)

time: 161 us -> 149 us (0.925)
  waiting for transfers between devices: 78 us -> 67.5 us
  local copies, waits for them, and re-layouts: 3.43 us -> 0.87 us
    ppermute x36, waiting for transfers between devices: 78 us -> 67.5 us  [swap(): return lax.ppermute(value, axis, [(i, i ^ bit) for i in range(size)])]
    unnamed x42 -> x48, local copies, waits for them, and re-layouts: 3.35 us -> 0.79 us
  transfers between devices with their start and end apart: 36 -> 36, of which waited for: 18 -> 19; matrix products, arithmetic and copies ran while one was open for 0% -> 0% of each run, Pallas kernels for 9% -> 13%
where the time goes in v1:
time: 149 us
  waiting for transfers between devices  67.5 us (45%)
  starting transfers between devices  44.3 us (30%)
  Pallas kernels  32.9 us (22%)
  other arithmetic  2.43 us (2%)
    ppermute x36, waiting for transfers between devices, swap(): return lax.ppermute(value, axis, [(i, i ^ bit) for i in range(size)])  67.5 us
    ppermute x36, starting transfers between devices, swap(): return lax.ppermute(value, axis, [(i, i ^ bit) for i in range(size)])  44.3 us
    pallas_call x2, Pallas kernels, attend(): pl.pallas_call(body, in_specs=[pl.BlockSpec(memory_space=pltpu.SMEM)] + [...  19.4 us
    pallas_call x2, Pallas kernels, multiply(): pl.pallas_call(body, in_specs=[pl.BlockSpec(memory_space=pl.ANY)] * (1 +...  10.4 us
    pallas_call x1, Pallas kernels, prepare(): pl.pallas_call(body, in_specs=[pl.BlockSpec(memory_space=pl.ANY)] * 4, ou...  3.11 us
  transfers between devices with their start and end apart: 36, of which 19 were waited for; matrix products, arithmetic and copies ran while one was open for 0% of the time, Pallas kernels for 13%

profile of v1, /device:TPU:0, one launch (start us, length us, event | category | flops | bytes accessed | tf_op | source)
XLA Modules:
  0.0 149.1 jit_solution(12229332605164246877)
XLA Ops:
  0.6 3.1 %prepare.1 = (bf16[128,2048]{1,0:T(8,128)(2,1)}, bf16[128,2048]{1,0:T(8,128)(2,1)}, bf16[128,2048]{1,0:T(8,128)(2,1)}, bf16[640,512]{1,0:T(8,128)(2,1)}) custom-call(bf16[128,8192]{1,0:T(8,128)(2,1)} %hidden_ref.5, bf16[1024,1024]{1,0:T(8,128)(2,1)} %rest_3_.3, bf16[1024,128]{1,0:T(8,128)(2,1)} %rest_3_.2, bf16[1024,128]{1,0:T(8,128)(2,1)} %rest_4_.1), custom_call_target="tpu_custom_call" | custom-call | bytes 4456448 | tf_op jit(solution)/shard_map/prepare/pallas_call | solution.py:83
  3.8 4.1 %collective-permute-start = (bf16[640,512]{1,0:T(8,128)(2,1)}, bf16[640,512]{1,0:T(8,128)(2,1)S(1)}, u32[]{:S(2)}, u32[]{:S(2)}) collective-permute-start(bf16[640,512]{1,0:T(8,128)(2,1)} %get-tuple-element.50), channel_id=1, source_target_pairs={{0,4},{1,5},{2,6},{3,7},{4,0},{5,1},{6,2},{7,3},{8,12},{9,13},{10,... | collective-permute-start | bytes 1966088 | tf_op jit(solution)/shard_map/ppermute | solution.py:17
  11.4 25.6 %collective-permute-done = bf16[640,512]{1,0:T(8,128)(2,1)S(1)} collective-permute-done((bf16[640,512]{1,0:T(8,128)(2,1)}, bf16[640,512]{1,0:T(8,128)(2,1)S(1)}, u32[]{:S(2)}, u32[]{:S(2)}) %collective-permute-start) | collective-permute-done | bytes 655392 | tf_op jit(solution)/shard_map/ppermute | solution.py:17
  37.0 1.6 %collective-permute-start.3 = (bf16[1,384,512]{2,1,0:T(8,128)(2,1)S(1)}, bf16[1,384,512]{2,1,0:T(8,128)(2,1)S(1)}, u32[]{:S(2)}, u32[]{:S(2)}) collective-permute-start(bf16[1,384,512]{2,1,0:T(8,128)(2,1)S(1)} %slice_bitcast_fusion), channel_id=1, source_target_pairs={{0,16},{8,24},{16,0},{24,8},{1,17},{9,25},{17,1},{25,9},{2,18},{10... | collective-permute-start | bytes 1179656 | tf_op jit(solution)/shard_map/ppermute | solution.py:17
  38.7 7.3 %collective-permute-done.2 = bf16[1,256,128]{2,1,0:T(8,128)(2,1)S(1)} collective-permute-done((bf16[1,256,128]{2,1,0:T(8,128)(2,1)S(1)}, bf16[1,256,128]{2,1,0:T(8,128)(2,1)S(1)}, u32[]{:S(2)}, u32[]{:S(2)}) %collective-permute-start.2) | collective-permute-done | bytes 65568 | tf_op jit(solution)/shard_map/ppermute | solution.py:17
  50.7 4.8 %collective-permute-done.7 = bf16[2,256,128]{2,1,0:T(8,128)(2,1)S(1)} collective-permute-done((bf16[2,256,128]{2,1,0:T(8,128)(2,1)S(1)}, bf16[2,256,128]{2,1,0:T(8,128)(2,1)S(1)}, u32[]{:S(2)}, u32[]{:S(2)}) %collective-permute-start.7) | collective-permute-done | bytes 131104 | tf_op jit(solution)/shard_map/ppermute | solution.py:17
  57.2 5.8 %multiply.2 = (f32[128,256]{1,0:T(8,128)}, f32[128,256]{1,0:T(8,128)}, f32[128,256]{1,0:T(8,128)}, f32[128,256]{1,0:T(8,128)}, f32[128,512]{1,0:T(8,128)}, /*ind...) custom-call(bf16[128,8192]{1,0:T(8,128)(2,1)} %hidden_ref.5, bf16[128,2048]{1,0:T(8,128)(2,1)} %copy-done.2, ...), custom_call_target="tpu_custom_call" | custom-call | flops 1610612736 | bytes 6815744 | tf_op jit(solution)/shard_map/multiply/pallas_call | solution.py:154
  68.9 4.5 %multiply.3 = (f32[128,512]{1,0:T(8,128)}, f32[128,512]{1,0:T(8,128)}, f32[128,512]{1,0:T(8,128)}, f32[128,512]{1,0:T(8,128)}) custom-call(bf16[128,8192]{1,0:T(8,128)(2,1)} %hidden_ref.5, bf16[128,2048]{1,0:T(8,128)(2,1)} %copy-done.2, bf16[128,2048]{1,0:T(8,128)(2,1)} %copy-done.3, bf16[128,2048]{1,0:T(8,128)(2,1)} %copy-done.4, ...), custom_call_target="tpu_custom_call" | custom-call | flops 1073741824 | bytes 5242880 | tf_op jit(solution)/shard_map/multiply/pallas_call | solution.py:154
  73.7 2.7 %collective-permute-start.15 = (bf16[1,128,256]{2,1,0:T(8,128)(2,1)S(1)}, bf16[1,128,256]{2,1,0:T(8,128)(2,1)S(1)}, u32[]{:S(2)}, u32[]{:S(2)}) collective-permute-start(bf16[1,128,256]{2,1,0:T(8,128)(2,1)S(1)} %fusion.6), channel_id=1, source_target_pairs={{0,4},{1,5},{2,6},{3,7},{4,0},{5,1},{6,2},{7,3},{8,12},{9,13},{10,... | collective-permute-start | bytes 196616 | tf_op jit(solution)/shard_map/ppermute | solution.py:17
  79.4 2.5 %collective-permute-start.18 = (bf16[2,128,256]{2,1,0:T(8,128)(2,1)S(1)}, bf16[2,128,256]{2,1,0:T(8,128)(2,1)S(1)}, u32[]{:S(2)}, u32[]{:S(2)}) collective-permute-start(bf16[2,128,256]{2,1,0:T(8,128)(2,1)S(1)} %pad_maximum_fusion.5.rest_2_), channel_id=1, source_target_pairs={{0,3},{1,2},{2,1},{3,0},{4,7},{5,6},{6,5},{7,4},{8,11},{9,10},{10,... | collective-permute-start | bytes 393224 | tf_op jit(solution)/shard_map/ppermute | solution.py:17
  83.0 2.6 %collective-permute-done.20.rest_8_ = f32[128,512]{1,0:T(8,128)S(1)} collective-permute-done((f32[128,512]{1,0:T(8,128)S(1)}, f32[128,512]{1,0:T(8,128)S(1)}, u32[]{:S(2)}, u32[]{:S(2)}) %collective-permute-start.20) | collective-permute-done | bytes 262176 | tf_op jit(solution)/shard_map/ppermute | solution.py:17
  85.6 6.7 %collective-permute-done.21.rest_9_ = f32[128,512]{1,0:T(8,128)S(1)} collective-permute-done((f32[128,512]{1,0:T(8,128)S(1)}, f32[128,512]{1,0:T(8,128)S(1)}, u32[]{:S(2)}, u32[]{:S(2)}) %collective-permute-start.21) | collective-permute-done | bytes 262176 | tf_op jit(solution)/shard_map/ppermute | solution.py:17
  92.3 2.4 %collective-permute-done.18.rest_5_ = bf16[2,128,256]{2,1,0:T(8,128)(2,1)S(1)} collective-permute-done((bf16[2,128,256]{2,1,0:T(8,128)(2,1)S(1)}, bf16[2,128,256]{2,1,0:T(8,128)(2,1)S(1)}, u32[]{:S(2)}, u32[]{:S(2)}) %collective-permute-start.18) | collective-permute-done | bytes 131104 | tf_op jit(solution)/shard_map/ppermute | solution.py:17
  99.1 9.3 %attend.2 = (f32[2048,128]{1,0:T(8,128)}, f32[2048,128]{1,0:T(8,128)}) custom-call(s32[1,4]{1,0:T(1,128)} %len_ref.3, bf16[128,1024]{1,0:T(8,128)(2,1)} %d_ref.3, bf16[8,256,128]{2,1,0:T(8,128)(2,1)} %copy-done.6, bf16[8,256,128]{2,1,0:T(8,128)(2,1)} %copy-done.12, bf16[2,128,256]{2,1,0:T(8,128)(2,1)} %copy-done.8, bf16[2,128,256]{2,1,0:T(8,128)(2,1)} %copy-done.23, ...), custom_call_target="tpu_custom_call" | custom-call | flops 1610612736 | bytes 3145728 | tf_op jit(solution)/shard_map/attend/pallas_call | solution.py:290
  110.3 10.1 %attend.3 = (f32[2048,128]{1,0:T(8,128)}, f32[2048,128]{1,0:T(8,128)}) custom-call(s32[1,4]{1,0:T(1,128)} %len_ref.3, bf16[128,1024]{1,0:T(8,128)(2,1)} %d_ref.3, bf16[8,256,128]{2,1,0:T(8,128)(2,1)} %copy-done.6, bf16[8,256,128]{2,1,0:T(8,128)(2,1)} %copy-done.12, bf16[2,128,256]{2,1,0:T(8,128)(2,1)} %copy-done.8, bf16[2,128,256]{2,1,0:T(8,128)(2,1)} %copy-done.23, ...), custom_call_target="tpu_custom_call" | custom-call | flops 1610612736 | bytes 3145728 | tf_op jit(solution)/shard_map/attend/pallas_call | solution.py:290
  120.4 2.9 %collective-permute-done.25 = f32[2048,128]{1,0:T(8,128)S(1)} collective-permute-done((f32[2048,128]{1,0:T(8,128)}, f32[2048,128]{1,0:T(8,128)S(1)}, u32[]{:S(2)}, u32[]{:S(2)}) %collective-permute-start.25) | collective-permute-done | bytes 1048608 | tf_op jit(solution)/shard_map/ppermute | solution.py:17
  124.9 3.8 %collective-permute-start.32 = (bf16[256,128]{1,0:T(8,128)(2,1)S(1)}, bf16[256,128]{1,0:T(8,128)(2,1)S(1)}, u32[]{:S(2)}, u32[]{:S(2)}) collective-permute-start(bf16[256,128]{1,0:T(8,128)(2,1)S(1)} %get-tuple-element.103), channel_id=1, source_target_pairs={{0,7},{1,6},{2,5},{3,4},{4,3},{5,2},{6,1},{7,0},{8,15},{9,14},{10,... | collective-permute-start | bytes 196616 | tf_op jit(solution)/shard_map/ppermute | solution.py:17
  129.2 1.9 %collective-permute-start.30 = (bf16[256,128]{1,0:T(8,128)(2,1)S(1)}, bf16[256,128]{1,0:T(8,128)(2,1)S(1)}, u32[]{:S(2)}, u32[]{:S(2)}) collective-permute-start(bf16[256,128]{1,0:T(8,128)(2,1)S(1)} %get-tuple-element.105), channel_id=1, source_target_pairs={{0,5},{1,4},{2,7},{3,6},{4,1},{5,0},{6,3},{7,2},{8,13},{9,12},{10,... | collective-permute-start | bytes 196616 | tf_op jit(solution)/shard_map/ppermute | solution.py:17
  132.9 1.7 %collective-permute-start.28 = (bf16[256,128]{1,0:T(8,128)(2,1)S(1)}, bf16[256,128]{1,0:T(8,128)(2,1)S(1)}, u32[]{:S(2)}, u32[]{:S(2)}) collective-permute-start(bf16[256,128]{1,0:T(8,128)(2,1)S(1)} %get-tuple-element.107), channel_id=1, source_target_pairs={{0,6},{1,7},{2,4},{3,5},{4,2},{5,3},{6,0},{7,1},{8,14},{9,15},{10,... | collective-permute-start | bytes 196616 | tf_op jit(solution)/shard_map/ppermute | solution.py:17
  134.6 1.6 %collective-permute-start.27 = (bf16[256,128]{1,0:T(8,128)(2,1)S(1)}, bf16[256,128]{1,0:T(8,128)(2,1)S(1)}, u32[]{:S(2)}, u32[]{:S(2)}) collective-permute-start(bf16[256,128]{1,0:T(8,128)(2,1)S(1)} %get-tuple-element.108), channel_id=1, source_target_pairs={{0,2},{1,3},{2,0},{3,1},{4,6},{5,7},{6,4},{7,5},{8,10},{9,11},{10,... | collective-permute-start | bytes 196616 | tf_op jit(solution)/shard_map/ppermute | solution.py:17
  136.2 2.2 %collective-permute-done.30 = bf16[256,128]{1,0:T(8,128)(2,1)S(1)} collective-permute-done((bf16[256,128]{1,0:T(8,128)(2,1)S(1)}, bf16[256,128]{1,0:T(8,128)(2,1)S(1)}, u32[]{:S(2)}, u32[]{:S(2)}) %collective-permute-start.30) | collective-permute-done | bytes 65568 | tf_op jit(solution)/shard_map/ppermute | solution.py:17
  139.7 1.8 %collective-permute-start.34 = (f32[256,128]{1,0:T(8,128)S(1)}, f32[256,128]{1,0:T(8,128)S(1)}, u32[]{:S(2)}, u32[]{:S(2)}) collective-permute-start(f32[256,128]{1,0:T(8,128)S(1)} %fusion.5), channel_id=1, source_target_pairs={{0,8},{8,0},{16,24},{24,16},{1,9},{9,1},{17,25},{25,17},{2,10},{10... | collective-permute-start | bytes 393224 | tf_op jit(solution)/shard_map/ppermute | solution.py:17
  141.9 3.4 %collective-permute-done.35 = f32[256,128]{1,0:T(8,128)S(1)} collective-permute-done((f32[256,128]{1,0:T(8,128)S(1)}, f32[256,128]{1,0:T(8,128)S(1)}, u32[]{:S(2)}, u32[]{:S(2)}) %collective-permute-start.35) | collective-permute-done | bytes 131104 | tf_op jit(solution)/shard_map/ppermute | solution.py:17
  145.3 3.0 %collective-permute-done.33 = f32[256,128]{1,0:T(8,128)S(1)} collective-permute-done((f32[256,128]{1,0:T(8,128)S(1)}, f32[256,128]{1,0:T(8,128)S(1)}, u32[]{:S(2)}, u32[]{:S(2)}) %collective-permute-start.33) | collective-permute-done | bytes 131104 | tf_op jit(solution)/shard_map/ppermute | solution.py:17
  (115 shorter events, 32.6 us)
Async XLA Ops:
  3.8 33.2 %collective-permute-start = (bf16[640,512]{1,0:T(8,128)(2,1)}, bf16[640,512]{1,0:T(8,128)(2,1)S(1)}, u32[]{:S(2)}, u32[]{:S(2)}) collective-permute-start(bf16[640,512]{1,0:T(8,128)(2,1)} %get-tuple-element.50), channel_id=1, source_target_pairs={{0,4},{1,5},{2,6},{3,7},{4,0},{5,1},{6,2},{7,3},{8,12},{9,13},{10,... | collective-permute-start | bytes 1966088 | tf_op jit(solution)/shard_map/ppermute | solution.py:17
  7.9 39.5 %collective-permute-start.4 = (bf16[128,2048]{1,0:T(8,128)(2,1)}, bf16[128,2048]{1,0:T(8,128)(2,1)S(1)}, u32[]{:S(2)}, u32[]{:S(2)}) collective-permute-start(bf16[128,2048]{1,0:T(8,128)(2,1)} %get-tuple-element.51), channel_id=1, source_target_pairs={{0,1},{1,0},{2,3},{3,2},{4,5},{5,4},{6,7},{7,6},{8,9},{9,8},{10,11... | collective-permute-start | bytes 1572872 | tf_op jit(solution)/shard_map/ppermute | solution.py:17
  9.4 38.0 %collective-permute-start.5 = (bf16[128,2048]{1,0:T(8,128)(2,1)}, bf16[128,2048]{1,0:T(8,128)(2,1)S(1)}, u32[]{:S(2)}, u32[]{:S(2)}) collective-permute-start(bf16[128,2048]{1,0:T(8,128)(2,1)} %get-tuple-element.52), channel_id=1, source_target_pairs={{0,2},{1,3},{2,0},{3,1},{4,6},{5,7},{6,4},{7,5},{8,10},{9,11},{10,... | collective-permute-start | bytes 1572872 | tf_op jit(solution)/shard_map/ppermute | solution.py:17
  11.0 37.2 %collective-permute-start.6 = (bf16[128,2048]{1,0:T(8,128)(2,1)}, bf16[128,2048]{1,0:T(8,128)(2,1)S(1)}, u32[]{:S(2)}, u32[]{:S(2)}) collective-permute-start(bf16[128,2048]{1,0:T(8,128)(2,1)} %get-tuple-element.53), channel_id=1, source_target_pairs={{0,3},{1,2},{2,1},{3,0},{4,7},{5,6},{6,5},{7,4},{8,11},{9,10},{10,... | collective-permute-start | bytes 1572872 | tf_op jit(solution)/shard_map/ppermute | solution.py:17
  37.0 10.3 %collective-permute-start.3 = (bf16[1,384,512]{2,1,0:T(8,128)(2,1)S(1)}, bf16[1,384,512]{2,1,0:T(8,128)(2,1)S(1)}, u32[]{:S(2)}, u32[]{:S(2)}) collective-permute-start(bf16[1,384,512]{2,1,0:T(8,128)(2,1)S(1)} %slice_bitcast_fusion), channel_id=1, source_target_pairs={{0,16},{8,24},{16,0},{24,8},{1,17},{9,25},{17,1},{25,9},{2,18},{10... | collective-permute-start | bytes 1179656 | tf_op jit(solution)/shard_map/ppermute | solution.py:17
  48.2 8.8 %collective-permute-start.1 = (bf16[1,256,512]{2,1,0:T(8,128)(2,1)S(1)}, bf16[1,256,512]{2,1,0:T(8,128)(2,1)S(1)}, u32[]{:S(2)}, u32[]{:S(2)}) collective-permute-start(bf16[1,256,512]{2,1,0:T(8,128)(2,1)S(1)} %slice_bitcast_fusion.1), channel_id=1, source_target_pairs={{0,16},{8,24},{16,0},{24,8},{1,17},{9,25},{17,1},{25,9},{2,18},{10... | collective-permute-start | bytes 786440 | tf_op jit(solution)/shard_map/ppermute | solution.py:17
  55.5 7.7 %collective-permute-start.9 = (bf16[4,256,128]{2,1,0:T(8,128)(2,1)S(1)}, bf16[4,256,128]{2,1,0:T(8,128)(2,1)S(1)}, u32[]{:S(2)}, u32[]{:S(2)}) collective-permute-start(bf16[4,256,128]{2,1,0:T(8,128)(2,1)S(1)} %pad_maximum_fusion.3), channel_id=1, source_target_pairs={{0,1},{1,0},{2,3},{3,2},{4,5},{5,4},{6,7},{7,6},{8,9},{9,8},{10,11... | collective-permute-start | bytes 786440 | tf_op jit(solution)/shard_map/ppermute | solution.py:17
  63.3 10.3 %collective-permute-start.10 = (bf16[8,256,128]{2,1,0:T(8,128)(2,1)S(1)}, bf16[8,256,128]{2,1,0:T(8,128)(2,1)S(1)}, u32[]{:S(2)}, u32[]{:S(2)}) collective-permute-start(bf16[8,256,128]{2,1,0:T(8,128)(2,1)S(1)} %pad_maximum_fusion.2.rest_0_), channel_id=1, source_target_pairs={{0,8},{8,0},{16,24},{24,16},{1,9},{9,1},{17,25},{25,17},{2,10},{10... | collective-permute-start | bytes 1572872 | tf_op jit(solution)/shard_map/ppermute | solution.py:17
  63.8 9.7 %collective-permute-start.12 = (f32[128,256]{1,0:T(8,128)}, f32[128,256]{1,0:T(8,128)S(1)}, u32[]{:S(2)}, u32[]{:S(2)}) collective-permute-start(f32[128,256]{1,0:T(8,128)} %get-tuple-element.66), channel_id=1, source_target_pairs={{0,1},{1,0},{2,3},{3,2},{4,5},{5,4},{6,7},{7,6},{8,9},{9,8},{10,11... | collective-permute-start | bytes 393224 | tf_op jit(solution)/shard_map/ppermute | solution.py:17
  65.3 8.2 %collective-permute-start.13 = (f32[128,256]{1,0:T(8,128)}, f32[128,256]{1,0:T(8,128)S(1)}, u32[]{:S(2)}, u32[]{:S(2)}) collective-permute-start(f32[128,256]{1,0:T(8,128)} %get-tuple-element.67), channel_id=1, source_target_pairs={{0,2},{1,3},{2,0},{3,1},{4,6},{5,7},{6,4},{7,5},{8,10},{9,11},{10,... | collective-permute-start | bytes 393224 | tf_op jit(solution)/shard_map/ppermute | solution.py:17
  66.2 7.4 %collective-permute-start.14 = (f32[128,256]{1,0:T(8,128)}, f32[128,256]{1,0:T(8,128)S(1)}, u32[]{:S(2)}, u32[]{:S(2)}) collective-permute-start(f32[128,256]{1,0:T(8,128)} %get-tuple-element.68), channel_id=1, source_target_pairs={{0,3},{1,2},{2,1},{3,0},{4,7},{5,6},{6,5},{7,4},{8,11},{9,10},{10,... | collective-permute-start | bytes 393224 | tf_op jit(solution)/shard_map/ppermute | solution.py:17
  67.3 14.8 %collective-permute-start.19 = (f32[128,512]{1,0:T(8,128)}, f32[128,512]{1,0:T(8,128)S(1)}, u32[]{:S(2)}, u32[]{:S(2)}) collective-permute-start(f32[128,512]{1,0:T(8,128)} %get-tuple-element.79), channel_id=1, source_target_pairs={{0,1},{1,0},{2,3},{3,2},{4,5},{5,4},{6,7},{7,6},{8,9},{9,8},{10,11... | collective-permute-start | bytes 786440 | tf_op jit(solution)/shard_map/ppermute | solution.py:17
  76.4 9.2 %collective-permute-start.20 = (f32[128,512]{1,0:T(8,128)S(1)}, f32[128,512]{1,0:T(8,128)S(1)}, u32[]{:S(2)}, u32[]{:S(2)}) collective-permute-start(f32[128,512]{1,0:T(8,128)S(1)} %copy-done.14), channel_id=1, source_target_pairs={{0,2},{1,3},{2,0},{3,1},{4,6},{5,7},{6,4},{7,5},{8,10},{9,11},{10,... | collective-permute-start | bytes 786440 | tf_op jit(solution)/shard_map/ppermute | solution.py:17
  77.8 14.4 %collective-permute-start.21 = (f32[128,512]{1,0:T(8,128)S(1)}, f32[128,512]{1,0:T(8,128)S(1)}, u32[]{:S(2)}, u32[]{:S(2)}) collective-permute-start(f32[128,512]{1,0:T(8,128)S(1)} %copy-done.13), channel_id=1, source_target_pairs={{0,3},{1,2},{2,1},{3,0},{4,7},{5,6},{6,5},{7,4},{8,11},{9,10},{10,... | collective-permute-start | bytes 786440 | tf_op jit(solution)/shard_map/ppermute | solution.py:17
  79.4 15.3 %collective-permute-start.18 = (bf16[2,128,256]{2,1,0:T(8,128)(2,1)S(1)}, bf16[2,128,256]{2,1,0:T(8,128)(2,1)S(1)}, u32[]{:S(2)}, u32[]{:S(2)}) collective-permute-start(bf16[2,128,256]{2,1,0:T(8,128)(2,1)S(1)} %pad_maximum_fusion.5.rest_2_), channel_id=1, source_target_pairs={{0,3},{1,2},{2,1},{3,0},{4,7},{5,6},{6,5},{7,4},{8,11},{9,10},{10,... | collective-permute-start | bytes 393224 | tf_op jit(solution)/shard_map/ppermute | solution.py:17
  81.9 13.6 %collective-permute-start.17 = (bf16[2,128,256]{2,1,0:T(8,128)(2,1)S(1)}, bf16[2,128,256]{2,1,0:T(8,128)(2,1)S(1)}, u32[]{:S(2)}, u32[]{:S(2)}) collective-permute-start(bf16[2,128,256]{2,1,0:T(8,128)(2,1)S(1)} %pad_maximum_fusion.5.rest_2_), channel_id=1, source_target_pairs={{0,2},{1,3},{2,0},{3,1},{4,6},{5,7},{6,4},{7,5},{8,10},{9,11},{10,... | collective-permute-start | bytes 393224 | tf_op jit(solution)/shard_map/ppermute | solution.py:17
  82.1 13.5 %collective-permute-start.16 = (bf16[2,128,256]{2,1,0:T(8,128)(2,1)S(1)}, bf16[2,128,256]{2,1,0:T(8,128)(2,1)S(1)}, u32[]{:S(2)}, u32[]{:S(2)}) collective-permute-start(bf16[2,128,256]{2,1,0:T(8,128)(2,1)S(1)} %pad_maximum_fusion.5.rest_2_), channel_id=1, source_target_pairs={{0,1},{1,0},{2,3},{3,2},{4,5},{5,4},{6,7},{7,6},{8,9},{9,8},{10,11... | collective-permute-start | bytes 393224 | tf_op jit(solution)/shard_map/ppermute | solution.py:17
  95.5 12.9 %collective-permute-start.22 = (f32[128,512]{1,0:T(8,128)}, f32[128,512]{1,0:T(8,128)S(1)}, u32[]{:S(2)}, u32[]{:S(2)}) collective-permute-start(f32[128,512]{1,0:T(8,128)} %get-tuple-element.87), channel_id=1, source_target_pairs={{0,1},{1,0},{2,3},{3,2},{4,5},{5,4},{6,7},{7,6},{8,9},{9,8},{10,11... | collective-permute-start | bytes 786440 | tf_op jit(solution)/shard_map/ppermute | solution.py:17
  96.7 11.7 %collective-permute-start.23 = (f32[128,512]{1,0:T(8,128)}, f32[128,512]{1,0:T(8,128)S(1)}, u32[]{:S(2)}, u32[]{:S(2)}) collective-permute-start(f32[128,512]{1,0:T(8,128)} %get-tuple-element.88), channel_id=1, source_target_pairs={{0,2},{1,3},{2,0},{3,1},{4,6},{5,7},{6,4},{7,5},{8,10},{9,11},{10,... | collective-permute-start | bytes 786440 | tf_op jit(solution)/shard_map/ppermute | solution.py:17
  98.1 11.4 %collective-permute-start.24 = (f32[128,512]{1,0:T(8,128)}, f32[128,512]{1,0:T(8,128)S(1)}, u32[]{:S(2)}, u32[]{:S(2)}) collective-permute-start(f32[128,512]{1,0:T(8,128)} %get-tuple-element.89), channel_id=1, source_target_pairs={{0,3},{1,2},{2,1},{3,0},{4,7},{5,6},{6,5},{7,4},{8,11},{9,10},{10,... | collective-permute-start | bytes 786440 | tf_op jit(solution)/shard_map/ppermute | solution.py:17
  124.7 8.2 %collective-permute-start.26 = (bf16[256,128]{1,0:T(8,128)(2,1)S(1)}, bf16[256,128]{1,0:T(8,128)(2,1)S(1)}, u32[]{:S(2)}, u32[]{:S(2)}) collective-permute-start(bf16[256,128]{1,0:T(8,128)(2,1)S(1)} %get-tuple-element.102), channel_id=1, source_target_pairs={{0,4},{1,5},{2,6},{3,7},{4,0},{5,1},{6,2},{7,3},{8,12},{9,13},{10,... | collective-permute-start | bytes 196616 | tf_op jit(solution)/shard_map/ppermute | solution.py:17
  124.9 9.7 %collective-permute-start.32 = (bf16[256,128]{1,0:T(8,128)(2,1)S(1)}, bf16[256,128]{1,0:T(8,128)(2,1)S(1)}, u32[]{:S(2)}, u32[]{:S(2)}) collective-permute-start(bf16[256,128]{1,0:T(8,128)(2,1)S(1)} %get-tuple-element.103), channel_id=1, source_target_pairs={{0,7},{1,6},{2,5},{3,4},{4,3},{5,2},{6,1},{7,0},{8,15},{9,14},{10,... | collective-permute-start | bytes 196616 | tf_op jit(solution)/shard_map/ppermute | solution.py:17
  128.7 7.5 %collective-permute-start.31 = (bf16[256,128]{1,0:T(8,128)(2,1)S(1)}, bf16[256,128]{1,0:T(8,128)(2,1)S(1)}, u32[]{:S(2)}, u32[]{:S(2)}) collective-permute-start(bf16[256,128]{1,0:T(8,128)(2,1)S(1)} %get-tuple-element.104), channel_id=1, source_target_pairs={{0,3},{1,2},{2,1},{3,0},{4,7},{5,6},{6,5},{7,4},{8,11},{9,10},{10,... | collective-permute-start | bytes 196616 | tf_op jit(solution)/shard_map/ppermute | solution.py:17
  129.2 9.3 %collective-permute-start.30 = (bf16[256,128]{1,0:T(8,128)(2,1)S(1)}, bf16[256,128]{1,0:T(8,128)(2,1)S(1)}, u32[]{:S(2)}, u32[]{:S(2)}) collective-permute-start(bf16[256,128]{1,0:T(8,128)(2,1)S(1)} %get-tuple-element.105), channel_id=1, source_target_pairs={{0,5},{1,4},{2,7},{3,6},{4,1},{5,0},{6,3},{7,2},{8,13},{9,12},{10,... | collective-permute-start | bytes 196616 | tf_op jit(solution)/shard_map/ppermute | solution.py:17
  (36 other events, 326.2 us)

commit v2 on v1

--- a/solution.py
+++ b/solution.py
@@ -354,7 +354,6 @@
         for bit in f_bits[2:]:
             cache, f_order = double(cache, f_order, "fsdp", n_fsdp, bit)
         far_b, cache, out_kv[0] = together(far_b, cache, out_kv[0])
-        cache = [cache, swap(cache, "dp", n_dp, 1)]
         far_b, _ = finish(far_b, order, "dp", n_dp, d_bits[1:])
         parts_kv = from_owners(out_kv)
         parts_a = from_owners(out_a)
@@ -362,13 +361,14 @@
         (out_b,) = multiply(
             hidden, received, near_b, far_b, layout_b, d_order, n_fsdp, (wide_b,)
         )
-        cache[1], out_b[0], *parts_kv = together(cache[1], out_b[0], *parts_kv)
+        out_b[0], parts_a[1], *parts_kv = together(out_b[0], parts_a[1], *parts_kv)
         own = functools.reduce(lambda a, b: a + b, parts_kv).astype(BF16)
         group, _ = double(own[None], [0], "fsdp", n_fsdp, inner)
+        group, cache, *tied = together(group, cache, *out_b, *parts_a[2:])
+        out_b, parts_a[2:] = tied[:inner], tied[inner:]
         group = [group] + [swap(group, "fsdp", n_fsdp, k) for k in range(1, inner)]
-        tied = together(*out_b, *group, *parts_a)
-        out_b, group, parts_a = tied[:inner], tied[inner : 2 * inner], tied[2 * inner :]
         g_order = [o for k in range(inner) for o in (k, k ^ inner)]
+        cache = [cache, swap(cache, "dp", n_dp, 1)]
         parts_b = from_owners(out_b)
         first = cuts[0][1] // head_dim
         sums = attend(lengths, parts_a, d_attn, 0, cache, group, g_order, ())
@@ -380,11 +380,9 @@
         for slot in range(1, n_fsdp):
             out = half[slot * size : (slot + 1) * size].astype(BF16)
             mine = mine + swap(out, "fsdp", n_fsdp, f_order[slot]).astype(F32)
-        for bit in bits_down(n_dp)[:-2]:
+        for bit in d_bits[:-1]:
             mine = mine + swap(mine, "dp", n_dp, bit)
-        beside, other, across = (swap(mine, "dp", n_dp, bit) for bit in (2, 1, 3))
-        mine = mine + beside
-        other = other + across
+        other = swap(mine, "dp", n_dp, 1)
         return jnp.where(even, mine, other), jnp.where(even, other, mine)
 
     return on_device

time: 149 us -> 149 us (level)
  waiting for transfers between devices: 67.5 us -> 63.6 us
  starting transfers between devices: 44.3 us -> 47.1 us
    ppermute x36 -> x35, waiting for transfers between devices: 67.5 us -> 63.6 us  [swap(): return lax.ppermute(value, axis, [(i, i ^ bit) for i in range(size)])]
    ppermute x36 -> x35, starting transfers between devices: 44.3 us -> 47.1 us  [swap(): return lax.ppermute(value, axis, [(i, i ^ bit) for i in range(size)])]
  transfers between devices with their start and end apart: 36 -> 35, of which waited for: 19 -> 16; matrix products, arithmetic and copies ran while one was open for 0% -> 0% of each run, Pallas kernels for 13% -> 13%
where the time goes in v2:
time: 149 us
  waiting for transfers between devices  63.6 us (43%)
  starting transfers between devices  47.1 us (32%)
  Pallas kernels  32.9 us (22%)
  other arithmetic  2.43 us (2%)
  local copies, waits for them, and re-layouts  1.78 us (1%)
    ppermute x35, waiting for transfers between devices, swap(): return lax.ppermute(value, axis, [(i, i ^ bit) for i in range(size)])  63.6 us
    ppermute x35, starting transfers between devices, swap(): return lax.ppermute(value, axis, [(i, i ^ bit) for i in range(size)])  47.1 us
    pallas_call x2, Pallas kernels, attend(): pl.pallas_call(body, in_specs=[pl.BlockSpec(memory_space=pltpu.SMEM)] + [...  19.4 us
    pallas_call x2, Pallas kernels, multiply(): pl.pallas_call(body, in_specs=[pl.BlockSpec(memory_space=pl.ANY)] * (1 +...  10.4 us
    pallas_call x1, Pallas kernels, prepare(): pl.pallas_call(body, in_specs=[pl.BlockSpec(memory_space=pl.ANY)] * 4, ou...  3.11 us
  transfers between devices with their start and end apart: 35, of which 16 were waited for; matrix products, arithmetic and copies ran while one was open for 0% of the time, Pallas kernels for 13%

profile of v2, /device:TPU:0, one launch (start us, length us, event | category | flops | bytes accessed | tf_op | source)
XLA Modules:
  0.0 148.9 jit_solution(4913521198098194238)
XLA Ops:
  0.6 3.1 %prepare.1 = (bf16[128,2048]{1,0:T(8,128)(2,1)}, bf16[128,2048]{1,0:T(8,128)(2,1)}, bf16[128,2048]{1,0:T(8,128)(2,1)}, bf16[640,512]{1,0:T(8,128)(2,1)}) custom-call(bf16[128,8192]{1,0:T(8,128)(2,1)} %hidden_ref.5, bf16[1024,1024]{1,0:T(8,128)(2,1)} %rest_3_.3, bf16[1024,128]{1,0:T(8,128)(2,1)} %rest_3_.2, bf16[1024,128]{1,0:T(8,128)(2,1)} %rest_4_.1), custom_call_target="tpu_custom_call" | custom-call | bytes 4456448 | tf_op jit(solution)/shard_map/prepare/pallas_call | solution.py:83
  3.8 4.1 %collective-permute-start.1 = (bf16[640,512]{1,0:T(8,128)(2,1)}, bf16[640,512]{1,0:T(8,128)(2,1)S(1)}, u32[]{:S(2)}, u32[]{:S(2)}) collective-permute-start(bf16[640,512]{1,0:T(8,128)(2,1)} %get-tuple-element.46), channel_id=1, source_target_pairs={{0,4},{1,5},{2,6},{3,7},{4,0},{5,1},{6,2},{7,3},{8,12},{9,13},{10,... | collective-permute-start | bytes 1966088 | tf_op jit(solution)/shard_map/ppermute | solution.py:17
  11.4 25.6 %collective-permute-done.1 = bf16[640,512]{1,0:T(8,128)(2,1)S(1)} collective-permute-done((bf16[640,512]{1,0:T(8,128)(2,1)}, bf16[640,512]{1,0:T(8,128)(2,1)S(1)}, u32[]{:S(2)}, u32[]{:S(2)}) %collective-permute-start.1) | collective-permute-done | bytes 655392 | tf_op jit(solution)/shard_map/ppermute | solution.py:17
  38.7 7.3 %collective-permute-done = bf16[1,256,128]{2,1,0:T(8,128)(2,1)S(1)} collective-permute-done((bf16[1,256,128]{2,1,0:T(8,128)(2,1)S(1)}, bf16[1,256,128]{2,1,0:T(8,128)(2,1)S(1)}, u32[]{:S(2)}, u32[]{:S(2)}) %collective-permute-start) | collective-permute-done | bytes 65568 | tf_op jit(solution)/shard_map/ppermute | solution.py:17
  50.7 4.8 %collective-permute-done.7 = bf16[2,256,128]{2,1,0:T(8,128)(2,1)S(1)} collective-permute-done((bf16[2,256,128]{2,1,0:T(8,128)(2,1)S(1)}, bf16[2,256,128]{2,1,0:T(8,128)(2,1)S(1)}, u32[]{:S(2)}, u32[]{:S(2)}) %collective-permute-start.7) | collective-permute-done | bytes 131104 | tf_op jit(solution)/shard_map/ppermute | solution.py:17
  57.2 5.8 %multiply.2 = (f32[128,256]{1,0:T(8,128)}, f32[128,256]{1,0:T(8,128)}, f32[128,256]{1,0:T(8,128)}, f32[128,256]{1,0:T(8,128)}, f32[128,512]{1,0:T(8,128)}, /*ind...) custom-call(bf16[128,8192]{1,0:T(8,128)(2,1)} %hidden_ref.5, bf16[128,2048]{1,0:T(8,128)(2,1)} %copy-done.2, ...), custom_call_target="tpu_custom_call" | custom-call | flops 1610612736 | bytes 6815744 | tf_op jit(solution)/shard_map/multiply/pallas_call | solution.py:154
  66.2 2.1 %collective-permute-start.14 = (f32[128,256]{1,0:T(8,128)}, f32[128,256]{1,0:T(8,128)S(1)}, u32[]{:S(2)}, u32[]{:S(2)}) collective-permute-start(f32[128,256]{1,0:T(8,128)} %get-tuple-element.64), channel_id=1, source_target_pairs={{0,3},{1,2},{2,1},{3,0},{4,7},{5,6},{6,5},{7,4},{8,11},{9,10},{10,... | collective-permute-start | bytes 393224 | tf_op jit(solution)/shard_map/ppermute | solution.py:17
  69.3 4.5 %multiply.3 = (f32[128,512]{1,0:T(8,128)}, f32[128,512]{1,0:T(8,128)}, f32[128,512]{1,0:T(8,128)}, f32[128,512]{1,0:T(8,128)}) custom-call(bf16[128,8192]{1,0:T(8,128)(2,1)} %hidden_ref.5, bf16[128,2048]{1,0:T(8,128)(2,1)} %copy-done.2, bf16[128,2048]{1,0:T(8,128)(2,1)} %copy-done.3, bf16[128,2048]{1,0:T(8,128)(2,1)} %copy-done.4, ...), custom_call_target="tpu_custom_call" | custom-call | flops 1073741824 | bytes 5242880 | tf_op jit(solution)/shard_map/multiply/pallas_call | solution.py:154
  73.9 4.0 %collective-permute-done.12 = f32[128,256]{1,0:T(8,128)S(1)} collective-permute-done((f32[128,256]{1,0:T(8,128)}, f32[128,256]{1,0:T(8,128)S(1)}, u32[]{:S(2)}, u32[]{:S(2)}) %collective-permute-start.12) | collective-permute-done | bytes 131104 | tf_op jit(solution)/shard_map/ppermute | solution.py:17
  77.9 1.8 %collective-permute-start.17 = (f32[128,512]{1,0:T(8,128)S(1)}, f32[128,512]{1,0:T(8,128)S(1)}, u32[]{:S(2)}, u32[]{:S(2)}) collective-permute-start(f32[128,512]{1,0:T(8,128)S(1)} %copy-done.15), channel_id=1, source_target_pairs={{0,3},{1,2},{2,1},{3,0},{4,7},{5,6},{6,5},{7,4},{8,11},{9,10},{10,... | collective-permute-start | bytes 786440 | tf_op jit(solution)/shard_map/ppermute | solution.py:17
  79.7 3.3 %collective-permute-start.15 = (bf16[1,128,256]{2,1,0:T(8,128)(2,1)S(1)}, bf16[1,128,256]{2,1,0:T(8,128)(2,1)S(1)}, u32[]{:S(2)}, u32[]{:S(2)}) collective-permute-start(bf16[1,128,256]{2,1,0:T(8,128)(2,1)S(1)} %fusion.6), channel_id=1, source_target_pairs={{0,4},{1,5},{2,6},{3,7},{4,0},{5,1},{6,2},{7,3},{8,12},{9,13},{10,... | collective-permute-start | bytes 196616 | tf_op jit(solution)/shard_map/ppermute | solution.py:17
  83.1 3.4 %collective-permute-done.15 = bf16[1,128,256]{2,1,0:T(8,128)(2,1)S(1)} collective-permute-done((bf16[1,128,256]{2,1,0:T(8,128)(2,1)S(1)}, bf16[1,128,256]{2,1,0:T(8,128)(2,1)S(1)}, u32[]{:S(2)}, u32[]{:S(2)}) %collective-permute-start.15) | collective-permute-done | bytes 65568 | tf_op jit(solution)/shard_map/ppermute | solution.py:17
  88.0 2.9 %collective-permute-start.21 = (bf16[2,128,256]{2,1,0:T(8,128)(2,1)S(1)}, bf16[2,128,256]{2,1,0:T(8,128)(2,1)S(1)}, u32[]{:S(2)}, u32[]{:S(2)}) collective-permute-start(bf16[2,128,256]{2,1,0:T(8,128)(2,1)S(1)} %pad_maximum_fusion.5.rest_2_), channel_id=1, source_target_pairs={{0,3},{1,2},{2,1},{3,0},{4,7},{5,6},{6,5},{7,4},{8,11},{9,10},{10,... | collective-permute-start | bytes 393224 | tf_op jit(solution)/shard_map/ppermute | solution.py:17
  93.1 2.3 %collective-permute-done.21.rest_5_ = bf16[2,128,256]{2,1,0:T(8,128)(2,1)S(1)} collective-permute-done((bf16[2,128,256]{2,1,0:T(8,128)(2,1)S(1)}, bf16[2,128,256]{2,1,0:T(8,128)(2,1)S(1)}, u32[]{:S(2)}, u32[]{:S(2)}) %collective-permute-start.21) | collective-permute-done | bytes 131104 | tf_op jit(solution)/shard_map/ppermute | solution.py:17
  95.4 2.9 %collective-permute-start.23 = (f32[128,512]{1,0:T(8,128)}, f32[128,512]{1,0:T(8,128)S(1)}, u32[]{:S(2)}, u32[]{:S(2)}) collective-permute-start(f32[128,512]{1,0:T(8,128)} %get-tuple-element.80), channel_id=1, source_target_pairs={{0,2},{1,3},{2,0},{3,1},{4,6},{5,7},{6,4},{7,5},{8,10},{9,11},{10,... | collective-permute-start | bytes 786440 | tf_op jit(solution)/shard_map/ppermute | solution.py:17
  98.3 2.7 %collective-permute-start.24 = (f32[128,512]{1,0:T(8,128)}, f32[128,512]{1,0:T(8,128)S(1)}, u32[]{:S(2)}, u32[]{:S(2)}) collective-permute-start(f32[128,512]{1,0:T(8,128)} %get-tuple-element.81), channel_id=1, source_target_pairs={{0,3},{1,2},{2,1},{3,0},{4,7},{5,6},{6,5},{7,4},{8,11},{9,10},{10,... | collective-permute-start | bytes 786440 | tf_op jit(solution)/shard_map/ppermute | solution.py:17
  101.8 9.3 %attend.2 = (f32[2048,128]{1,0:T(8,128)}, f32[2048,128]{1,0:T(8,128)}) custom-call(s32[1,4]{1,0:T(1,128)} %len_ref.3, bf16[128,1024]{1,0:T(8,128)(2,1)} %d_ref.3, bf16[8,256,128]{2,1,0:T(8,128)(2,1)} %copy-done.6, bf16[8,256,128]{2,1,0:T(8,128)(2,1)} %copy-done.12, bf16[2,128,256]{2,1,0:T(8,128)(2,1)} %copy-done.8, bf16[2,128,256]{2,1,0:T(8,128)(2,1)} %copy-done.22, ...), custom_call_target="tpu_custom_call" | custom-call | flops 1610612736 | bytes 3145728 | tf_op jit(solution)/shard_map/attend/pallas_call | solution.py:290
  112.0 10.1 %attend.3 = (f32[2048,128]{1,0:T(8,128)}, f32[2048,128]{1,0:T(8,128)}) custom-call(s32[1,4]{1,0:T(1,128)} %len_ref.3, bf16[128,1024]{1,0:T(8,128)(2,1)} %d_ref.3, bf16[8,256,128]{2,1,0:T(8,128)(2,1)} %copy-done.6, bf16[8,256,128]{2,1,0:T(8,128)(2,1)} %copy-done.12, bf16[2,128,256]{2,1,0:T(8,128)(2,1)} %copy-done.8, bf16[2,128,256]{2,1,0:T(8,128)(2,1)} %copy-done.22, ...), custom_call_target="tpu_custom_call" | custom-call | flops 1610612736 | bytes 3145728 | tf_op jit(solution)/shard_map/attend/pallas_call | solution.py:290
  122.2 2.9 %collective-permute-done.25 = f32[2048,128]{1,0:T(8,128)S(1)} collective-permute-done((f32[2048,128]{1,0:T(8,128)}, f32[2048,128]{1,0:T(8,128)S(1)}, u32[]{:S(2)}, u32[]{:S(2)}) %collective-permute-start.25) | collective-permute-done | bytes 1048608 | tf_op jit(solution)/shard_map/ppermute | solution.py:17
  127.3 2.6 %collective-permute-start.32 = (bf16[256,128]{1,0:T(8,128)(2,1)S(1)}, bf16[256,128]{1,0:T(8,128)(2,1)S(1)}, u32[]{:S(2)}, u32[]{:S(2)}) collective-permute-start(bf16[256,128]{1,0:T(8,128)(2,1)S(1)} %get-tuple-element.93), channel_id=1, source_target_pairs={{0,7},{1,6},{2,5},{3,4},{4,3},{5,2},{6,1},{7,0},{8,15},{9,14},{10,... | collective-permute-start | bytes 196616 | tf_op jit(solution)/shard_map/ppermute | solution.py:17
  130.9 3.1 %collective-permute-start.30 = (bf16[256,128]{1,0:T(8,128)(2,1)S(1)}, bf16[256,128]{1,0:T(8,128)(2,1)S(1)}, u32[]{:S(2)}, u32[]{:S(2)}) collective-permute-start(bf16[256,128]{1,0:T(8,128)(2,1)S(1)} %get-tuple-element.95), channel_id=1, source_target_pairs={{0,5},{1,4},{2,7},{3,6},{4,1},{5,0},{6,3},{7,2},{8,13},{9,12},{10,... | collective-permute-start | bytes 196616 | tf_op jit(solution)/shard_map/ppermute | solution.py:17
  134.1 2.1 %collective-permute-start.28 = (bf16[256,128]{1,0:T(8,128)(2,1)S(1)}, bf16[256,128]{1,0:T(8,128)(2,1)S(1)}, u32[]{:S(2)}, u32[]{:S(2)}) collective-permute-start(bf16[256,128]{1,0:T(8,128)(2,1)S(1)} %get-tuple-element.97), channel_id=1, source_target_pairs={{0,6},{1,7},{2,4},{3,5},{4,2},{5,3},{6,0},{7,1},{8,14},{9,15},{10,... | collective-permute-start | bytes 196616 | tf_op jit(solution)/shard_map/ppermute | solution.py:17
  137.4 2.1 %collective-permute-done.30 = bf16[256,128]{1,0:T(8,128)(2,1)S(1)} collective-permute-done((bf16[256,128]{1,0:T(8,128)(2,1)S(1)}, bf16[256,128]{1,0:T(8,128)(2,1)S(1)}, u32[]{:S(2)}, u32[]{:S(2)}) %collective-permute-start.30) | collective-permute-done | bytes 65568 | tf_op jit(solution)/shard_map/ppermute | solution.py:17
  142.4 4.4 %collective-permute-done.33 = f32[256,128]{1,0:T(8,128)S(1)} collective-permute-done((f32[256,128]{1,0:T(8,128)S(1)}, f32[256,128]{1,0:T(8,128)S(1)}, u32[]{:S(2)}, u32[]{:S(2)}) %collective-permute-start.33) | collective-permute-done | bytes 131104 | tf_op jit(solution)/shard_map/ppermute | solution.py:17
  (112 shorter events, 30.6 us)
Async XLA Ops:
  3.8 33.2 %collective-permute-start.1 = (bf16[640,512]{1,0:T(8,128)(2,1)}, bf16[640,512]{1,0:T(8,128)(2,1)S(1)}, u32[]{:S(2)}, u32[]{:S(2)}) collective-permute-start(bf16[640,512]{1,0:T(8,128)(2,1)} %get-tuple-element.46), channel_id=1, source_target_pairs={{0,4},{1,5},{2,6},{3,7},{4,0},{5,1},{6,2},{7,3},{8,12},{9,13},{10,... | collective-permute-start | bytes 1966088 | tf_op jit(solution)/shard_map/ppermute | solution.py:17
  7.9 39.5 %collective-permute-start.3 = (bf16[128,2048]{1,0:T(8,128)(2,1)}, bf16[128,2048]{1,0:T(8,128)(2,1)S(1)}, u32[]{:S(2)}, u32[]{:S(2)}) collective-permute-start(bf16[128,2048]{1,0:T(8,128)(2,1)} %get-tuple-element.47), channel_id=1, source_target_pairs={{0,1},{1,0},{2,3},{3,2},{4,5},{5,4},{6,7},{7,6},{8,9},{9,8},{10,11... | collective-permute-start | bytes 1572872 | tf_op jit(solution)/shard_map/ppermute | solution.py:17
  9.4 38.0 %collective-permute-start.4 = (bf16[128,2048]{1,0:T(8,128)(2,1)}, bf16[128,2048]{1,0:T(8,128)(2,1)S(1)}, u32[]{:S(2)}, u32[]{:S(2)}) collective-permute-start(bf16[128,2048]{1,0:T(8,128)(2,1)} %get-tuple-element.48), channel_id=1, source_target_pairs={{0,2},{1,3},{2,0},{3,1},{4,6},{5,7},{6,4},{7,5},{8,10},{9,11},{10,... | collective-permute-start | bytes 1572872 | tf_op jit(solution)/shard_map/ppermute | solution.py:17
  11.0 37.2 %collective-permute-start.5 = (bf16[128,2048]{1,0:T(8,128)(2,1)}, bf16[128,2048]{1,0:T(8,128)(2,1)S(1)}, u32[]{:S(2)}, u32[]{:S(2)}) collective-permute-start(bf16[128,2048]{1,0:T(8,128)(2,1)} %get-tuple-element.49), channel_id=1, source_target_pairs={{0,3},{1,2},{2,1},{3,0},{4,7},{5,6},{6,5},{7,4},{8,11},{9,10},{10,... | collective-permute-start | bytes 1572872 | tf_op jit(solution)/shard_map/ppermute | solution.py:17
  37.0 10.3 %collective-permute-start.2 = (bf16[1,384,512]{2,1,0:T(8,128)(2,1)S(1)}, bf16[1,384,512]{2,1,0:T(8,128)(2,1)S(1)}, u32[]{:S(2)}, u32[]{:S(2)}) collective-permute-start(bf16[1,384,512]{2,1,0:T(8,128)(2,1)S(1)} %slice_bitcast_fusion), channel_id=1, source_target_pairs={{0,16},{8,24},{16,0},{24,8},{1,17},{9,25},{17,1},{25,9},{2,18},{10... | collective-permute-start | bytes 1179656 | tf_op jit(solution)/shard_map/ppermute | solution.py:17
  38.6 7.4 %collective-permute-start = (bf16[1,256,128]{2,1,0:T(8,128)(2,1)S(1)}, bf16[1,256,128]{2,1,0:T(8,128)(2,1)S(1)}, u32[]{:S(2)}, u32[]{:S(2)}) collective-permute-start(bf16[1,256,128]{2,1,0:T(8,128)(2,1)S(1)} %select_bitcast_fusion), channel_id=1, source_target_pairs={{0,4},{1,5},{2,6},{3,7},{4,0},{5,1},{6,2},{7,3},{8,12},{9,13},{10,... | collective-permute-start | bytes 196616 | tf_op jit(solution)/shard_map/ppermute | solution.py:17
  48.2 8.8 %collective-permute-start.6 = (bf16[1,256,512]{2,1,0:T(8,128)(2,1)S(1)}, bf16[1,256,512]{2,1,0:T(8,128)(2,1)S(1)}, u32[]{:S(2)}, u32[]{:S(2)}) collective-permute-start(bf16[1,256,512]{2,1,0:T(8,128)(2,1)S(1)} %slice_bitcast_fusion.1), channel_id=1, source_target_pairs={{0,16},{8,24},{16,0},{24,8},{1,17},{9,25},{17,1},{25,9},{2,18},{10... | collective-permute-start | bytes 786440 | tf_op jit(solution)/shard_map/ppermute | solution.py:17
  55.5 7.7 %collective-permute-start.9 = (bf16[4,256,128]{2,1,0:T(8,128)(2,1)S(1)}, bf16[4,256,128]{2,1,0:T(8,128)(2,1)S(1)}, u32[]{:S(2)}, u32[]{:S(2)}) collective-permute-start(bf16[4,256,128]{2,1,0:T(8,128)(2,1)S(1)} %pad_maximum_fusion.3), channel_id=1, source_target_pairs={{0,1},{1,0},{2,3},{3,2},{4,5},{5,4},{6,7},{7,6},{8,9},{9,8},{10,11... | collective-permute-start | bytes 786440 | tf_op jit(solution)/shard_map/ppermute | solution.py:17
  63.3 16.4 %collective-permute-start.11 = (f32[128,512]{1,0:T(8,128)}, f32[128,512]{1,0:T(8,128)S(1)}, u32[]{:S(2)}, u32[]{:S(2)}) collective-permute-start(f32[128,512]{1,0:T(8,128)} %get-tuple-element.60), channel_id=1, source_target_pairs={{0,1},{1,0},{2,3},{3,2},{4,5},{5,4},{6,7},{7,6},{8,9},{9,8},{10,11... | collective-permute-start | bytes 786440 | tf_op jit(solution)/shard_map/ppermute | solution.py:17
  64.9 13.0 %collective-permute-start.12 = (f32[128,256]{1,0:T(8,128)}, f32[128,256]{1,0:T(8,128)S(1)}, u32[]{:S(2)}, u32[]{:S(2)}) collective-permute-start(f32[128,256]{1,0:T(8,128)} %get-tuple-element.62), channel_id=1, source_target_pairs={{0,1},{1,0},{2,3},{3,2},{4,5},{5,4},{6,7},{7,6},{8,9},{9,8},{10,11... | collective-permute-start | bytes 393224 | tf_op jit(solution)/shard_map/ppermute | solution.py:17
  65.4 14.3 %collective-permute-start.13 = (f32[128,256]{1,0:T(8,128)}, f32[128,256]{1,0:T(8,128)S(1)}, u32[]{:S(2)}, u32[]{:S(2)}) collective-permute-start(f32[128,256]{1,0:T(8,128)} %get-tuple-element.63), channel_id=1, source_target_pairs={{0,2},{1,3},{2,0},{3,1},{4,6},{5,7},{6,4},{7,5},{8,10},{9,11},{10,... | collective-permute-start | bytes 393224 | tf_op jit(solution)/shard_map/ppermute | solution.py:17
  66.2 13.4 %collective-permute-start.14 = (f32[128,256]{1,0:T(8,128)}, f32[128,256]{1,0:T(8,128)S(1)}, u32[]{:S(2)}, u32[]{:S(2)}) collective-permute-start(f32[128,256]{1,0:T(8,128)} %get-tuple-element.64), channel_id=1, source_target_pairs={{0,3},{1,2},{2,1},{3,0},{4,7},{5,6},{6,5},{7,4},{8,11},{9,10},{10,... | collective-permute-start | bytes 393224 | tf_op jit(solution)/shard_map/ppermute | solution.py:17
  68.4 18.1 %collective-permute-start.16 = (f32[128,512]{1,0:T(8,128)}, f32[128,512]{1,0:T(8,128)S(1)}, u32[]{:S(2)}, u32[]{:S(2)}) collective-permute-start(f32[128,512]{1,0:T(8,128)} %get-tuple-element.74), channel_id=1, source_target_pairs={{0,2},{1,3},{2,0},{3,1},{4,6},{5,7},{6,4},{7,5},{8,10},{9,11},{10,... | collective-permute-start | bytes 786440 | tf_op jit(solution)/shard_map/ppermute | solution.py:17
  77.9 10.2 %collective-permute-start.17 = (f32[128,512]{1,0:T(8,128)S(1)}, f32[128,512]{1,0:T(8,128)S(1)}, u32[]{:S(2)}, u32[]{:S(2)}) collective-permute-start(f32[128,512]{1,0:T(8,128)S(1)} %copy-done.15), channel_id=1, source_target_pairs={{0,3},{1,2},{2,1},{3,0},{4,7},{5,6},{6,5},{7,4},{8,11},{9,10},{10,... | collective-permute-start | bytes 786440 | tf_op jit(solution)/shard_map/ppermute | solution.py:17
  88.0 12.9 %collective-permute-start.18 = (bf16[8,256,128]{2,1,0:T(8,128)(2,1)S(1)}, bf16[8,256,128]{2,1,0:T(8,128)(2,1)S(1)}, u32[]{:S(2)}, u32[]{:S(2)}) collective-permute-start(bf16[8,256,128]{2,1,0:T(8,128)(2,1)S(1)} %pad_maximum_fusion.2.rest_0_), channel_id=1, source_target_pairs={{0,8},{8,0},{16,24},{24,16},{1,9},{9,1},{17,25},{25,17},{2,10},{10... | collective-permute-start | bytes 1572872 | tf_op jit(solution)/shard_map/ppermute | solution.py:17
  88.0 7.3 %collective-permute-start.21 = (bf16[2,128,256]{2,1,0:T(8,128)(2,1)S(1)}, bf16[2,128,256]{2,1,0:T(8,128)(2,1)S(1)}, u32[]{:S(2)}, u32[]{:S(2)}) collective-permute-start(bf16[2,128,256]{2,1,0:T(8,128)(2,1)S(1)} %pad_maximum_fusion.5.rest_2_), channel_id=1, source_target_pairs={{0,3},{1,2},{2,1},{3,0},{4,7},{5,6},{6,5},{7,4},{8,11},{9,10},{10,... | collective-permute-start | bytes 393224 | tf_op jit(solution)/shard_map/ppermute | solution.py:17
  91.1 9.9 %collective-permute-start.19 = (bf16[2,128,256]{2,1,0:T(8,128)(2,1)S(1)}, bf16[2,128,256]{2,1,0:T(8,128)(2,1)S(1)}, u32[]{:S(2)}, u32[]{:S(2)}) collective-permute-start(bf16[2,128,256]{2,1,0:T(8,128)(2,1)S(1)} %pad_maximum_fusion.5.rest_2_), channel_id=1, source_target_pairs={{0,1},{1,0},{2,3},{3,2},{4,5},{5,4},{6,7},{7,6},{8,9},{9,8},{10,11... | collective-permute-start | bytes 393224 | tf_op jit(solution)/shard_map/ppermute | solution.py:17
  92.5 18.6 %collective-permute-start.22 = (f32[128,512]{1,0:T(8,128)}, f32[128,512]{1,0:T(8,128)S(1)}, u32[]{:S(2)}, u32[]{:S(2)}) collective-permute-start(f32[128,512]{1,0:T(8,128)} %get-tuple-element.79), channel_id=1, source_target_pairs={{0,1},{1,0},{2,3},{3,2},{4,5},{5,4},{6,7},{7,6},{8,9},{9,8},{10,11... | collective-permute-start | bytes 786440 | tf_op jit(solution)/shard_map/ppermute | solution.py:17
  95.4 15.7 %collective-permute-start.23 = (f32[128,512]{1,0:T(8,128)}, f32[128,512]{1,0:T(8,128)S(1)}, u32[]{:S(2)}, u32[]{:S(2)}) collective-permute-start(f32[128,512]{1,0:T(8,128)} %get-tuple-element.80), channel_id=1, source_target_pairs={{0,2},{1,3},{2,0},{3,1},{4,6},{5,7},{6,4},{7,5},{8,10},{9,11},{10,... | collective-permute-start | bytes 786440 | tf_op jit(solution)/shard_map/ppermute | solution.py:17
  98.3 12.9 %collective-permute-start.24 = (f32[128,512]{1,0:T(8,128)}, f32[128,512]{1,0:T(8,128)S(1)}, u32[]{:S(2)}, u32[]{:S(2)}) collective-permute-start(f32[128,512]{1,0:T(8,128)} %get-tuple-element.81), channel_id=1, source_target_pairs={{0,3},{1,2},{2,1},{3,0},{4,7},{5,6},{6,5},{7,4},{8,11},{9,10},{10,... | collective-permute-start | bytes 786440 | tf_op jit(solution)/shard_map/ppermute | solution.py:17
  126.5 7.6 %collective-permute-start.26 = (bf16[256,128]{1,0:T(8,128)(2,1)S(1)}, bf16[256,128]{1,0:T(8,128)(2,1)S(1)}, u32[]{:S(2)}, u32[]{:S(2)}) collective-permute-start(bf16[256,128]{1,0:T(8,128)(2,1)S(1)} %get-tuple-element.92), channel_id=1, source_target_pairs={{0,4},{1,5},{2,6},{3,7},{4,0},{5,1},{6,2},{7,3},{8,12},{9,13},{10,... | collective-permute-start | bytes 196616 | tf_op jit(solution)/shard_map/ppermute | solution.py:17
  127.3 8.8 %collective-permute-start.32 = (bf16[256,128]{1,0:T(8,128)(2,1)S(1)}, bf16[256,128]{1,0:T(8,128)(2,1)S(1)}, u32[]{:S(2)}, u32[]{:S(2)}) collective-permute-start(bf16[256,128]{1,0:T(8,128)(2,1)S(1)} %get-tuple-element.93), channel_id=1, source_target_pairs={{0,7},{1,6},{2,5},{3,4},{4,3},{5,2},{6,1},{7,0},{8,15},{9,14},{10,... | collective-permute-start | bytes 196616 | tf_op jit(solution)/shard_map/ppermute | solution.py:17
  130.0 7.4 %collective-permute-start.31 = (bf16[256,128]{1,0:T(8,128)(2,1)S(1)}, bf16[256,128]{1,0:T(8,128)(2,1)S(1)}, u32[]{:S(2)}, u32[]{:S(2)}) collective-permute-start(bf16[256,128]{1,0:T(8,128)(2,1)S(1)} %get-tuple-element.94), channel_id=1, source_target_pairs={{0,3},{1,2},{2,1},{3,0},{4,7},{5,6},{6,5},{7,4},{8,11},{9,10},{10,... | collective-permute-start | bytes 196616 | tf_op jit(solution)/shard_map/ppermute | solution.py:17
  130.9 8.6 %collective-permute-start.30 = (bf16[256,128]{1,0:T(8,128)(2,1)S(1)}, bf16[256,128]{1,0:T(8,128)(2,1)S(1)}, u32[]{:S(2)}, u32[]{:S(2)}) collective-permute-start(bf16[256,128]{1,0:T(8,128)(2,1)S(1)} %get-tuple-element.95), channel_id=1, source_target_pairs={{0,5},{1,4},{2,7},{3,6},{4,1},{5,0},{6,3},{7,2},{8,13},{9,12},{10,... | collective-permute-start | bytes 196616 | tf_op jit(solution)/shard_map/ppermute | solution.py:17
  (34 other events, 302.8 us)

commit v3 on v2

--- a/solution.py
+++ b/solution.py
@@ -173,45 +173,52 @@
 def attend(lengths, terms, d_attn, first_head, cache, group, g_order, sums):
     tokens = d_attn.shape[0]
     n_blocks, block, head_dim = cache[0].shape
-    slots = n_blocks // len(group)
     n_convs = lengths.shape[1]
     scale = head_dim ** (-0.5)
     to_log2 = scale * math.log2(math.e)
     n_heads = terms[0].shape[1] // head_dim
-    pair = 2 if n_heads % 2 == 0 else 1
-    lanes = pair * tokens
+    lanes = n_heads * tokens
     n_cache = n_blocks * block
     n_group = n_blocks * tokens
-    chunk = 512
+    slots = n_blocks // len(group)
+    chunk = min(512, n_cache)
     n_part, n_sum = len(terms), len(sums)
+    dims = (((1,), (1,)), ((), ()))
+    spans = [(at, chunk) for at in range(0, n_cache, chunk)]
+    spans += [(n_cache + i * slots * tokens, slots * tokens) for i in range(len(group))]
+    n_first = n_cache // chunk
+
+    def tiles(value):
+        return value.reshape(value.shape[0] // 8, 8, lanes)
 
     def body(len_ref, d_ref, *rest):
         cache_refs, rest = rest[:2], rest[2:]
         group_refs, rest = rest[: len(group)], rest[len(group) :]
         part_refs, rest = rest[:n_part], rest[n_part:]
         sum_refs, rest = rest[:n_sum], rest[n_sum:]
-        keep_ref, give_ref, gk, gv, s_ref, p_ref, q_ref, ck_ref, cv_ref, sems = rest
+        keep_ref, give_ref, out_ref, s_ref, p_ref, q_ref, dq_ref, ck_ref, cv_ref, sems = rest
         me, dp = lax.axis_index("fsdp"), lax.axis_index("dp")
-        even = dp % 2 == 0
-
-        @pl.when(even)
+        odd = dp % 2
+
+        @pl.when(odd == 0)
         def _():
             pltpu.make_async_copy(cache_refs[0], ck_ref, sems.at[0]).start()
             pltpu.make_async_copy(cache_refs[1], cv_ref, sems.at[1]).start()
 
-        @pl.when(jnp.logical_not(even))
+        @pl.when(odd == 1)
         def _():
             pltpu.make_async_copy(cache_refs[1], ck_ref, sems.at[0]).start()
             pltpu.make_async_copy(cache_refs[0], cv_ref, sems.at[1]).start()
 
         for h in range(n_heads):
             at = slice(h * head_dim, (h + 1) * head_dim)
+            rows = pl.ds(h * tokens, tokens)
             q = part_refs[0][:, at]
             for ref in part_refs[1:]:
                 q = q + ref[:, at]
-            q_ref[h, 0] = q.astype(BF16)
+            q_ref[rows] = q.astype(BF16)
             at = (first_head + h) * head_dim
-            q_ref[h, 1] = d_ref[:, at : at + head_dim]
+            dq_ref[rows] = d_ref[:, at : at + head_dim]
 
         q_pos = me * tokens + lax.broadcasted_iota(jnp.int32, (1, lanes), 1) % tokens
         begin = jnp.zeros((1, lanes), jnp.int32)
@@ -220,73 +227,74 @@
             end = end + len_ref[0, i]
             begin = jnp.where(end <= q_pos, end, begin)
 
+        def group_rows(i, at):
+            return group_refs[i][...].reshape(slots * tokens, 2 * head_dim)[:, at : at + head_dim]
+
+        def cache_rows(ref, i):
+            return ref[...].reshape(n_cache, head_dim)[i * chunk : (i + 1) * chunk]
+
+        for i in range(len(group)):
+            at, size = spans[n_first + i]
+            s = lax.dot_general(group_rows(i, 0), q_ref[...], dims, preferred_element_type=F32)
+            for j in range(slots):
+                pos = (me ^ g_order[i * slots + j]) * tokens
+                pos = pos + lax.broadcasted_iota(jnp.int32, (tokens, lanes), 0)
+                allowed = (pos <= q_pos) & (pos >= begin)
+                here = s[j * tokens : (j + 1) * tokens]
+                s_ref[pl.ds(at + j * tokens, tokens)] = jnp.where(allowed, here, -jnp.inf)
+
         pltpu.make_async_copy(cache_refs[0], ck_ref, sems.at[0]).wait()
         pltpu.make_async_copy(cache_refs[1], cv_ref, sems.at[1]).wait()
-
-        @pl.loop(0, n_heads // pair)
-        def _(step):
-            rows_q = jnp.concatenate([q_ref[step * pair + i, 0] for i in range(pair)], axis=0)
-            rows_d = jnp.concatenate([q_ref[step * pair + i, 1] for i in range(pair)], axis=0)
-            dims = (((1,), (1,)), ((), ()))
-            top = jnp.full((1, lanes), -jnp.inf, F32)
-            cache_spans = [
-                (b, r, min(chunk, block)) for b in range(n_blocks) for r in range(0, block, min(chunk, block))
-            ]
-            for b, r, size in cache_spans:
-                s = lax.dot_general(
-                    ck_ref[b, r : r + size], rows_q, dims, preferred_element_type=F32
-                )
-                s_ref[pl.ds(b * block + r, size)] = s
-                top = jnp.maximum(top, jnp.max(s, axis=0, keepdims=True))
-            for b in range(n_blocks):
-                s = lax.dot_general(group_refs[b // slots][b % slots, :, :head_dim], rows_q, dims, preferred_element_type=F32)
-                pos = (me ^ g_order[b]) * tokens + lax.broadcasted_iota(jnp.int32, (tokens, lanes), 0)
-                s = jnp.where((pos <= q_pos) & (pos >= begin), s, -jnp.inf)
-                s_ref[pl.ds(n_cache + b * tokens, tokens)] = s
-                top = jnp.maximum(top, jnp.max(s, axis=0, keepdims=True))
-            total = jnp.zeros((1, lanes), F32)
-            for r in range(0, n_cache + n_group, chunk):
-                e = jnp.exp2((s_ref[pl.ds(r, chunk)] - top) * to_log2)
-                s_ref[pl.ds(r, chunk)] = e
-                total = total + jnp.sum(e, axis=0, keepdims=True)
-            inv = 1.0 / total
-            delta = jnp.zeros((1, lanes), F32)
-            for b in range(n_blocks):
-                p = s_ref[pl.ds(n_cache + b * tokens, tokens)] * inv
-                dp_ = lax.dot_general(group_refs[b // slots][b % slots, :, head_dim:], rows_d, dims, preferred_element_type=F32)
-                delta = delta + jnp.sum(p.astype(BF16).astype(F32) * dp_, axis=0, keepdims=True)
-            for b, r, size in cache_spans:
-                at = pl.ds(b * block + r, size)
-                p = s_ref[at] * inv
-                pb = p.astype(BF16)
-                dp_ = lax.dot_general(
-                    cv_ref[b, r : r + size], rows_d, dims, preferred_element_type=F32
-                )
-                s_ref[at] = p
-                p_ref[at] = dp_
-                delta = delta + jnp.sum(pb.astype(F32) * dp_, axis=0, keepdims=True)
-                g = jnp.dot(pb, rows_d, preferred_element_type=F32)
-                gv[at] = jnp.where(step == 0, 0.0, gv[at]) + g
-            for b, r, size in cache_spans:
-                at = pl.ds(b * block + r, size)
-                ds = (s_ref[at] * (p_ref[at] - delta)).astype(BF16)
-                g = jnp.dot(ds, rows_q, preferred_element_type=F32)
-                gk[at] = jnp.where(step == 0, 0.0, gk[at]) + g
-
-        keep_in, give_in = (sum_refs[0][...], sum_refs[1][...]) if n_sum else (0.0, 0.0)
-
-        @pl.when(even)
-        def _():
-            keep_ref[...] = keep_in + gk[...] * scale
-            give_ref[...] = give_in + gv[...]
-
-        @pl.when(jnp.logical_not(even))
-        def _():
-            keep_ref[...] = keep_in + gv[...]
-            give_ref[...] = give_in + gk[...] * scale
-
-    rows = n_heads * tokens
-    flops = 2 * rows * head_dim * (5 * n_cache + 2 * n_group)
+        for i in range(n_first):
+            at, size = spans[i]
+            s_ref[pl.ds(at, size)] = lax.dot_general(
+                cache_rows(ck_ref, i), q_ref[...], dims, preferred_element_type=F32
+            )
+
+        tops, totals = [], []
+        for at, size in spans:
+            top = jnp.max(tiles(s_ref[pl.ds(at, size)]), axis=0)
+            top = jnp.maximum(top, -1e30)
+            e = jnp.exp2((tiles(s_ref[pl.ds(at, size)]) - top) * to_log2)
+            s_ref[pl.ds(at, size)] = e.reshape(size, lanes)
+            tops.append(top)
+            totals.append(jnp.sum(e, axis=0))
+        top = functools.reduce(jnp.maximum, tops)
+        top = jnp.max(top, axis=0, keepdims=True)
+        factors = [jnp.exp2((own - top) * to_log2) for own in tops]
+        total = functools.reduce(lambda a, b: a + b, [t * f for t, f in zip(totals, factors)])
+        inv = 1.0 / jnp.sum(total, axis=0, keepdims=True)
+        factors = [f * inv for f in factors]
+
+        delta = jnp.zeros((8, lanes), F32)
+        for i in range(len(group)):
+            at, size = spans[n_first + i]
+            d_prob = lax.dot_general(
+                group_rows(i, head_dim), dq_ref[...], dims, preferred_element_type=F32
+            )
+            p = tiles(s_ref[pl.ds(at, size)]) * factors[n_first + i]
+            delta = delta + jnp.sum(p.astype(BF16).astype(F32) * tiles(d_prob), axis=0)
+        for i in range(n_first):
+            at, size = spans[i]
+            p_ref[pl.ds(at, size)] = lax.dot_general(
+                cache_rows(cv_ref, i), dq_ref[...], dims, preferred_element_type=F32
+            )
+            p = (tiles(s_ref[pl.ds(at, size)]) * factors[i]).reshape(size, lanes).astype(BF16)
+            delta = delta + jnp.sum(tiles(p.astype(F32)) * tiles(p_ref[pl.ds(at, size)]), axis=0)
+            out_ref[1 - odd, pl.ds(at, size)] = jnp.dot(p, dq_ref[...], preferred_element_type=F32)
+        delta = jnp.sum(delta, axis=0, keepdims=True)
+        for i in range(n_first):
+            at, size = spans[i]
+            p = tiles(s_ref[pl.ds(at, size)]) * factors[i]
+            ds = p * (tiles(p_ref[pl.ds(at, size)]) - delta)
+            ds = ds.reshape(size, lanes).astype(BF16)
+            g = jnp.dot(ds, q_ref[...], preferred_element_type=F32) * scale
+            out_ref[odd, pl.ds(at, size)] = g
+
+        for i, ref in enumerate((keep_ref, give_ref)):
+            ref[...] = sum_refs[i][...] + out_ref[i] if n_sum else out_ref[i]
+
+    flops = 2 * lanes * head_dim * (5 * n_cache + 2 * n_group)
     return pl.pallas_call(
         body,
         in_specs=[pl.BlockSpec(memory_space=pltpu.SMEM)]
@@ -296,11 +304,11 @@
         out_specs=[pl.BlockSpec(memory_space=pltpu.VMEM)] * 2,
         out_shape=[jax.ShapeDtypeStruct((n_cache, head_dim), F32)] * 2,
         scratch_shapes=[
-            pltpu.VMEM((n_cache, head_dim), F32),
-            pltpu.VMEM((n_cache, head_dim), F32),
+            pltpu.VMEM((2, n_cache, head_dim), F32),
             pltpu.VMEM((n_cache + n_group, lanes), F32),
             pltpu.VMEM((n_cache, lanes), F32),
-            pltpu.VMEM((n_heads, 2, tokens, head_dim), BF16),
+            pltpu.VMEM((lanes, head_dim), BF16),
+            pltpu.VMEM((lanes, head_dim), BF16),
             pltpu.VMEM((n_blocks, block, head_dim), BF16),
             pltpu.VMEM((n_blocks, block, head_dim), BF16),
             pltpu.SemaphoreType.DMA((2,)),
@@ -309,7 +317,7 @@
         cost_estimate=pl.CostEstimate(
             flops=flops,
             bytes_accessed=12 * n_cache * head_dim,
-            transcendentals=rows * (n_cache + n_group),
+            transcendentals=lanes * (n_cache + n_group),
         ),
         name="attend",
     )(lengths, d_attn, *cache, *group, *terms, *sums)

time: 149 us -> 147 us (0.987)
  Pallas kernels: 32.9 us -> 31.3 us
    pallas_call x2, Pallas kernels: 19.4 us -> 17.8 us  [attend(): pl.pallas_call(body, in_specs=[pl.BlockSpec(memory_space=pltpu.SMEM)] + [...]
where the time goes in v3:
time: 147 us
  waiting for transfers between devices  63.4 us (43%)
  starting transfers between devices  47.2 us (32%)
  Pallas kernels  31.3 us (21%)
  other arithmetic  2.43 us (2%)
  local copies, waits for them, and re-layouts  1.78 us (1%)
    ppermute x35, waiting for transfers between devices, swap(): return lax.ppermute(value, axis, [(i, i ^ bit) for i in range(size)])  63.4 us
    ppermute x35, starting transfers between devices, swap(): return lax.ppermute(value, axis, [(i, i ^ bit) for i in range(size)])  47.2 us
    pallas_call x2, Pallas kernels, attend(): pl.pallas_call(body, in_specs=[pl.BlockSpec(memory_space=pltpu.SMEM)] + [...  17.8 us
    pallas_call x2, Pallas kernels, multiply(): pl.pallas_call(body, in_specs=[pl.BlockSpec(memory_space=pl.ANY)] * (1 +...  10.4 us
    pallas_call x1, Pallas kernels, prepare(): pl.pallas_call(body, in_specs=[pl.BlockSpec(memory_space=pl.ANY)] * 4, ou...  3.11 us
  transfers between devices with their start and end apart: 35, of which 16 were waited for; matrix products, arithmetic and copies ran while one was open for 0% of the time, Pallas kernels for 13%

profile of v3, /device:TPU:0, one launch (start us, length us, event | category | flops | bytes accessed | tf_op | source)
XLA Modules:
  0.0 147.2 jit_solution(4281353923252769279)
XLA Ops:
  0.6 3.1 %prepare.1 = (bf16[128,2048]{1,0:T(8,128)(2,1)}, bf16[128,2048]{1,0:T(8,128)(2,1)}, bf16[128,2048]{1,0:T(8,128)(2,1)}, bf16[640,512]{1,0:T(8,128)(2,1)}) custom-call(bf16[128,8192]{1,0:T(8,128)(2,1)} %hidden_ref.5, bf16[1024,1024]{1,0:T(8,128)(2,1)} %rest_3_.3, bf16[1024,128]{1,0:T(8,128)(2,1)} %rest_3_.2, bf16[1024,128]{1,0:T(8,128)(2,1)} %rest_4_.1), custom_call_target="tpu_custom_call" | custom-call | bytes 4456448 | tf_op jit(solution)/shard_map/prepare/pallas_call | solution.py:83
  3.8 4.1 %collective-permute-start.1 = (bf16[640,512]{1,0:T(8,128)(2,1)}, bf16[640,512]{1,0:T(8,128)(2,1)S(1)}, u32[]{:S(2)}, u32[]{:S(2)}) collective-permute-start(bf16[640,512]{1,0:T(8,128)(2,1)} %get-tuple-element.46), channel_id=1, source_target_pairs={{0,4},{1,5},{2,6},{3,7},{4,0},{5,1},{6,2},{7,3},{8,12},{9,13},{10,... | collective-permute-start | bytes 1966088 | tf_op jit(solution)/shard_map/ppermute | solution.py:17
  11.4 25.6 %collective-permute-done.1 = bf16[640,512]{1,0:T(8,128)(2,1)S(1)} collective-permute-done((bf16[640,512]{1,0:T(8,128)(2,1)}, bf16[640,512]{1,0:T(8,128)(2,1)S(1)}, u32[]{:S(2)}, u32[]{:S(2)}) %collective-permute-start.1) | collective-permute-done | bytes 655392 | tf_op jit(solution)/shard_map/ppermute | solution.py:17
  38.7 7.3 %collective-permute-done = bf16[1,256,128]{2,1,0:T(8,128)(2,1)S(1)} collective-permute-done((bf16[1,256,128]{2,1,0:T(8,128)(2,1)S(1)}, bf16[1,256,128]{2,1,0:T(8,128)(2,1)S(1)}, u32[]{:S(2)}, u32[]{:S(2)}) %collective-permute-start) | collective-permute-done | bytes 65568 | tf_op jit(solution)/shard_map/ppermute | solution.py:17
  50.7 4.8 %collective-permute-done.7 = bf16[2,256,128]{2,1,0:T(8,128)(2,1)S(1)} collective-permute-done((bf16[2,256,128]{2,1,0:T(8,128)(2,1)S(1)}, bf16[2,256,128]{2,1,0:T(8,128)(2,1)S(1)}, u32[]{:S(2)}, u32[]{:S(2)}) %collective-permute-start.7) | collective-permute-done | bytes 131104 | tf_op jit(solution)/shard_map/ppermute | solution.py:17
  57.2 5.8 %multiply.2 = (f32[128,256]{1,0:T(8,128)}, f32[128,256]{1,0:T(8,128)}, f32[128,256]{1,0:T(8,128)}, f32[128,256]{1,0:T(8,128)}, f32[128,512]{1,0:T(8,128)}, /*ind...) custom-call(bf16[128,8192]{1,0:T(8,128)(2,1)} %hidden_ref.5, bf16[128,2048]{1,0:T(8,128)(2,1)} %copy-done.2, ...), custom_call_target="tpu_custom_call" | custom-call | flops 1610612736 | bytes 6815744 | tf_op jit(solution)/shard_map/multiply/pallas_call | solution.py:154
  66.2 2.1 %collective-permute-start.14 = (f32[128,256]{1,0:T(8,128)}, f32[128,256]{1,0:T(8,128)S(1)}, u32[]{:S(2)}, u32[]{:S(2)}) collective-permute-start(f32[128,256]{1,0:T(8,128)} %get-tuple-element.64), channel_id=1, source_target_pairs={{0,3},{1,2},{2,1},{3,0},{4,7},{5,6},{6,5},{7,4},{8,11},{9,10},{10,... | collective-permute-start | bytes 393224 | tf_op jit(solution)/shard_map/ppermute | solution.py:17
  69.3 4.5 %multiply.3 = (f32[128,512]{1,0:T(8,128)}, f32[128,512]{1,0:T(8,128)}, f32[128,512]{1,0:T(8,128)}, f32[128,512]{1,0:T(8,128)}) custom-call(bf16[128,8192]{1,0:T(8,128)(2,1)} %hidden_ref.5, bf16[128,2048]{1,0:T(8,128)(2,1)} %copy-done.2, bf16[128,2048]{1,0:T(8,128)(2,1)} %copy-done.3, bf16[128,2048]{1,0:T(8,128)(2,1)} %copy-done.4, ...), custom_call_target="tpu_custom_call" | custom-call | flops 1073741824 | bytes 5242880 | tf_op jit(solution)/shard_map/multiply/pallas_call | solution.py:154
  73.9 4.0 %collective-permute-done.12 = f32[128,256]{1,0:T(8,128)S(1)} collective-permute-done((f32[128,256]{1,0:T(8,128)}, f32[128,256]{1,0:T(8,128)S(1)}, u32[]{:S(2)}, u32[]{:S(2)}) %collective-permute-start.12) | collective-permute-done | bytes 131104 | tf_op jit(solution)/shard_map/ppermute | solution.py:17
  77.9 1.8 %collective-permute-start.17 = (f32[128,512]{1,0:T(8,128)S(1)}, f32[128,512]{1,0:T(8,128)S(1)}, u32[]{:S(2)}, u32[]{:S(2)}) collective-permute-start(f32[128,512]{1,0:T(8,128)S(1)} %copy-done.15), channel_id=1, source_target_pairs={{0,3},{1,2},{2,1},{3,0},{4,7},{5,6},{6,5},{7,4},{8,11},{9,10},{10,... | collective-permute-start | bytes 786440 | tf_op jit(solution)/shard_map/ppermute | solution.py:17
  79.7 3.3 %collective-permute-start.15 = (bf16[1,128,256]{2,1,0:T(8,128)(2,1)S(1)}, bf16[1,128,256]{2,1,0:T(8,128)(2,1)S(1)}, u32[]{:S(2)}, u32[]{:S(2)}) collective-permute-start(bf16[1,128,256]{2,1,0:T(8,128)(2,1)S(1)} %fusion.6), channel_id=1, source_target_pairs={{0,4},{1,5},{2,6},{3,7},{4,0},{5,1},{6,2},{7,3},{8,12},{9,13},{10,... | collective-permute-start | bytes 196616 | tf_op jit(solution)/shard_map/ppermute | solution.py:17
  83.1 3.4 %collective-permute-done.15 = bf16[1,128,256]{2,1,0:T(8,128)(2,1)S(1)} collective-permute-done((bf16[1,128,256]{2,1,0:T(8,128)(2,1)S(1)}, bf16[1,128,256]{2,1,0:T(8,128)(2,1)S(1)}, u32[]{:S(2)}, u32[]{:S(2)}) %collective-permute-start.15) | collective-permute-done | bytes 65568 | tf_op jit(solution)/shard_map/ppermute | solution.py:17
  88.0 2.9 %collective-permute-start.21 = (bf16[2,128,256]{2,1,0:T(8,128)(2,1)S(1)}, bf16[2,128,256]{2,1,0:T(8,128)(2,1)S(1)}, u32[]{:S(2)}, u32[]{:S(2)}) collective-permute-start(bf16[2,128,256]{2,1,0:T(8,128)(2,1)S(1)} %pad_maximum_fusion.5.rest_2_), channel_id=1, source_target_pairs={{0,3},{1,2},{2,1},{3,0},{4,7},{5,6},{6,5},{7,4},{8,11},{9,10},{10,... | collective-permute-start | bytes 393224 | tf_op jit(solution)/shard_map/ppermute | solution.py:17
  93.1 2.3 %collective-permute-done.21.rest_5_ = bf16[2,128,256]{2,1,0:T(8,128)(2,1)S(1)} collective-permute-done((bf16[2,128,256]{2,1,0:T(8,128)(2,1)S(1)}, bf16[2,128,256]{2,1,0:T(8,128)(2,1)S(1)}, u32[]{:S(2)}, u32[]{:S(2)}) %collective-permute-start.21) | collective-permute-done | bytes 131104 | tf_op jit(solution)/shard_map/ppermute | solution.py:17
  95.4 2.9 %collective-permute-start.23 = (f32[128,512]{1,0:T(8,128)}, f32[128,512]{1,0:T(8,128)S(1)}, u32[]{:S(2)}, u32[]{:S(2)}) collective-permute-start(f32[128,512]{1,0:T(8,128)} %get-tuple-element.80), channel_id=1, source_target_pairs={{0,2},{1,3},{2,0},{3,1},{4,6},{5,7},{6,4},{7,5},{8,10},{9,11},{10,... | collective-permute-start | bytes 786440 | tf_op jit(solution)/shard_map/ppermute | solution.py:17
  98.3 2.7 %collective-permute-start.24 = (f32[128,512]{1,0:T(8,128)}, f32[128,512]{1,0:T(8,128)S(1)}, u32[]{:S(2)}, u32[]{:S(2)}) collective-permute-start(f32[128,512]{1,0:T(8,128)} %get-tuple-element.81), channel_id=1, source_target_pairs={{0,3},{1,2},{2,1},{3,0},{4,7},{5,6},{6,5},{7,4},{8,11},{9,10},{10,... | collective-permute-start | bytes 786440 | tf_op jit(solution)/shard_map/ppermute | solution.py:17
  101.8 8.6 %attend.2 = (f32[2048,128]{1,0:T(8,128)}, f32[2048,128]{1,0:T(8,128)}) custom-call(s32[1,4]{1,0:T(1,128)} %len_ref.3, bf16[128,1024]{1,0:T(8,128)(2,1)} %d_ref.3, bf16[8,256,128]{2,1,0:T(8,128)(2,1)} %copy-done.6, bf16[8,256,128]{2,1,0:T(8,128)(2,1)} %copy-done.12, bf16[2,128,256]{2,1,0:T(8,128)(2,1)} %copy-done.8, bf16[2,128,256]{2,1,0:T(8,128)(2,1)} %copy-done.22, ...), custom_call_target="tpu_custom_call" | custom-call | flops 1610612736 | bytes 3145728 | tf_op jit(solution)/shard_map/attend/pallas_call | solution.py:298
  111.3 9.3 %attend.3 = (f32[2048,128]{1,0:T(8,128)}, f32[2048,128]{1,0:T(8,128)}) custom-call(s32[1,4]{1,0:T(1,128)} %len_ref.3, bf16[128,1024]{1,0:T(8,128)(2,1)} %d_ref.3, bf16[8,256,128]{2,1,0:T(8,128)(2,1)} %copy-done.6, bf16[8,256,128]{2,1,0:T(8,128)(2,1)} %copy-done.12, bf16[2,128,256]{2,1,0:T(8,128)(2,1)} %copy-done.8, bf16[2,128,256]{2,1,0:T(8,128)(2,1)} %copy-done.22, ...), custom_call_target="tpu_custom_call" | custom-call | flops 1610612736 | bytes 3145728 | tf_op jit(solution)/shard_map/attend/pallas_call | solution.py:298
  120.7 2.9 %collective-permute-done.25 = f32[2048,128]{1,0:T(8,128)S(1)} collective-permute-done((f32[2048,128]{1,0:T(8,128)}, f32[2048,128]{1,0:T(8,128)S(1)}, u32[]{:S(2)}, u32[]{:S(2)}) %collective-permute-start.25) | collective-permute-done | bytes 1048608 | tf_op jit(solution)/shard_map/ppermute | solution.py:17
  126.3 2.9 %collective-permute-start.32 = (bf16[256,128]{1,0:T(8,128)(2,1)S(1)}, bf16[256,128]{1,0:T(8,128)(2,1)S(1)}, u32[]{:S(2)}, u32[]{:S(2)}) collective-permute-start(bf16[256,128]{1,0:T(8,128)(2,1)S(1)} %get-tuple-element.93), channel_id=1, source_target_pairs={{0,7},{1,6},{2,5},{3,4},{4,3},{5,2},{6,1},{7,0},{8,15},{9,14},{10,... | collective-permute-start | bytes 196616 | tf_op jit(solution)/shard_map/ppermute | solution.py:17
  129.4 3.1 %collective-permute-start.30 = (bf16[256,128]{1,0:T(8,128)(2,1)S(1)}, bf16[256,128]{1,0:T(8,128)(2,1)S(1)}, u32[]{:S(2)}, u32[]{:S(2)}) collective-permute-start(bf16[256,128]{1,0:T(8,128)(2,1)S(1)} %get-tuple-element.95), channel_id=1, source_target_pairs={{0,5},{1,4},{2,7},{3,6},{4,1},{5,0},{6,3},{7,2},{8,13},{9,12},{10,... | collective-permute-start | bytes 196616 | tf_op jit(solution)/shard_map/ppermute | solution.py:17
  133.0 2.3 %collective-permute-start.28 = (bf16[256,128]{1,0:T(8,128)(2,1)S(1)}, bf16[256,128]{1,0:T(8,128)(2,1)S(1)}, u32[]{:S(2)}, u32[]{:S(2)}) collective-permute-start(bf16[256,128]{1,0:T(8,128)(2,1)S(1)} %get-tuple-element.97), channel_id=1, source_target_pairs={{0,6},{1,7},{2,4},{3,5},{4,2},{5,3},{6,0},{7,1},{8,14},{9,15},{10,... | collective-permute-start | bytes 196616 | tf_op jit(solution)/shard_map/ppermute | solution.py:17
  135.5 2.8 %collective-permute-done.30 = bf16[256,128]{1,0:T(8,128)(2,1)S(1)} collective-permute-done((bf16[256,128]{1,0:T(8,128)(2,1)S(1)}, bf16[256,128]{1,0:T(8,128)(2,1)S(1)}, u32[]{:S(2)}, u32[]{:S(2)}) %collective-permute-start.30) | collective-permute-done | bytes 65568 | tf_op jit(solution)/shard_map/ppermute | solution.py:17
  141.3 3.7 %collective-permute-done.33 = f32[256,128]{1,0:T(8,128)S(1)} collective-permute-done((f32[256,128]{1,0:T(8,128)S(1)}, f32[256,128]{1,0:T(8,128)S(1)}, u32[]{:S(2)}, u32[]{:S(2)}) %collective-permute-start.33) | collective-permute-done | bytes 131104 | tf_op jit(solution)/shard_map/ppermute | solution.py:17
  (112 shorter events, 30.0 us)
Async XLA Ops:
  3.8 33.2 %collective-permute-start.1 = (bf16[640,512]{1,0:T(8,128)(2,1)}, bf16[640,512]{1,0:T(8,128)(2,1)S(1)}, u32[]{:S(2)}, u32[]{:S(2)}) collective-permute-start(bf16[640,512]{1,0:T(8,128)(2,1)} %get-tuple-element.46), channel_id=1, source_target_pairs={{0,4},{1,5},{2,6},{3,7},{4,0},{5,1},{6,2},{7,3},{8,12},{9,13},{10,... | collective-permute-start | bytes 1966088 | tf_op jit(solution)/shard_map/ppermute | solution.py:17
  7.9 39.5 %collective-permute-start.3 = (bf16[128,2048]{1,0:T(8,128)(2,1)}, bf16[128,2048]{1,0:T(8,128)(2,1)S(1)}, u32[]{:S(2)}, u32[]{:S(2)}) collective-permute-start(bf16[128,2048]{1,0:T(8,128)(2,1)} %get-tuple-element.47), channel_id=1, source_target_pairs={{0,1},{1,0},{2,3},{3,2},{4,5},{5,4},{6,7},{7,6},{8,9},{9,8},{10,11... | collective-permute-start | bytes 1572872 | tf_op jit(solution)/shard_map/ppermute | solution.py:17
  9.4 38.0 %collective-permute-start.4 = (bf16[128,2048]{1,0:T(8,128)(2,1)}, bf16[128,2048]{1,0:T(8,128)(2,1)S(1)}, u32[]{:S(2)}, u32[]{:S(2)}) collective-permute-start(bf16[128,2048]{1,0:T(8,128)(2,1)} %get-tuple-element.48), channel_id=1, source_target_pairs={{0,2},{1,3},{2,0},{3,1},{4,6},{5,7},{6,4},{7,5},{8,10},{9,11},{10,... | collective-permute-start | bytes 1572872 | tf_op jit(solution)/shard_map/ppermute | solution.py:17
  11.0 37.2 %collective-permute-start.5 = (bf16[128,2048]{1,0:T(8,128)(2,1)}, bf16[128,2048]{1,0:T(8,128)(2,1)S(1)}, u32[]{:S(2)}, u32[]{:S(2)}) collective-permute-start(bf16[128,2048]{1,0:T(8,128)(2,1)} %get-tuple-element.49), channel_id=1, source_target_pairs={{0,3},{1,2},{2,1},{3,0},{4,7},{5,6},{6,5},{7,4},{8,11},{9,10},{10,... | collective-permute-start | bytes 1572872 | tf_op jit(solution)/shard_map/ppermute | solution.py:17
  37.0 10.3 %collective-permute-start.2 = (bf16[1,384,512]{2,1,0:T(8,128)(2,1)S(1)}, bf16[1,384,512]{2,1,0:T(8,128)(2,1)S(1)}, u32[]{:S(2)}, u32[]{:S(2)}) collective-permute-start(bf16[1,384,512]{2,1,0:T(8,128)(2,1)S(1)} %slice_bitcast_fusion), channel_id=1, source_target_pairs={{0,16},{8,24},{16,0},{24,8},{1,17},{9,25},{17,1},{25,9},{2,18},{10... | collective-permute-start | bytes 1179656 | tf_op jit(solution)/shard_map/ppermute | solution.py:17
  38.6 7.4 %collective-permute-start = (bf16[1,256,128]{2,1,0:T(8,128)(2,1)S(1)}, bf16[1,256,128]{2,1,0:T(8,128)(2,1)S(1)}, u32[]{:S(2)}, u32[]{:S(2)}) collective-permute-start(bf16[1,256,128]{2,1,0:T(8,128)(2,1)S(1)} %select_bitcast_fusion), channel_id=1, source_target_pairs={{0,4},{1,5},{2,6},{3,7},{4,0},{5,1},{6,2},{7,3},{8,12},{9,13},{10,... | collective-permute-start | bytes 196616 | tf_op jit(solution)/shard_map/ppermute | solution.py:17
  48.2 8.8 %collective-permute-start.6 = (bf16[1,256,512]{2,1,0:T(8,128)(2,1)S(1)}, bf16[1,256,512]{2,1,0:T(8,128)(2,1)S(1)}, u32[]{:S(2)}, u32[]{:S(2)}) collective-permute-start(bf16[1,256,512]{2,1,0:T(8,128)(2,1)S(1)} %slice_bitcast_fusion.1), channel_id=1, source_target_pairs={{0,16},{8,24},{16,0},{24,8},{1,17},{9,25},{17,1},{25,9},{2,18},{10... | collective-permute-start | bytes 786440 | tf_op jit(solution)/shard_map/ppermute | solution.py:17
  55.5 7.7 %collective-permute-start.9 = (bf16[4,256,128]{2,1,0:T(8,128)(2,1)S(1)}, bf16[4,256,128]{2,1,0:T(8,128)(2,1)S(1)}, u32[]{:S(2)}, u32[]{:S(2)}) collective-permute-start(bf16[4,256,128]{2,1,0:T(8,128)(2,1)S(1)} %pad_maximum_fusion.3), channel_id=1, source_target_pairs={{0,1},{1,0},{2,3},{3,2},{4,5},{5,4},{6,7},{7,6},{8,9},{9,8},{10,11... | collective-permute-start | bytes 786440 | tf_op jit(solution)/shard_map/ppermute | solution.py:17
  63.3 16.4 %collective-permute-start.11 = (f32[128,512]{1,0:T(8,128)}, f32[128,512]{1,0:T(8,128)S(1)}, u32[]{:S(2)}, u32[]{:S(2)}) collective-permute-start(f32[128,512]{1,0:T(8,128)} %get-tuple-element.60), channel_id=1, source_target_pairs={{0,1},{1,0},{2,3},{3,2},{4,5},{5,4},{6,7},{7,6},{8,9},{9,8},{10,11... | collective-permute-start | bytes 786440 | tf_op jit(solution)/shard_map/ppermute | solution.py:17
  64.9 13.0 %collective-permute-start.12 = (f32[128,256]{1,0:T(8,128)}, f32[128,256]{1,0:T(8,128)S(1)}, u32[]{:S(2)}, u32[]{:S(2)}) collective-permute-start(f32[128,256]{1,0:T(8,128)} %get-tuple-element.62), channel_id=1, source_target_pairs={{0,1},{1,0},{2,3},{3,2},{4,5},{5,4},{6,7},{7,6},{8,9},{9,8},{10,11... | collective-permute-start | bytes 393224 | tf_op jit(solution)/shard_map/ppermute | solution.py:17
  65.4 14.3 %collective-permute-start.13 = (f32[128,256]{1,0:T(8,128)}, f32[128,256]{1,0:T(8,128)S(1)}, u32[]{:S(2)}, u32[]{:S(2)}) collective-permute-start(f32[128,256]{1,0:T(8,128)} %get-tuple-element.63), channel_id=1, source_target_pairs={{0,2},{1,3},{2,0},{3,1},{4,6},{5,7},{6,4},{7,5},{8,10},{9,11},{10,... | collective-permute-start | bytes 393224 | tf_op jit(solution)/shard_map/ppermute | solution.py:17
  66.2 13.4 %collective-permute-start.14 = (f32[128,256]{1,0:T(8,128)}, f32[128,256]{1,0:T(8,128)S(1)}, u32[]{:S(2)}, u32[]{:S(2)}) collective-permute-start(f32[128,256]{1,0:T(8,128)} %get-tuple-element.64), channel_id=1, source_target_pairs={{0,3},{1,2},{2,1},{3,0},{4,7},{5,6},{6,5},{7,4},{8,11},{9,10},{10,... | collective-permute-start | bytes 393224 | tf_op jit(solution)/shard_map/ppermute | solution.py:17
  68.4 18.1 %collective-permute-start.16 = (f32[128,512]{1,0:T(8,128)}, f32[128,512]{1,0:T(8,128)S(1)}, u32[]{:S(2)}, u32[]{:S(2)}) collective-permute-start(f32[128,512]{1,0:T(8,128)} %get-tuple-element.74), channel_id=1, source_target_pairs={{0,2},{1,3},{2,0},{3,1},{4,6},{5,7},{6,4},{7,5},{8,10},{9,11},{10,... | collective-permute-start | bytes 786440 | tf_op jit(solution)/shard_map/ppermute | solution.py:17
  77.9 10.2 %collective-permute-start.17 = (f32[128,512]{1,0:T(8,128)S(1)}, f32[128,512]{1,0:T(8,128)S(1)}, u32[]{:S(2)}, u32[]{:S(2)}) collective-permute-start(f32[128,512]{1,0:T(8,128)S(1)} %copy-done.15), channel_id=1, source_target_pairs={{0,3},{1,2},{2,1},{3,0},{4,7},{5,6},{6,5},{7,4},{8,11},{9,10},{10,... | collective-permute-start | bytes 786440 | tf_op jit(solution)/shard_map/ppermute | solution.py:17
  88.0 12.9 %collective-permute-start.18 = (bf16[8,256,128]{2,1,0:T(8,128)(2,1)S(1)}, bf16[8,256,128]{2,1,0:T(8,128)(2,1)S(1)}, u32[]{:S(2)}, u32[]{:S(2)}) collective-permute-start(bf16[8,256,128]{2,1,0:T(8,128)(2,1)S(1)} %pad_maximum_fusion.2.rest_0_), channel_id=1, source_target_pairs={{0,8},{8,0},{16,24},{24,16},{1,9},{9,1},{17,25},{25,17},{2,10},{10... | collective-permute-start | bytes 1572872 | tf_op jit(solution)/shard_map/ppermute | solution.py:17
  88.0 7.3 %collective-permute-start.21 = (bf16[2,128,256]{2,1,0:T(8,128)(2,1)S(1)}, bf16[2,128,256]{2,1,0:T(8,128)(2,1)S(1)}, u32[]{:S(2)}, u32[]{:S(2)}) collective-permute-start(bf16[2,128,256]{2,1,0:T(8,128)(2,1)S(1)} %pad_maximum_fusion.5.rest_2_), channel_id=1, source_target_pairs={{0,3},{1,2},{2,1},{3,0},{4,7},{5,6},{6,5},{7,4},{8,11},{9,10},{10,... | collective-permute-start | bytes 393224 | tf_op jit(solution)/shard_map/ppermute | solution.py:17
  91.0 7.3 %collective-permute-start.20 = (bf16[2,128,256]{2,1,0:T(8,128)(2,1)S(1)}, bf16[2,128,256]{2,1,0:T(8,128)(2,1)S(1)}, u32[]{:S(2)}, u32[]{:S(2)}) collective-permute-start(bf16[2,128,256]{2,1,0:T(8,128)(2,1)S(1)} %pad_maximum_fusion.5.rest_2_), channel_id=1, source_target_pairs={{0,2},{1,3},{2,0},{3,1},{4,6},{5,7},{6,4},{7,5},{8,10},{9,11},{10,... | collective-permute-start | bytes 393224 | tf_op jit(solution)/shard_map/ppermute | solution.py:17
  91.1 9.9 %collective-permute-start.19 = (bf16[2,128,256]{2,1,0:T(8,128)(2,1)S(1)}, bf16[2,128,256]{2,1,0:T(8,128)(2,1)S(1)}, u32[]{:S(2)}, u32[]{:S(2)}) collective-permute-start(bf16[2,128,256]{2,1,0:T(8,128)(2,1)S(1)} %pad_maximum_fusion.5.rest_2_), channel_id=1, source_target_pairs={{0,1},{1,0},{2,3},{3,2},{4,5},{5,4},{6,7},{7,6},{8,9},{9,8},{10,11... | collective-permute-start | bytes 393224 | tf_op jit(solution)/shard_map/ppermute | solution.py:17
  92.5 17.9 %collective-permute-start.22 = (f32[128,512]{1,0:T(8,128)}, f32[128,512]{1,0:T(8,128)S(1)}, u32[]{:S(2)}, u32[]{:S(2)}) collective-permute-start(f32[128,512]{1,0:T(8,128)} %get-tuple-element.79), channel_id=1, source_target_pairs={{0,1},{1,0},{2,3},{3,2},{4,5},{5,4},{6,7},{7,6},{8,9},{9,8},{10,11... | collective-permute-start | bytes 786440 | tf_op jit(solution)/shard_map/ppermute | solution.py:17
  95.4 15.1 %collective-permute-start.23 = (f32[128,512]{1,0:T(8,128)}, f32[128,512]{1,0:T(8,128)S(1)}, u32[]{:S(2)}, u32[]{:S(2)}) collective-permute-start(f32[128,512]{1,0:T(8,128)} %get-tuple-element.80), channel_id=1, source_target_pairs={{0,2},{1,3},{2,0},{3,1},{4,6},{5,7},{6,4},{7,5},{8,10},{9,11},{10,... | collective-permute-start | bytes 786440 | tf_op jit(solution)/shard_map/ppermute | solution.py:17
  98.3 12.2 %collective-permute-start.24 = (f32[128,512]{1,0:T(8,128)}, f32[128,512]{1,0:T(8,128)S(1)}, u32[]{:S(2)}, u32[]{:S(2)}) collective-permute-start(f32[128,512]{1,0:T(8,128)} %get-tuple-element.81), channel_id=1, source_target_pairs={{0,3},{1,2},{2,1},{3,0},{4,7},{5,6},{6,5},{7,4},{8,11},{9,10},{10,... | collective-permute-start | bytes 786440 | tf_op jit(solution)/shard_map/ppermute | solution.py:17
  124.9 8.1 %collective-permute-start.26 = (bf16[256,128]{1,0:T(8,128)(2,1)S(1)}, bf16[256,128]{1,0:T(8,128)(2,1)S(1)}, u32[]{:S(2)}, u32[]{:S(2)}) collective-permute-start(bf16[256,128]{1,0:T(8,128)(2,1)S(1)} %get-tuple-element.92), channel_id=1, source_target_pairs={{0,4},{1,5},{2,6},{3,7},{4,0},{5,1},{6,2},{7,3},{8,12},{9,13},{10,... | collective-permute-start | bytes 196616 | tf_op jit(solution)/shard_map/ppermute | solution.py:17
  126.3 9.1 %collective-permute-start.32 = (bf16[256,128]{1,0:T(8,128)(2,1)S(1)}, bf16[256,128]{1,0:T(8,128)(2,1)S(1)}, u32[]{:S(2)}, u32[]{:S(2)}) collective-permute-start(bf16[256,128]{1,0:T(8,128)(2,1)S(1)} %get-tuple-element.93), channel_id=1, source_target_pairs={{0,7},{1,6},{2,5},{3,4},{4,3},{5,2},{6,1},{7,0},{8,15},{9,14},{10,... | collective-permute-start | bytes 196616 | tf_op jit(solution)/shard_map/ppermute | solution.py:17
  129.4 8.9 %collective-permute-start.30 = (bf16[256,128]{1,0:T(8,128)(2,1)S(1)}, bf16[256,128]{1,0:T(8,128)(2,1)S(1)}, u32[]{:S(2)}, u32[]{:S(2)}) collective-permute-start(bf16[256,128]{1,0:T(8,128)(2,1)S(1)} %get-tuple-element.95), channel_id=1, source_target_pairs={{0,5},{1,4},{2,7},{3,6},{4,1},{5,0},{6,3},{7,2},{8,13},{9,12},{10,... | collective-permute-start | bytes 196616 | tf_op jit(solution)/shard_map/ppermute | solution.py:17
  (34 other events, 301.4 us)

commit v4 on v3

--- a/solution.py
+++ b/solution.py
@@ -365,15 +365,15 @@
         far_b, _ = finish(far_b, order, "dp", n_dp, d_bits[1:])
         parts_kv = from_owners(out_kv)
         parts_a = from_owners(out_a)
+        own = functools.reduce(lambda a, b: a + b, parts_kv).astype(BF16)
+        far_b[1], own = together(far_b[1], own)
+        group, _ = double(own[None], [0], "fsdp", n_fsdp, inner)
         near_b, layout_b = [(w_query, at_b, wide_b)], [(0, 0, share, wide_b, 0, 0)]
         (out_b,) = multiply(
             hidden, received, near_b, far_b, layout_b, d_order, n_fsdp, (wide_b,)
         )
-        out_b[0], parts_a[1], *parts_kv = together(out_b[0], parts_a[1], *parts_kv)
-        own = functools.reduce(lambda a, b: a + b, parts_kv).astype(BF16)
-        group, _ = double(own[None], [0], "fsdp", n_fsdp, inner)
-        group, cache, *tied = together(group, cache, *out_b, *parts_a[2:])
-        out_b, parts_a[2:] = tied[:inner], tied[inner:]
+        group, cache, *tied = together(group, cache, *out_b, *parts_a[1:])
+        out_b, parts_a[1:] = tied[:inner], tied[inner:]
         group = [group] + [swap(group, "fsdp", n_fsdp, k) for k in range(1, inner)]
         g_order = [o for k in range(inner) for o in (k, k ^ inner)]
         cache = [cache, swap(cache, "dp", n_dp, 1)]

time: 147 us -> 146 us (level)
  waiting for transfers between devices: 63.4 us -> 61.9 us
    ppermute x35, waiting for transfers between devices: 63.4 us -> 61.9 us  [swap(): return lax.ppermute(value, axis, [(i, i ^ bit) for i in range(size)])]
  transfers between devices with their start and end apart: 35 -> 35, of which waited for: 16 -> 18; matrix products, arithmetic and copies ran while one was open for 0% -> 1% of each run, Pallas kernels for 13% -> 13%
where the time goes in v4:
time: 146 us; the launch traced here: 145 us
  waiting for transfers between devices  61.9 us (42%)
  starting transfers between devices  45.9 us (31%)
  Pallas kernels  31.4 us (22%)
  other arithmetic  3.34 us (2%)
  local copies, waits for them, and re-layouts  1.78 us (1%)
    ppermute x35, waiting for transfers between devices, swap(): return lax.ppermute(value, axis, [(i, i ^ bit) for i in range(size)])  61.9 us
    ppermute x35, starting transfers between devices, swap(): return lax.ppermute(value, axis, [(i, i ^ bit) for i in range(size)])  45.9 us
    pallas_call x2, Pallas kernels, attend(): pl.pallas_call(body, in_specs=[pl.BlockSpec(memory_space=pltpu.SMEM)] + [...  17.9 us
    pallas_call x2, Pallas kernels, multiply(): pl.pallas_call(body, in_specs=[pl.BlockSpec(memory_space=pl.ANY)] * (1 +...  10.4 us
    pallas_call x1, Pallas kernels, prepare(): pl.pallas_call(body, in_specs=[pl.BlockSpec(memory_space=pl.ANY)] * 4, ou...  3.12 us
  transfers between devices with their start and end apart: 35, of which 18 were waited for; matrix products, arithmetic and copies ran while one was open for 1% of the time, Pallas kernels for 13%

profile of v4, /device:TPU:0, one launch (start us, length us, event | category | flops | bytes accessed | tf_op | source)
XLA Modules:
  0.0 145.3 jit_solution(9548703000124979611)
XLA Ops:
  0.6 3.1 %prepare.1 = (bf16[128,2048]{1,0:T(8,128)(2,1)}, bf16[128,2048]{1,0:T(8,128)(2,1)}, bf16[128,2048]{1,0:T(8,128)(2,1)}, bf16[640,512]{1,0:T(8,128)(2,1)}) custom-call(bf16[128,8192]{1,0:T(8,128)(2,1)} %hidden_ref.5, bf16[1024,1024]{1,0:T(8,128)(2,1)} %rest_3_.3, bf16[1024,128]{1,0:T(8,128)(2,1)} %rest_3_.2, bf16[1024,128]{1,0:T(8,128)(2,1)} %rest_4_.1), custom_call_target="tpu_custom_call" | custom-call | bytes 4456448 | tf_op jit(solution)/shard_map/prepare/pallas_call | solution.py:83
  3.8 4.1 %collective-permute-start = (bf16[640,512]{1,0:T(8,128)(2,1)}, bf16[640,512]{1,0:T(8,128)(2,1)S(1)}, u32[]{:S(2)}, u32[]{:S(2)}) collective-permute-start(bf16[640,512]{1,0:T(8,128)(2,1)} %get-tuple-element.43), channel_id=1, source_target_pairs={{0,4},{1,5},{2,6},{3,7},{4,0},{5,1},{6,2},{7,3},{8,12},{9,13},{10,... | collective-permute-start | bytes 1966088 | tf_op jit(solution)/shard_map/ppermute | solution.py:17
  11.4 25.6 %collective-permute-done = bf16[640,512]{1,0:T(8,128)(2,1)S(1)} collective-permute-done((bf16[640,512]{1,0:T(8,128)(2,1)}, bf16[640,512]{1,0:T(8,128)(2,1)S(1)}, u32[]{:S(2)}, u32[]{:S(2)}) %collective-permute-start) | collective-permute-done | bytes 655392 | tf_op jit(solution)/shard_map/ppermute | solution.py:17
  37.0 1.6 %collective-permute-start.3 = (bf16[1,384,512]{2,1,0:T(8,128)(2,1)S(1)}, bf16[1,384,512]{2,1,0:T(8,128)(2,1)S(1)}, u32[]{:S(2)}, u32[]{:S(2)}) collective-permute-start(bf16[1,384,512]{2,1,0:T(8,128)(2,1)S(1)} %slice_bitcast_fusion), channel_id=1, source_target_pairs={{0,16},{8,24},{16,0},{24,8},{1,17},{9,25},{17,1},{25,9},{2,18},{10... | collective-permute-start | bytes 1179656 | tf_op jit(solution)/shard_map/ppermute | solution.py:17
  38.7 7.3 %collective-permute-done.2 = bf16[1,256,128]{2,1,0:T(8,128)(2,1)S(1)} collective-permute-done((bf16[1,256,128]{2,1,0:T(8,128)(2,1)S(1)}, bf16[1,256,128]{2,1,0:T(8,128)(2,1)S(1)}, u32[]{:S(2)}, u32[]{:S(2)}) %collective-permute-start.2) | collective-permute-done | bytes 65568 | tf_op jit(solution)/shard_map/ppermute | solution.py:17
  50.7 4.8 %collective-permute-done.7 = bf16[2,256,128]{2,1,0:T(8,128)(2,1)S(1)} collective-permute-done((bf16[2,256,128]{2,1,0:T(8,128)(2,1)S(1)}, bf16[2,256,128]{2,1,0:T(8,128)(2,1)S(1)}, u32[]{:S(2)}, u32[]{:S(2)}) %collective-permute-start.7) | collective-permute-done | bytes 131104 | tf_op jit(solution)/shard_map/ppermute | solution.py:17
  55.5 1.6 %collective-permute-start.9 = (bf16[4,256,128]{2,1,0:T(8,128)(2,1)S(1)}, bf16[4,256,128]{2,1,0:T(8,128)(2,1)S(1)}, u32[]{:S(2)}, u32[]{:S(2)}) collective-permute-start(bf16[4,256,128]{2,1,0:T(8,128)(2,1)S(1)} %pad_maximum_fusion.3), channel_id=1, source_target_pairs={{0,1},{1,0},{2,3},{3,2},{4,5},{5,4},{6,7},{7,6},{8,9},{9,8},{10,11... | collective-permute-start | bytes 786440 | tf_op jit(solution)/shard_map/ppermute | solution.py:17
  57.2 5.8 %multiply.2 = (f32[128,256]{1,0:T(8,128)}, f32[128,256]{1,0:T(8,128)}, f32[128,256]{1,0:T(8,128)}, f32[128,256]{1,0:T(8,128)}, f32[128,512]{1,0:T(8,128)}, /*ind...) custom-call(bf16[128,8192]{1,0:T(8,128)(2,1)} %hidden_ref.5, bf16[128,2048]{1,0:T(8,128)(2,1)} %copy-done.2, ...), custom_call_target="tpu_custom_call" | custom-call | flops 1610612736 | bytes 6815744 | tf_op jit(solution)/shard_map/multiply/pallas_call | solution.py:154
  63.3 1.6 %collective-permute-start.11 = (f32[128,256]{1,0:T(8,128)}, f32[128,256]{1,0:T(8,128)S(1)}, u32[]{:S(2)}, u32[]{:S(2)}) collective-permute-start(f32[128,256]{1,0:T(8,128)} %get-tuple-element.57), channel_id=1, source_target_pairs={{0,1},{1,0},{2,3},{3,2},{4,5},{5,4},{6,7},{7,6},{8,9},{9,8},{10,11... | collective-permute-start | bytes 393224 | tf_op jit(solution)/shard_map/ppermute | solution.py:17
  75.0 2.8 %collective-permute-start.14 = (bf16[1,128,256]{2,1,0:T(8,128)(2,1)S(1)}, bf16[1,128,256]{2,1,0:T(8,128)(2,1)S(1)}, u32[]{:S(2)}, u32[]{:S(2)}) collective-permute-start(bf16[1,128,256]{2,1,0:T(8,128)(2,1)S(1)} %bitcast.7), channel_id=1, source_target_pairs={{0,4},{1,5},{2,6},{3,7},{4,0},{5,1},{6,2},{7,3},{8,12},{9,13},{10,... | collective-permute-start | bytes 196616 | tf_op jit(solution)/shard_map/ppermute | solution.py:17
  77.8 4.6 %multiply.3 = (f32[128,512]{1,0:T(8,128)}, f32[128,512]{1,0:T(8,128)}, f32[128,512]{1,0:T(8,128)}, f32[128,512]{1,0:T(8,128)}) custom-call(bf16[128,8192]{1,0:T(8,128)(2,1)} %hidden_ref.5, bf16[128,2048]{1,0:T(8,128)(2,1)} %copy-done.2, bf16[128,2048]{1,0:T(8,128)(2,1)} %copy-done.3, bf16[128,2048]{1,0:T(8,128)(2,1)} %copy-done.4, ...), custom_call_target="tpu_custom_call" | custom-call | flops 1073741824 | bytes 5242880 | tf_op jit(solution)/shard_map/multiply/pallas_call | solution.py:154
  82.3 2.2 %collective-permute-done.14 = bf16[1,128,256]{2,1,0:T(8,128)(2,1)S(1)} collective-permute-done((bf16[1,128,256]{2,1,0:T(8,128)(2,1)S(1)}, bf16[1,128,256]{2,1,0:T(8,128)(2,1)S(1)}, u32[]{:S(2)}, u32[]{:S(2)}) %collective-permute-start.14) | collective-permute-done | bytes 65568 | tf_op jit(solution)/shard_map/ppermute | solution.py:17
  86.1 2.9 %collective-permute-start.21 = (bf16[2,128,256]{2,1,0:T(8,128)(2,1)S(1)}, bf16[2,128,256]{2,1,0:T(8,128)(2,1)S(1)}, u32[]{:S(2)}, u32[]{:S(2)}) collective-permute-start(bf16[2,128,256]{2,1,0:T(8,128)(2,1)S(1)} %pad_maximum_fusion.5.rest_2_), channel_id=1, source_target_pairs={{0,3},{1,2},{2,1},{3,0},{4,7},{5,6},{6,5},{7,4},{8,11},{9,10},{10,... | collective-permute-start | bytes 393224 | tf_op jit(solution)/shard_map/ppermute | solution.py:17
  91.2 2.2 %collective-permute-done.21.rest_5_ = bf16[2,128,256]{2,1,0:T(8,128)(2,1)S(1)} collective-permute-done((bf16[2,128,256]{2,1,0:T(8,128)(2,1)S(1)}, bf16[2,128,256]{2,1,0:T(8,128)(2,1)S(1)}, u32[]{:S(2)}, u32[]{:S(2)}) %collective-permute-start.21) | collective-permute-done | bytes 131104 | tf_op jit(solution)/shard_map/ppermute | solution.py:17
  93.5 2.9 %collective-permute-start.23 = (f32[128,512]{1,0:T(8,128)}, f32[128,512]{1,0:T(8,128)S(1)}, u32[]{:S(2)}, u32[]{:S(2)}) collective-permute-start(f32[128,512]{1,0:T(8,128)} %get-tuple-element.74), channel_id=1, source_target_pairs={{0,2},{1,3},{2,0},{3,1},{4,6},{5,7},{6,4},{7,5},{8,10},{9,11},{10,... | collective-permute-start | bytes 786440 | tf_op jit(solution)/shard_map/ppermute | solution.py:17
  96.4 2.7 %collective-permute-start.24 = (f32[128,512]{1,0:T(8,128)}, f32[128,512]{1,0:T(8,128)S(1)}, u32[]{:S(2)}, u32[]{:S(2)}) collective-permute-start(f32[128,512]{1,0:T(8,128)} %get-tuple-element.75), channel_id=1, source_target_pairs={{0,3},{1,2},{2,1},{3,0},{4,7},{5,6},{6,5},{7,4},{8,11},{9,10},{10,... | collective-permute-start | bytes 786440 | tf_op jit(solution)/shard_map/ppermute | solution.py:17
  99.9 8.6 %attend.2 = (f32[2048,128]{1,0:T(8,128)}, f32[2048,128]{1,0:T(8,128)}) custom-call(s32[1,4]{1,0:T(1,128)} %len_ref.3, bf16[128,1024]{1,0:T(8,128)(2,1)} %d_ref.3, bf16[8,256,128]{2,1,0:T(8,128)(2,1)} %copy-done.6, bf16[8,256,128]{2,1,0:T(8,128)(2,1)} %copy-done.11, bf16[2,128,256]{2,1,0:T(8,128)(2,1)} %copy-done.8, bf16[2,128,256]{2,1,0:T(8,128)(2,1)} %copy-done.20, ...), custom_call_target="tpu_custom_call" | custom-call | flops 1610612736 | bytes 3145728 | tf_op jit(solution)/shard_map/attend/pallas_call | solution.py:298
  109.5 9.3 %attend.3 = (f32[2048,128]{1,0:T(8,128)}, f32[2048,128]{1,0:T(8,128)}) custom-call(s32[1,4]{1,0:T(1,128)} %len_ref.3, bf16[128,1024]{1,0:T(8,128)(2,1)} %d_ref.3, bf16[8,256,128]{2,1,0:T(8,128)(2,1)} %copy-done.6, bf16[8,256,128]{2,1,0:T(8,128)(2,1)} %copy-done.11, bf16[2,128,256]{2,1,0:T(8,128)(2,1)} %copy-done.8, bf16[2,128,256]{2,1,0:T(8,128)(2,1)} %copy-done.20, ...), custom_call_target="tpu_custom_call" | custom-call | flops 1610612736 | bytes 3145728 | tf_op jit(solution)/shard_map/attend/pallas_call | solution.py:298
  118.8 2.9 %collective-permute-done.25 = f32[2048,128]{1,0:T(8,128)S(1)} collective-permute-done((f32[2048,128]{1,0:T(8,128)}, f32[2048,128]{1,0:T(8,128)S(1)}, u32[]{:S(2)}, u32[]{:S(2)}) %collective-permute-start.25) | collective-permute-done | bytes 1048608 | tf_op jit(solution)/shard_map/ppermute | solution.py:17
  124.4 2.9 %collective-permute-start.32 = (bf16[256,128]{1,0:T(8,128)(2,1)S(1)}, bf16[256,128]{1,0:T(8,128)(2,1)S(1)}, u32[]{:S(2)}, u32[]{:S(2)}) collective-permute-start(bf16[256,128]{1,0:T(8,128)(2,1)S(1)} %get-tuple-element.87), channel_id=1, source_target_pairs={{0,7},{1,6},{2,5},{3,4},{4,3},{5,2},{6,1},{7,0},{8,15},{9,14},{10,... | collective-permute-start | bytes 196616 | tf_op jit(solution)/shard_map/ppermute | solution.py:17
  127.6 3.1 %collective-permute-start.30 = (bf16[256,128]{1,0:T(8,128)(2,1)S(1)}, bf16[256,128]{1,0:T(8,128)(2,1)S(1)}, u32[]{:S(2)}, u32[]{:S(2)}) collective-permute-start(bf16[256,128]{1,0:T(8,128)(2,1)S(1)} %get-tuple-element.89), channel_id=1, source_target_pairs={{0,5},{1,4},{2,7},{3,6},{4,1},{5,0},{6,3},{7,2},{8,13},{9,12},{10,... | collective-permute-start | bytes 196616 | tf_op jit(solution)/shard_map/ppermute | solution.py:17
  131.2 2.3 %collective-permute-start.28 = (bf16[256,128]{1,0:T(8,128)(2,1)S(1)}, bf16[256,128]{1,0:T(8,128)(2,1)S(1)}, u32[]{:S(2)}, u32[]{:S(2)}) collective-permute-start(bf16[256,128]{1,0:T(8,128)(2,1)S(1)} %get-tuple-element.91), channel_id=1, source_target_pairs={{0,6},{1,7},{2,4},{3,5},{4,2},{5,3},{6,0},{7,1},{8,14},{9,15},{10,... | collective-permute-start | bytes 196616 | tf_op jit(solution)/shard_map/ppermute | solution.py:17
  133.7 2.8 %collective-permute-done.30 = bf16[256,128]{1,0:T(8,128)(2,1)S(1)} collective-permute-done((bf16[256,128]{1,0:T(8,128)(2,1)S(1)}, bf16[256,128]{1,0:T(8,128)(2,1)S(1)}, u32[]{:S(2)}, u32[]{:S(2)}) %collective-permute-start.30) | collective-permute-done | bytes 65568 | tf_op jit(solution)/shard_map/ppermute | solution.py:17
  139.5 3.6 %collective-permute-done.33 = f32[256,128]{1,0:T(8,128)S(1)} collective-permute-done((f32[256,128]{1,0:T(8,128)S(1)}, f32[256,128]{1,0:T(8,128)S(1)}, u32[]{:S(2)}, u32[]{:S(2)}) %collective-permute-start.33) | collective-permute-done | bytes 131104 | tf_op jit(solution)/shard_map/ppermute | solution.py:17
  (108 shorter events, 33.1 us)
Async XLA Ops:
  3.8 33.2 %collective-permute-start = (bf16[640,512]{1,0:T(8,128)(2,1)}, bf16[640,512]{1,0:T(8,128)(2,1)S(1)}, u32[]{:S(2)}, u32[]{:S(2)}) collective-permute-start(bf16[640,512]{1,0:T(8,128)(2,1)} %get-tuple-element.43), channel_id=1, source_target_pairs={{0,4},{1,5},{2,6},{3,7},{4,0},{5,1},{6,2},{7,3},{8,12},{9,13},{10,... | collective-permute-start | bytes 1966088 | tf_op jit(solution)/shard_map/ppermute | solution.py:17
  7.9 39.5 %collective-permute-start.4 = (bf16[128,2048]{1,0:T(8,128)(2,1)}, bf16[128,2048]{1,0:T(8,128)(2,1)S(1)}, u32[]{:S(2)}, u32[]{:S(2)}) collective-permute-start(bf16[128,2048]{1,0:T(8,128)(2,1)} %get-tuple-element.44), channel_id=1, source_target_pairs={{0,1},{1,0},{2,3},{3,2},{4,5},{5,4},{6,7},{7,6},{8,9},{9,8},{10,11... | collective-permute-start | bytes 1572872 | tf_op jit(solution)/shard_map/ppermute | solution.py:17
  9.4 38.0 %collective-permute-start.5 = (bf16[128,2048]{1,0:T(8,128)(2,1)}, bf16[128,2048]{1,0:T(8,128)(2,1)S(1)}, u32[]{:S(2)}, u32[]{:S(2)}) collective-permute-start(bf16[128,2048]{1,0:T(8,128)(2,1)} %get-tuple-element.45), channel_id=1, source_target_pairs={{0,2},{1,3},{2,0},{3,1},{4,6},{5,7},{6,4},{7,5},{8,10},{9,11},{10,... | collective-permute-start | bytes 1572872 | tf_op jit(solution)/shard_map/ppermute | solution.py:17
  11.0 37.2 %collective-permute-start.6 = (bf16[128,2048]{1,0:T(8,128)(2,1)}, bf16[128,2048]{1,0:T(8,128)(2,1)S(1)}, u32[]{:S(2)}, u32[]{:S(2)}) collective-permute-start(bf16[128,2048]{1,0:T(8,128)(2,1)} %get-tuple-element.46), channel_id=1, source_target_pairs={{0,3},{1,2},{2,1},{3,0},{4,7},{5,6},{6,5},{7,4},{8,11},{9,10},{10,... | collective-permute-start | bytes 1572872 | tf_op jit(solution)/shard_map/ppermute | solution.py:17
  37.0 10.3 %collective-permute-start.3 = (bf16[1,384,512]{2,1,0:T(8,128)(2,1)S(1)}, bf16[1,384,512]{2,1,0:T(8,128)(2,1)S(1)}, u32[]{:S(2)}, u32[]{:S(2)}) collective-permute-start(bf16[1,384,512]{2,1,0:T(8,128)(2,1)S(1)} %slice_bitcast_fusion), channel_id=1, source_target_pairs={{0,16},{8,24},{16,0},{24,8},{1,17},{9,25},{17,1},{25,9},{2,18},{10... | collective-permute-start | bytes 1179656 | tf_op jit(solution)/shard_map/ppermute | solution.py:17
  38.6 7.4 %collective-permute-start.2 = (bf16[1,256,128]{2,1,0:T(8,128)(2,1)S(1)}, bf16[1,256,128]{2,1,0:T(8,128)(2,1)S(1)}, u32[]{:S(2)}, u32[]{:S(2)}) collective-permute-start(bf16[1,256,128]{2,1,0:T(8,128)(2,1)S(1)} %select_bitcast_fusion), channel_id=1, source_target_pairs={{0,4},{1,5},{2,6},{3,7},{4,0},{5,1},{6,2},{7,3},{8,12},{9,13},{10,... | collective-permute-start | bytes 196616 | tf_op jit(solution)/shard_map/ppermute | solution.py:17
  48.2 8.8 %collective-permute-start.1 = (bf16[1,256,512]{2,1,0:T(8,128)(2,1)S(1)}, bf16[1,256,512]{2,1,0:T(8,128)(2,1)S(1)}, u32[]{:S(2)}, u32[]{:S(2)}) collective-permute-start(bf16[1,256,512]{2,1,0:T(8,128)(2,1)S(1)} %slice_bitcast_fusion.1), channel_id=1, source_target_pairs={{0,16},{8,24},{16,0},{24,8},{1,17},{9,25},{17,1},{25,9},{2,18},{10... | collective-permute-start | bytes 786440 | tf_op jit(solution)/shard_map/ppermute | solution.py:17
  55.5 7.7 %collective-permute-start.9 = (bf16[4,256,128]{2,1,0:T(8,128)(2,1)S(1)}, bf16[4,256,128]{2,1,0:T(8,128)(2,1)S(1)}, u32[]{:S(2)}, u32[]{:S(2)}) collective-permute-start(bf16[4,256,128]{2,1,0:T(8,128)(2,1)S(1)} %pad_maximum_fusion.3), channel_id=1, source_target_pairs={{0,1},{1,0},{2,3},{3,2},{4,5},{5,4},{6,7},{7,6},{8,9},{9,8},{10,11... | collective-permute-start | bytes 786440 | tf_op jit(solution)/shard_map/ppermute | solution.py:17
  63.2 11.7 %collective-permute-start.10 = (bf16[2,256,512]{2,1,0:T(8,128)(2,1)S(1)}, bf16[2,256,512]{2,1,0:T(8,128)(2,1)S(1)}, u32[]{:S(2)}, u32[]{:S(2)}) collective-permute-start(bf16[2,256,512]{2,1,0:T(8,128)(2,1)S(1)} %pad_maximum_fusion.1.rest_4_), channel_id=1, source_target_pairs={{0,8},{8,0},{16,24},{24,16},{1,9},{9,1},{17,25},{25,17},{2,10},{10... | collective-permute-start | bytes 1572872 | tf_op jit(solution)/shard_map/ppermute | solution.py:17
  65.7 8.3 %collective-permute-start.13 = (f32[128,256]{1,0:T(8,128)}, f32[128,256]{1,0:T(8,128)S(1)}, u32[]{:S(2)}, u32[]{:S(2)}) collective-permute-start(f32[128,256]{1,0:T(8,128)} %get-tuple-element.59), channel_id=1, source_target_pairs={{0,3},{1,2},{2,1},{3,0},{4,7},{5,6},{6,5},{7,4},{8,11},{9,10},{10,... | collective-permute-start | bytes 393224 | tf_op jit(solution)/shard_map/ppermute | solution.py:17
  66.9 17.7 %collective-permute-start.15 = (f32[128,512]{1,0:T(8,128)}, f32[128,512]{1,0:T(8,128)S(1)}, u32[]{:S(2)}, u32[]{:S(2)}) collective-permute-start(f32[128,512]{1,0:T(8,128)} %get-tuple-element.67), channel_id=1, source_target_pairs={{0,1},{1,0},{2,3},{3,2},{4,5},{5,4},{6,7},{7,6},{8,9},{9,8},{10,11... | collective-permute-start | bytes 786440 | tf_op jit(solution)/shard_map/ppermute | solution.py:17
  69.5 15.1 %collective-permute-start.16 = (f32[128,512]{1,0:T(8,128)}, f32[128,512]{1,0:T(8,128)S(1)}, u32[]{:S(2)}, u32[]{:S(2)}) collective-permute-start(f32[128,512]{1,0:T(8,128)} %get-tuple-element.68), channel_id=1, source_target_pairs={{0,2},{1,3},{2,0},{3,1},{4,6},{5,7},{6,4},{7,5},{8,10},{9,11},{10,... | collective-permute-start | bytes 786440 | tf_op jit(solution)/shard_map/ppermute | solution.py:17
  71.5 14.7 %collective-permute-start.17 = (f32[128,512]{1,0:T(8,128)}, f32[128,512]{1,0:T(8,128)S(1)}, u32[]{:S(2)}, u32[]{:S(2)}) collective-permute-start(f32[128,512]{1,0:T(8,128)} %get-tuple-element.69), channel_id=1, source_target_pairs={{0,3},{1,2},{2,1},{3,0},{4,7},{5,6},{6,5},{7,4},{8,11},{9,10},{10,... | collective-permute-start | bytes 786440 | tf_op jit(solution)/shard_map/ppermute | solution.py:17
  75.0 9.5 %collective-permute-start.14 = (bf16[1,128,256]{2,1,0:T(8,128)(2,1)S(1)}, bf16[1,128,256]{2,1,0:T(8,128)(2,1)S(1)}, u32[]{:S(2)}, u32[]{:S(2)}) collective-permute-start(bf16[1,128,256]{2,1,0:T(8,128)(2,1)S(1)} %bitcast.7), channel_id=1, source_target_pairs={{0,4},{1,5},{2,6},{3,7},{4,0},{5,1},{6,2},{7,3},{8,12},{9,13},{10,... | collective-permute-start | bytes 196616 | tf_op jit(solution)/shard_map/ppermute | solution.py:17
  86.1 13.0 %collective-permute-start.18 = (bf16[8,256,128]{2,1,0:T(8,128)(2,1)S(1)}, bf16[8,256,128]{2,1,0:T(8,128)(2,1)S(1)}, u32[]{:S(2)}, u32[]{:S(2)}) collective-permute-start(bf16[8,256,128]{2,1,0:T(8,128)(2,1)S(1)} %pad_maximum_fusion.2.rest_0_), channel_id=1, source_target_pairs={{0,8},{8,0},{16,24},{24,16},{1,9},{9,1},{17,25},{25,17},{2,10},{10... | collective-permute-start | bytes 1572872 | tf_op jit(solution)/shard_map/ppermute | solution.py:17
  86.1 7.3 %collective-permute-start.21 = (bf16[2,128,256]{2,1,0:T(8,128)(2,1)S(1)}, bf16[2,128,256]{2,1,0:T(8,128)(2,1)S(1)}, u32[]{:S(2)}, u32[]{:S(2)}) collective-permute-start(bf16[2,128,256]{2,1,0:T(8,128)(2,1)S(1)} %pad_maximum_fusion.5.rest_2_), channel_id=1, source_target_pairs={{0,3},{1,2},{2,1},{3,0},{4,7},{5,6},{6,5},{7,4},{8,11},{9,10},{10,... | collective-permute-start | bytes 393224 | tf_op jit(solution)/shard_map/ppermute | solution.py:17
  89.1 7.3 %collective-permute-start.20 = (bf16[2,128,256]{2,1,0:T(8,128)(2,1)S(1)}, bf16[2,128,256]{2,1,0:T(8,128)(2,1)S(1)}, u32[]{:S(2)}, u32[]{:S(2)}) collective-permute-start(bf16[2,128,256]{2,1,0:T(8,128)(2,1)S(1)} %pad_maximum_fusion.5.rest_2_), channel_id=1, source_target_pairs={{0,2},{1,3},{2,0},{3,1},{4,6},{5,7},{6,4},{7,5},{8,10},{9,11},{10,... | collective-permute-start | bytes 393224 | tf_op jit(solution)/shard_map/ppermute | solution.py:17
  89.2 9.9 %collective-permute-start.19 = (bf16[2,128,256]{2,1,0:T(8,128)(2,1)S(1)}, bf16[2,128,256]{2,1,0:T(8,128)(2,1)S(1)}, u32[]{:S(2)}, u32[]{:S(2)}) collective-permute-start(bf16[2,128,256]{2,1,0:T(8,128)(2,1)S(1)} %pad_maximum_fusion.5.rest_2_), channel_id=1, source_target_pairs={{0,1},{1,0},{2,3},{3,2},{4,5},{5,4},{6,7},{7,6},{8,9},{9,8},{10,11... | collective-permute-start | bytes 393224 | tf_op jit(solution)/shard_map/ppermute | solution.py:17
  90.6 18.0 %collective-permute-start.22 = (f32[128,512]{1,0:T(8,128)}, f32[128,512]{1,0:T(8,128)S(1)}, u32[]{:S(2)}, u32[]{:S(2)}) collective-permute-start(f32[128,512]{1,0:T(8,128)} %get-tuple-element.73), channel_id=1, source_target_pairs={{0,1},{1,0},{2,3},{3,2},{4,5},{5,4},{6,7},{7,6},{8,9},{9,8},{10,11... | collective-permute-start | bytes 786440 | tf_op jit(solution)/shard_map/ppermute | solution.py:17
  93.5 15.1 %collective-permute-start.23 = (f32[128,512]{1,0:T(8,128)}, f32[128,512]{1,0:T(8,128)S(1)}, u32[]{:S(2)}, u32[]{:S(2)}) collective-permute-start(f32[128,512]{1,0:T(8,128)} %get-tuple-element.74), channel_id=1, source_target_pairs={{0,2},{1,3},{2,0},{3,1},{4,6},{5,7},{6,4},{7,5},{8,10},{9,11},{10,... | collective-permute-start | bytes 786440 | tf_op jit(solution)/shard_map/ppermute | solution.py:17
  96.4 12.2 %collective-permute-start.24 = (f32[128,512]{1,0:T(8,128)}, f32[128,512]{1,0:T(8,128)S(1)}, u32[]{:S(2)}, u32[]{:S(2)}) collective-permute-start(f32[128,512]{1,0:T(8,128)} %get-tuple-element.75), channel_id=1, source_target_pairs={{0,3},{1,2},{2,1},{3,0},{4,7},{5,6},{6,5},{7,4},{8,11},{9,10},{10,... | collective-permute-start | bytes 786440 | tf_op jit(solution)/shard_map/ppermute | solution.py:17
  123.1 8.1 %collective-permute-start.26 = (bf16[256,128]{1,0:T(8,128)(2,1)S(1)}, bf16[256,128]{1,0:T(8,128)(2,1)S(1)}, u32[]{:S(2)}, u32[]{:S(2)}) collective-permute-start(bf16[256,128]{1,0:T(8,128)(2,1)S(1)} %get-tuple-element.86), channel_id=1, source_target_pairs={{0,4},{1,5},{2,6},{3,7},{4,0},{5,1},{6,2},{7,3},{8,12},{9,13},{10,... | collective-permute-start | bytes 196616 | tf_op jit(solution)/shard_map/ppermute | solution.py:17
  124.4 9.1 %collective-permute-start.32 = (bf16[256,128]{1,0:T(8,128)(2,1)S(1)}, bf16[256,128]{1,0:T(8,128)(2,1)S(1)}, u32[]{:S(2)}, u32[]{:S(2)}) collective-permute-start(bf16[256,128]{1,0:T(8,128)(2,1)S(1)} %get-tuple-element.87), channel_id=1, source_target_pairs={{0,7},{1,6},{2,5},{3,4},{4,3},{5,2},{6,1},{7,0},{8,15},{9,14},{10,... | collective-permute-start | bytes 196616 | tf_op jit(solution)/shard_map/ppermute | solution.py:17
  127.6 8.9 %collective-permute-start.30 = (bf16[256,128]{1,0:T(8,128)(2,1)S(1)}, bf16[256,128]{1,0:T(8,128)(2,1)S(1)}, u32[]{:S(2)}, u32[]{:S(2)}) collective-permute-start(bf16[256,128]{1,0:T(8,128)(2,1)S(1)} %get-tuple-element.89), channel_id=1, source_target_pairs={{0,5},{1,4},{2,7},{3,6},{4,1},{5,0},{6,3},{7,2},{8,13},{9,12},{10,... | collective-permute-start | bytes 196616 | tf_op jit(solution)/shard_map/ppermute | solution.py:17
  (32 other events, 274.8 us)

commit v5 on v4

--- a/solution.py
+++ b/solution.py
@@ -170,19 +170,19 @@
     return [list(out[g * inner : (g + 1) * inner]) for g in range(len(groups))]
 
 
-def attend(lengths, terms, d_attn, first_head, cache, group, g_order, sums):
+def attend(lengths, partials, d_attn, cache, group, g_order):
     tokens = d_attn.shape[0]
     n_blocks, block, head_dim = cache[0].shape
     n_convs = lengths.shape[1]
     scale = head_dim ** (-0.5)
     to_log2 = scale * math.log2(math.e)
-    n_heads = terms[0].shape[1] // head_dim
+    n_heads = d_attn.shape[1] // head_dim
     lanes = n_heads * tokens
     n_cache = n_blocks * block
     n_group = n_blocks * tokens
     slots = n_blocks // len(group)
     chunk = min(512, n_cache)
-    n_part, n_sum = len(terms), len(sums)
+    n_part = sum(len(terms) for terms in partials)
     dims = (((1,), (1,)), ((), ()))
     spans = [(at, chunk) for at in range(0, n_cache, chunk)]
     spans += [(n_cache + i * slots * tokens, slots * tokens) for i in range(len(group))]
@@ -194,8 +194,7 @@
     def body(len_ref, d_ref, *rest):
         cache_refs, rest = rest[:2], rest[2:]
         group_refs, rest = rest[: len(group)], rest[len(group) :]
-        part_refs, rest = rest[:n_part], rest[n_part:]
-        sum_refs, rest = rest[:n_sum], rest[n_sum:]
+        part_refs, rest = list(rest[:n_part]), rest[n_part:]
         keep_ref, give_ref, out_ref, s_ref, p_ref, q_ref, dq_ref, ck_ref, cv_ref, sems = rest
         me, dp = lax.axis_index("fsdp"), lax.axis_index("dp")
         odd = dp % 2
@@ -210,15 +209,17 @@
             pltpu.make_async_copy(cache_refs[1], ck_ref, sems.at[0]).start()
             pltpu.make_async_copy(cache_refs[0], cv_ref, sems.at[1]).start()
 
-        for h in range(n_heads):
-            at = slice(h * head_dim, (h + 1) * head_dim)
-            rows = pl.ds(h * tokens, tokens)
-            q = part_refs[0][:, at]
-            for ref in part_refs[1:]:
-                q = q + ref[:, at]
-            q_ref[rows] = q.astype(BF16)
-            at = (first_head + h) * head_dim
-            dq_ref[rows] = d_ref[:, at : at + head_dim]
+        h = 0
+        for terms in partials:
+            refs, part_refs = part_refs[: len(terms)], part_refs[len(terms) :]
+            for at in range(0, terms[0].shape[1], head_dim):
+                rows = pl.ds(h * tokens, tokens)
+                q = refs[0][:, at : at + head_dim]
+                for ref in refs[1:]:
+                    q = q + ref[:, at : at + head_dim]
+                q_ref[rows] = q.astype(BF16)
+                dq_ref[rows] = d_ref[:, h * head_dim : (h + 1) * head_dim]
+                h += 1
 
         q_pos = me * tokens + lax.broadcasted_iota(jnp.int32, (1, lanes), 1) % tokens
         begin = jnp.zeros((1, lanes), jnp.int32)
@@ -292,7 +293,7 @@
             out_ref[odd, pl.ds(at, size)] = g
 
         for i, ref in enumerate((keep_ref, give_ref)):
-            ref[...] = sum_refs[i][...] + out_ref[i] if n_sum else out_ref[i]
+            ref[...] = out_ref[i]
 
     flops = 2 * lanes * head_dim * (5 * n_cache + 2 * n_group)
     return pl.pallas_call(
@@ -300,7 +301,7 @@
         in_specs=[pl.BlockSpec(memory_space=pltpu.SMEM)]
         + [pl.BlockSpec(memory_space=pltpu.VMEM)]
         + [pl.BlockSpec(memory_space=pl.ANY)] * 2
-        + [pl.BlockSpec(memory_space=pltpu.VMEM)] * (len(group) + n_part + n_sum),
+        + [pl.BlockSpec(memory_space=pltpu.VMEM)] * (len(group) + n_part),
         out_specs=[pl.BlockSpec(memory_space=pltpu.VMEM)] * 2,
         out_shape=[jax.ShapeDtypeStruct((n_cache, head_dim), F32)] * 2,
         scratch_shapes=[
@@ -320,7 +321,7 @@
             transcendentals=lanes * (n_cache + n_group),
         ),
         name="attend",
-    )(lengths, d_attn, *cache, *group, *terms, *sums)
+    )(lengths, d_attn, *cache, *group, *[term for terms in partials for term in terms])
 
 
 def make_on_device(n_dp, n_fsdp):
@@ -366,21 +367,20 @@
         parts_kv = from_owners(out_kv)
         parts_a = from_owners(out_a)
         own = functools.reduce(lambda a, b: a + b, parts_kv).astype(BF16)
-        far_b[1], own = together(far_b[1], own)
+        far_b[1], own, cache = together(far_b[1], own, cache)
+        cache = [cache, swap(cache, "dp", n_dp, 1)]
         group, _ = double(own[None], [0], "fsdp", n_fsdp, inner)
         near_b, layout_b = [(w_query, at_b, wide_b)], [(0, 0, share, wide_b, 0, 0)]
         (out_b,) = multiply(
             hidden, received, near_b, far_b, layout_b, d_order, n_fsdp, (wide_b,)
         )
-        group, cache, *tied = together(group, cache, *out_b, *parts_a[1:])
+        group, cache[1], *tied = together(group, cache[1], *out_b, *parts_a[1:])
         out_b, parts_a[1:] = tied[:inner], tied[inner:]
+        parts_b = from_owners(out_b)
+        group, parts_b[1] = together(group, parts_b[1])
         group = [group] + [swap(group, "fsdp", n_fsdp, k) for k in range(1, inner)]
         g_order = [o for k in range(inner) for o in (k, k ^ inner)]
-        cache = [cache, swap(cache, "dp", n_dp, 1)]
-        parts_b = from_owners(out_b)
-        first = cuts[0][1] // head_dim
-        sums = attend(lengths, parts_a, d_attn, 0, cache, group, g_order, ())
-        keep, give = attend(lengths, parts_b, d_attn, first, cache, group, g_order, sums)
+        keep, give = attend(lengths, [parts_a, parts_b], d_attn, cache, group, g_order)
 
         half = keep + swap(give, "dp", n_dp, 1)
         size = half.shape[0] // n_fsdp

time: 146 us -> 153 us (1.048)
  waiting for transfers between devices: 61.9 us -> 76.6 us
  Pallas kernels: 31.4 us -> 26.2 us
    ppermute x35, waiting for transfers between devices: 61.9 us -> 76.6 us  [swap(): return lax.ppermute(value, axis, [(i, i ^ bit) for i in range(size)])]
    pallas_call x2 -> x1, Pallas kernels: 17.9 us -> 12.7 us  [attend(): pl.pallas_call(body, in_specs=[pl.BlockSpec(memory_space=pltpu.SMEM)] + [...]
  transfers between devices with their start and end apart: 35 -> 35, of which waited for: 18 -> 22; matrix products, arithmetic and copies ran while one was open for 1% -> 1% of each run, Pallas kernels for 13% -> 7%
where the time goes in v5:
time: 153 us
  waiting for transfers between devices  76.6 us (50%)
  starting transfers between devices  45.1 us (29%)
  Pallas kernels  26.2 us (17%)
  other arithmetic  3.34 us (2%)
    ppermute x35, waiting for transfers between devices, swap(): return lax.ppermute(value, axis, [(i, i ^ bit) for i in range(size)])  76.6 us
    ppermute x35, starting transfers between devices, swap(): return lax.ppermute(value, axis, [(i, i ^ bit) for i in range(size)])  45.1 us
    pallas_call x1, Pallas kernels, attend(): pl.pallas_call(body, in_specs=[pl.BlockSpec(memory_space=pltpu.SMEM)] + [...  12.7 us
    pallas_call x2, Pallas kernels, multiply(): pl.pallas_call(body, in_specs=[pl.BlockSpec(memory_space=pl.ANY)] * (1 +...  10.4 us
    pallas_call x1, Pallas kernels, prepare(): pl.pallas_call(body, in_specs=[pl.BlockSpec(memory_space=pl.ANY)] * 4, ou...  3.08 us
  transfers between devices with their start and end apart: 35, of which 22 were waited for; matrix products, arithmetic and copies ran while one was open for 1% of the time, Pallas kernels for 7%

profile of v5, /device:TPU:0, one launch (start us, length us, event | category | flops | bytes accessed | tf_op | source)
XLA Modules:
  0.0 153.0 jit_solution(16825467940589516736)
XLA Ops:
  0.6 3.1 %prepare.1 = (bf16[128,2048]{1,0:T(8,128)(2,1)}, bf16[128,2048]{1,0:T(8,128)(2,1)}, bf16[128,2048]{1,0:T(8,128)(2,1)}, bf16[640,512]{1,0:T(8,128)(2,1)}) custom-call(bf16[128,8192]{1,0:T(8,128)(2,1)} %hidden_ref.5, bf16[1024,1024]{1,0:T(8,128)(2,1)} %rest_3_.3, bf16[1024,128]{1,0:T(8,128)(2,1)} %rest_3_.2, bf16[1024,128]{1,0:T(8,128)(2,1)} %rest_4_.1), custom_call_target="tpu_custom_call" | custom-call | bytes 4456448 | tf_op jit(solution)/shard_map/prepare/pallas_call | solution.py:83
  3.7 4.1 %collective-permute-start = (bf16[640,512]{1,0:T(8,128)(2,1)}, bf16[640,512]{1,0:T(8,128)(2,1)S(1)}, u32[]{:S(2)}, u32[]{:S(2)}) collective-permute-start(bf16[640,512]{1,0:T(8,128)(2,1)} %get-tuple-element.44), channel_id=1, source_target_pairs={{0,4},{1,5},{2,6},{3,7},{4,0},{5,1},{6,2},{7,3},{8,12},{9,13},{10,... | collective-permute-start | bytes 1966088 | tf_op jit(solution)/shard_map/ppermute | solution.py:17
  11.3 25.6 %collective-permute-done = bf16[640,512]{1,0:T(8,128)(2,1)S(1)} collective-permute-done((bf16[640,512]{1,0:T(8,128)(2,1)}, bf16[640,512]{1,0:T(8,128)(2,1)S(1)}, u32[]{:S(2)}, u32[]{:S(2)}) %collective-permute-start) | collective-permute-done | bytes 655392 | tf_op jit(solution)/shard_map/ppermute | solution.py:17
  38.7 7.3 %collective-permute-done.2 = bf16[1,256,128]{2,1,0:T(8,128)(2,1)S(1)} collective-permute-done((bf16[1,256,128]{2,1,0:T(8,128)(2,1)S(1)}, bf16[1,256,128]{2,1,0:T(8,128)(2,1)S(1)}, u32[]{:S(2)}, u32[]{:S(2)}) %collective-permute-start.2) | collective-permute-done | bytes 65568 | tf_op jit(solution)/shard_map/ppermute | solution.py:17
  50.6 4.8 %collective-permute-done.7 = bf16[2,256,128]{2,1,0:T(8,128)(2,1)S(1)} collective-permute-done((bf16[2,256,128]{2,1,0:T(8,128)(2,1)S(1)}, bf16[2,256,128]{2,1,0:T(8,128)(2,1)S(1)}, u32[]{:S(2)}, u32[]{:S(2)}) %collective-permute-start.7) | collective-permute-done | bytes 131104 | tf_op jit(solution)/shard_map/ppermute | solution.py:17
  57.2 5.9 %multiply.2 = (f32[128,256]{1,0:T(8,128)}, f32[128,256]{1,0:T(8,128)}, f32[128,256]{1,0:T(8,128)}, f32[128,256]{1,0:T(8,128)}, f32[128,512]{1,0:T(8,128)}, /*ind...) custom-call(bf16[128,8192]{1,0:T(8,128)(2,1)} %hidden_ref.5, bf16[128,2048]{1,0:T(8,128)(2,1)} %copy-done.2, ...), custom_call_target="tpu_custom_call" | custom-call | flops 1610612736 | bytes 6815744 | tf_op jit(solution)/shard_map/multiply/pallas_call | solution.py:154
  66.8 2.6 %collective-permute-done.11 = f32[128,256]{1,0:T(8,128)S(1)} collective-permute-done((f32[128,256]{1,0:T(8,128)}, f32[128,256]{1,0:T(8,128)S(1)}, u32[]{:S(2)}, u32[]{:S(2)}) %collective-permute-start.11) | collective-permute-done | bytes 131104 | tf_op jit(solution)/shard_map/ppermute | solution.py:17
  69.4 2.0 %collective-permute-done.12 = f32[128,256]{1,0:T(8,128)S(1)} collective-permute-done((f32[128,256]{1,0:T(8,128)}, f32[128,256]{1,0:T(8,128)S(1)}, u32[]{:S(2)}, u32[]{:S(2)}) %collective-permute-start.12) | collective-permute-done | bytes 131104 | tf_op jit(solution)/shard_map/ppermute | solution.py:17
  71.4 2.0 %collective-permute-done.13 = f32[128,256]{1,0:T(8,128)S(1)} collective-permute-done((f32[128,256]{1,0:T(8,128)}, f32[128,256]{1,0:T(8,128)S(1)}, u32[]{:S(2)}, u32[]{:S(2)}) %collective-permute-start.13) | collective-permute-done | bytes 131104 | tf_op jit(solution)/shard_map/ppermute | solution.py:17
  78.0 2.7 %collective-permute-start.14 = (bf16[1,128,256]{2,1,0:T(8,128)(2,1)S(1)}, bf16[1,128,256]{2,1,0:T(8,128)(2,1)S(1)}, u32[]{:S(2)}, u32[]{:S(2)}) collective-permute-start(bf16[1,128,256]{2,1,0:T(8,128)(2,1)S(1)} %bitcast.7), channel_id=1, source_target_pairs={{0,4},{1,5},{2,6},{3,7},{4,0},{5,1},{6,2},{7,3},{8,12},{9,13},{10,... | collective-permute-start | bytes 196616 | tf_op jit(solution)/shard_map/ppermute | solution.py:17
  80.7 4.6 %multiply.3 = (f32[128,512]{1,0:T(8,128)}, f32[128,512]{1,0:T(8,128)}, f32[128,512]{1,0:T(8,128)}, f32[128,512]{1,0:T(8,128)}) custom-call(bf16[128,8192]{1,0:T(8,128)(2,1)} %hidden_ref.5, bf16[128,2048]{1,0:T(8,128)(2,1)} %copy-done.2, bf16[128,2048]{1,0:T(8,128)(2,1)} %copy-done.3, bf16[128,2048]{1,0:T(8,128)(2,1)} %copy-done.4, ...), custom_call_target="tpu_custom_call" | custom-call | flops 1073741824 | bytes 5242880 | tf_op jit(solution)/shard_map/multiply/pallas_call | solution.py:154
  85.3 4.7 %collective-permute-done.14 = bf16[1,128,256]{2,1,0:T(8,128)(2,1)S(1)} collective-permute-done((bf16[1,128,256]{2,1,0:T(8,128)(2,1)S(1)}, bf16[1,128,256]{2,1,0:T(8,128)(2,1)S(1)}, u32[]{:S(2)}, u32[]{:S(2)}) %collective-permute-start.14) | collective-permute-done | bytes 65568 | tf_op jit(solution)/shard_map/ppermute | solution.py:17
  96.0 3.4 %collective-permute-done.19.rest_11_ = f32[128,512]{1,0:T(8,128)S(1)} collective-permute-done((f32[128,512]{1,0:T(8,128)}, f32[128,512]{1,0:T(8,128)S(1)}, u32[]{:S(2)}, u32[]{:S(2)}) %collective-permute-start.19) | collective-permute-done | bytes 262176 | tf_op jit(solution)/shard_map/ppermute | solution.py:17
  99.4 3.6 %collective-permute-start.22 = (bf16[2,128,256]{2,1,0:T(8,128)(2,1)S(1)}, bf16[2,128,256]{2,1,0:T(8,128)(2,1)S(1)}, u32[]{:S(2)}, u32[]{:S(2)}) collective-permute-start(bf16[2,128,256]{2,1,0:T(8,128)(2,1)S(1)} %pad_maximum_fusion.5.rest_2_), channel_id=1, source_target_pairs={{0,3},{1,2},{2,1},{3,0},{4,7},{5,6},{6,5},{7,4},{8,11},{9,10},{10,... | collective-permute-start | bytes 393224 | tf_op jit(solution)/shard_map/ppermute | solution.py:17
  104.5 4.5 %collective-permute-done.24.rest_13_ = f32[128,512]{1,0:T(8,128)S(1)} collective-permute-done((f32[128,512]{1,0:T(8,128)}, f32[128,512]{1,0:T(8,128)S(1)}, u32[]{:S(2)}, u32[]{:S(2)}) %collective-permute-start.24) | collective-permute-done | bytes 262176 | tf_op jit(solution)/shard_map/ppermute | solution.py:17
  109.1 2.3 %collective-permute-done.22.rest_5_ = bf16[2,128,256]{2,1,0:T(8,128)(2,1)S(1)} collective-permute-done((bf16[2,128,256]{2,1,0:T(8,128)(2,1)S(1)}, bf16[2,128,256]{2,1,0:T(8,128)(2,1)S(1)}, u32[]{:S(2)}, u32[]{:S(2)}) %collective-permute-start.22) | collective-permute-done | bytes 131104 | tf_op jit(solution)/shard_map/ppermute | solution.py:17
  113.0 12.7 %attend.1 = (f32[2048,128]{1,0:T(8,128)}, f32[2048,128]{1,0:T(8,128)}) custom-call(s32[1,4]{1,0:T(1,128)} %len_ref.1, bf16[128,1024]{1,0:T(8,128)(2,1)} %d_ref.1, bf16[8,256,128]{2,1,0:T(8,128)(2,1)} %copy-done.6, bf16[8,256,128]{2,1,0:T(8,128)(2,1)} %copy-done.11, bf16[2,128,256]{2,1,0:T(8,128)(2,1)} %copy-done.8, bf16[2,128,256]{2,1,0:T(8,128)(2,1)} %copy-done.20, ...), custom_call_target="tpu_custom_call" | custom-call | flops 3221225472 | bytes 3145728 | tf_op jit(solution)/shard_map/attend/pallas_call | solution.py:299
  125.8 2.9 %collective-permute-done.25 = f32[2048,128]{1,0:T(8,128)S(1)} collective-permute-done((f32[2048,128]{1,0:T(8,128)}, f32[2048,128]{1,0:T(8,128)S(1)}, u32[]{:S(2)}, u32[]{:S(2)}) %collective-permute-start.25) | collective-permute-done | bytes 1048608 | tf_op jit(solution)/shard_map/ppermute | solution.py:17
  130.1 2.0 %collective-permute-start.26 = (bf16[256,128]{1,0:T(8,128)(2,1)S(1)}, bf16[256,128]{1,0:T(8,128)(2,1)S(1)}, u32[]{:S(2)}, u32[]{:S(2)}) collective-permute-start(bf16[256,128]{1,0:T(8,128)(2,1)S(1)} %get-tuple-element.88), channel_id=1, source_target_pairs={{0,4},{1,5},{2,6},{3,7},{4,0},{5,1},{6,2},{7,3},{8,12},{9,13},{10,... | collective-permute-start | bytes 196616 | tf_op jit(solution)/shard_map/ppermute | solution.py:17
  132.1 2.5 %collective-permute-start.32 = (bf16[256,128]{1,0:T(8,128)(2,1)S(1)}, bf16[256,128]{1,0:T(8,128)(2,1)S(1)}, u32[]{:S(2)}, u32[]{:S(2)}) collective-permute-start(bf16[256,128]{1,0:T(8,128)(2,1)S(1)} %get-tuple-element.89), channel_id=1, source_target_pairs={{0,7},{1,6},{2,5},{3,4},{4,3},{5,2},{6,1},{7,0},{8,15},{9,14},{10,... | collective-permute-start | bytes 196616 | tf_op jit(solution)/shard_map/ppermute | solution.py:17
  134.6 3.4 %collective-permute-start.30 = (bf16[256,128]{1,0:T(8,128)(2,1)S(1)}, bf16[256,128]{1,0:T(8,128)(2,1)S(1)}, u32[]{:S(2)}, u32[]{:S(2)}) collective-permute-start(bf16[256,128]{1,0:T(8,128)(2,1)S(1)} %get-tuple-element.91), channel_id=1, source_target_pairs={{0,5},{1,4},{2,7},{3,6},{4,1},{5,0},{6,3},{7,2},{8,13},{9,12},{10,... | collective-permute-start | bytes 196616 | tf_op jit(solution)/shard_map/ppermute | solution.py:17
  138.9 2.1 %collective-permute-start.28 = (bf16[256,128]{1,0:T(8,128)(2,1)S(1)}, bf16[256,128]{1,0:T(8,128)(2,1)S(1)}, u32[]{:S(2)}, u32[]{:S(2)}) collective-permute-start(bf16[256,128]{1,0:T(8,128)(2,1)S(1)} %get-tuple-element.93), channel_id=1, source_target_pairs={{0,6},{1,7},{2,4},{3,5},{4,2},{5,3},{6,0},{7,1},{8,14},{9,15},{10,... | collective-permute-start | bytes 196616 | tf_op jit(solution)/shard_map/ppermute | solution.py:17
  141.0 2.6 %collective-permute-done.30 = bf16[256,128]{1,0:T(8,128)(2,1)S(1)} collective-permute-done((bf16[256,128]{1,0:T(8,128)(2,1)S(1)}, bf16[256,128]{1,0:T(8,128)(2,1)S(1)}, u32[]{:S(2)}, u32[]{:S(2)}) %collective-permute-start.30) | collective-permute-done | bytes 65568 | tf_op jit(solution)/shard_map/ppermute | solution.py:17
  147.1 3.7 %collective-permute-done.33 = f32[256,128]{1,0:T(8,128)S(1)} collective-permute-done((f32[256,128]{1,0:T(8,128)S(1)}, f32[256,128]{1,0:T(8,128)S(1)}, u32[]{:S(2)}, u32[]{:S(2)}) %collective-permute-start.33) | collective-permute-done | bytes 131104 | tf_op jit(solution)/shard_map/ppermute | solution.py:17
  (107 shorter events, 37.0 us)
Async XLA Ops:
  3.7 33.2 %collective-permute-start = (bf16[640,512]{1,0:T(8,128)(2,1)}, bf16[640,512]{1,0:T(8,128)(2,1)S(1)}, u32[]{:S(2)}, u32[]{:S(2)}) collective-permute-start(bf16[640,512]{1,0:T(8,128)(2,1)} %get-tuple-element.44), channel_id=1, source_target_pairs={{0,4},{1,5},{2,6},{3,7},{4,0},{5,1},{6,2},{7,3},{8,12},{9,13},{10,... | collective-permute-start | bytes 1966088 | tf_op jit(solution)/shard_map/ppermute | solution.py:17
  7.8 39.5 %collective-permute-start.4 = (bf16[128,2048]{1,0:T(8,128)(2,1)}, bf16[128,2048]{1,0:T(8,128)(2,1)S(1)}, u32[]{:S(2)}, u32[]{:S(2)}) collective-permute-start(bf16[128,2048]{1,0:T(8,128)(2,1)} %get-tuple-element.45), channel_id=1, source_target_pairs={{0,1},{1,0},{2,3},{3,2},{4,5},{5,4},{6,7},{7,6},{8,9},{9,8},{10,11... | collective-permute-start | bytes 1572872 | tf_op jit(solution)/shard_map/ppermute | solution.py:17
  9.4 38.0 %collective-permute-start.5 = (bf16[128,2048]{1,0:T(8,128)(2,1)}, bf16[128,2048]{1,0:T(8,128)(2,1)S(1)}, u32[]{:S(2)}, u32[]{:S(2)}) collective-permute-start(bf16[128,2048]{1,0:T(8,128)(2,1)} %get-tuple-element.46), channel_id=1, source_target_pairs={{0,2},{1,3},{2,0},{3,1},{4,6},{5,7},{6,4},{7,5},{8,10},{9,11},{10,... | collective-permute-start | bytes 1572872 | tf_op jit(solution)/shard_map/ppermute | solution.py:17
  10.9 37.2 %collective-permute-start.6 = (bf16[128,2048]{1,0:T(8,128)(2,1)}, bf16[128,2048]{1,0:T(8,128)(2,1)S(1)}, u32[]{:S(2)}, u32[]{:S(2)}) collective-permute-start(bf16[128,2048]{1,0:T(8,128)(2,1)} %get-tuple-element.47), channel_id=1, source_target_pairs={{0,3},{1,2},{2,1},{3,0},{4,7},{5,6},{6,5},{7,4},{8,11},{9,10},{10,... | collective-permute-start | bytes 1572872 | tf_op jit(solution)/shard_map/ppermute | solution.py:17
  37.0 10.3 %collective-permute-start.3 = (bf16[1,384,512]{2,1,0:T(8,128)(2,1)S(1)}, bf16[1,384,512]{2,1,0:T(8,128)(2,1)S(1)}, u32[]{:S(2)}, u32[]{:S(2)}) collective-permute-start(bf16[1,384,512]{2,1,0:T(8,128)(2,1)S(1)} %slice_bitcast_fusion), channel_id=1, source_target_pairs={{0,16},{8,24},{16,0},{24,8},{1,17},{9,25},{17,1},{25,9},{2,18},{10... | collective-permute-start | bytes 1179656 | tf_op jit(solution)/shard_map/ppermute | solution.py:17
  38.6 7.4 %collective-permute-start.2 = (bf16[1,256,128]{2,1,0:T(8,128)(2,1)S(1)}, bf16[1,256,128]{2,1,0:T(8,128)(2,1)S(1)}, u32[]{:S(2)}, u32[]{:S(2)}) collective-permute-start(bf16[1,256,128]{2,1,0:T(8,128)(2,1)S(1)} %select_bitcast_fusion), channel_id=1, source_target_pairs={{0,4},{1,5},{2,6},{3,7},{4,0},{5,1},{6,2},{7,3},{8,12},{9,13},{10,... | collective-permute-start | bytes 196616 | tf_op jit(solution)/shard_map/ppermute | solution.py:17
  48.2 8.8 %collective-permute-start.1 = (bf16[1,256,512]{2,1,0:T(8,128)(2,1)S(1)}, bf16[1,256,512]{2,1,0:T(8,128)(2,1)S(1)}, u32[]{:S(2)}, u32[]{:S(2)}) collective-permute-start(bf16[1,256,512]{2,1,0:T(8,128)(2,1)S(1)} %slice_bitcast_fusion.1), channel_id=1, source_target_pairs={{0,16},{8,24},{16,0},{24,8},{1,17},{9,25},{17,1},{25,9},{2,18},{10... | collective-permute-start | bytes 786440 | tf_op jit(solution)/shard_map/ppermute | solution.py:17
  55.4 7.7 %collective-permute-start.9 = (bf16[4,256,128]{2,1,0:T(8,128)(2,1)S(1)}, bf16[4,256,128]{2,1,0:T(8,128)(2,1)S(1)}, u32[]{:S(2)}, u32[]{:S(2)}) collective-permute-start(bf16[4,256,128]{2,1,0:T(8,128)(2,1)S(1)} %pad_maximum_fusion.3), channel_id=1, source_target_pairs={{0,1},{1,0},{2,3},{3,2},{4,5},{5,4},{6,7},{7,6},{8,9},{9,8},{10,11... | collective-permute-start | bytes 786440 | tf_op jit(solution)/shard_map/ppermute | solution.py:17
  63.2 11.1 %collective-permute-start.10 = (bf16[2,256,512]{2,1,0:T(8,128)(2,1)S(1)}, bf16[2,256,512]{2,1,0:T(8,128)(2,1)S(1)}, u32[]{:S(2)}, u32[]{:S(2)}) collective-permute-start(bf16[2,256,512]{2,1,0:T(8,128)(2,1)S(1)} %pad_maximum_fusion.1.rest_4_), channel_id=1, source_target_pairs={{0,8},{8,0},{16,24},{24,16},{1,9},{9,1},{17,25},{25,17},{2,10},{10... | collective-permute-start | bytes 1572872 | tf_op jit(solution)/shard_map/ppermute | solution.py:17
  65.7 7.7 %collective-permute-start.13 = (f32[128,256]{1,0:T(8,128)}, f32[128,256]{1,0:T(8,128)S(1)}, u32[]{:S(2)}, u32[]{:S(2)}) collective-permute-start(f32[128,256]{1,0:T(8,128)} %get-tuple-element.60), channel_id=1, source_target_pairs={{0,3},{1,2},{2,1},{3,0},{4,7},{5,6},{6,5},{7,4},{8,11},{9,10},{10,... | collective-permute-start | bytes 393224 | tf_op jit(solution)/shard_map/ppermute | solution.py:17
  74.4 17.2 %collective-permute-start.15 = (bf16[8,256,128]{2,1,0:T(8,128)(2,1)S(1)}, bf16[8,256,128]{2,1,0:T(8,128)(2,1)S(1)}, u32[]{:S(2)}, u32[]{:S(2)}) collective-permute-start(bf16[8,256,128]{2,1,0:T(8,128)(2,1)S(1)} %pad_maximum_fusion.2.rest_0_), channel_id=1, source_target_pairs={{0,8},{8,0},{16,24},{24,16},{1,9},{9,1},{17,25},{25,17},{2,10},{10... | collective-permute-start | bytes 1572872 | tf_op jit(solution)/shard_map/ppermute | solution.py:17
  74.4 15.6 %collective-permute-start.16 = (f32[128,512]{1,0:T(8,128)}, f32[128,512]{1,0:T(8,128)S(1)}, u32[]{:S(2)}, u32[]{:S(2)}) collective-permute-start(f32[128,512]{1,0:T(8,128)} %get-tuple-element.69), channel_id=1, source_target_pairs={{0,1},{1,0},{2,3},{3,2},{4,5},{5,4},{6,7},{7,6},{8,9},{9,8},{10,11... | collective-permute-start | bytes 786440 | tf_op jit(solution)/shard_map/ppermute | solution.py:17
  76.0 14.0 %collective-permute-start.17 = (f32[128,512]{1,0:T(8,128)}, f32[128,512]{1,0:T(8,128)S(1)}, u32[]{:S(2)}, u32[]{:S(2)}) collective-permute-start(f32[128,512]{1,0:T(8,128)} %get-tuple-element.70), channel_id=1, source_target_pairs={{0,2},{1,3},{2,0},{3,1},{4,6},{5,7},{6,4},{7,5},{8,10},{9,11},{10,... | collective-permute-start | bytes 786440 | tf_op jit(solution)/shard_map/ppermute | solution.py:17
  76.9 14.7 %collective-permute-start.18 = (f32[128,512]{1,0:T(8,128)}, f32[128,512]{1,0:T(8,128)S(1)}, u32[]{:S(2)}, u32[]{:S(2)}) collective-permute-start(f32[128,512]{1,0:T(8,128)} %get-tuple-element.71), channel_id=1, source_target_pairs={{0,3},{1,2},{2,1},{3,0},{4,7},{5,6},{6,5},{7,4},{8,11},{9,10},{10,... | collective-permute-start | bytes 786440 | tf_op jit(solution)/shard_map/ppermute | solution.py:17
  78.0 12.0 %collective-permute-start.14 = (bf16[1,128,256]{2,1,0:T(8,128)(2,1)S(1)}, bf16[1,128,256]{2,1,0:T(8,128)(2,1)S(1)}, u32[]{:S(2)}, u32[]{:S(2)}) collective-permute-start(bf16[1,128,256]{2,1,0:T(8,128)(2,1)S(1)} %bitcast.7), channel_id=1, source_target_pairs={{0,4},{1,5},{2,6},{3,7},{4,0},{5,1},{6,2},{7,3},{8,12},{9,13},{10,... | collective-permute-start | bytes 196616 | tf_op jit(solution)/shard_map/ppermute | solution.py:17
  91.6 7.8 %collective-permute-start.19 = (f32[128,512]{1,0:T(8,128)}, f32[128,512]{1,0:T(8,128)S(1)}, u32[]{:S(2)}, u32[]{:S(2)}) collective-permute-start(f32[128,512]{1,0:T(8,128)} %get-tuple-element.74), channel_id=1, source_target_pairs={{0,1},{1,0},{2,3},{3,2},{4,5},{5,4},{6,7},{7,6},{8,9},{9,8},{10,11... | collective-permute-start | bytes 786440 | tf_op jit(solution)/shard_map/ppermute | solution.py:17
  93.2 11.4 %collective-permute-start.23 = (f32[128,512]{1,0:T(8,128)}, f32[128,512]{1,0:T(8,128)S(1)}, u32[]{:S(2)}, u32[]{:S(2)}) collective-permute-start(f32[128,512]{1,0:T(8,128)} %get-tuple-element.82), channel_id=1, source_target_pairs={{0,2},{1,3},{2,0},{3,1},{4,6},{5,7},{6,4},{7,5},{8,10},{9,11},{10,... | collective-permute-start | bytes 786440 | tf_op jit(solution)/shard_map/ppermute | solution.py:17
  95.0 14.1 %collective-permute-start.24 = (f32[128,512]{1,0:T(8,128)}, f32[128,512]{1,0:T(8,128)S(1)}, u32[]{:S(2)}, u32[]{:S(2)}) collective-permute-start(f32[128,512]{1,0:T(8,128)} %get-tuple-element.83), channel_id=1, source_target_pairs={{0,3},{1,2},{2,1},{3,0},{4,7},{5,6},{6,5},{7,4},{8,11},{9,10},{10,... | collective-permute-start | bytes 786440 | tf_op jit(solution)/shard_map/ppermute | solution.py:17
  99.4 11.9 %collective-permute-start.22 = (bf16[2,128,256]{2,1,0:T(8,128)(2,1)S(1)}, bf16[2,128,256]{2,1,0:T(8,128)(2,1)S(1)}, u32[]{:S(2)}, u32[]{:S(2)}) collective-permute-start(bf16[2,128,256]{2,1,0:T(8,128)(2,1)S(1)} %pad_maximum_fusion.5.rest_2_), channel_id=1, source_target_pairs={{0,3},{1,2},{2,1},{3,0},{4,7},{5,6},{6,5},{7,4},{8,11},{9,10},{10,... | collective-permute-start | bytes 393224 | tf_op jit(solution)/shard_map/ppermute | solution.py:17
  103.0 8.9 %collective-permute-start.21 = (bf16[2,128,256]{2,1,0:T(8,128)(2,1)S(1)}, bf16[2,128,256]{2,1,0:T(8,128)(2,1)S(1)}, u32[]{:S(2)}, u32[]{:S(2)}) collective-permute-start(bf16[2,128,256]{2,1,0:T(8,128)(2,1)S(1)} %pad_maximum_fusion.5.rest_2_), channel_id=1, source_target_pairs={{0,2},{1,3},{2,0},{3,1},{4,6},{5,7},{6,4},{7,5},{8,10},{9,11},{10,... | collective-permute-start | bytes 393224 | tf_op jit(solution)/shard_map/ppermute | solution.py:17
  103.2 9.2 %collective-permute-start.20 = (bf16[2,128,256]{2,1,0:T(8,128)(2,1)S(1)}, bf16[2,128,256]{2,1,0:T(8,128)(2,1)S(1)}, u32[]{:S(2)}, u32[]{:S(2)}) collective-permute-start(bf16[2,128,256]{2,1,0:T(8,128)(2,1)S(1)} %pad_maximum_fusion.5.rest_2_), channel_id=1, source_target_pairs={{0,1},{1,0},{2,3},{3,2},{4,5},{5,4},{6,7},{7,6},{8,9},{9,8},{10,11... | collective-permute-start | bytes 393224 | tf_op jit(solution)/shard_map/ppermute | solution.py:17
  130.1 8.8 %collective-permute-start.26 = (bf16[256,128]{1,0:T(8,128)(2,1)S(1)}, bf16[256,128]{1,0:T(8,128)(2,1)S(1)}, u32[]{:S(2)}, u32[]{:S(2)}) collective-permute-start(bf16[256,128]{1,0:T(8,128)(2,1)S(1)} %get-tuple-element.88), channel_id=1, source_target_pairs={{0,4},{1,5},{2,6},{3,7},{4,0},{5,1},{6,2},{7,3},{8,12},{9,13},{10,... | collective-permute-start | bytes 196616 | tf_op jit(solution)/shard_map/ppermute | solution.py:17
  132.1 8.9 %collective-permute-start.32 = (bf16[256,128]{1,0:T(8,128)(2,1)S(1)}, bf16[256,128]{1,0:T(8,128)(2,1)S(1)}, u32[]{:S(2)}, u32[]{:S(2)}) collective-permute-start(bf16[256,128]{1,0:T(8,128)(2,1)S(1)} %get-tuple-element.89), channel_id=1, source_target_pairs={{0,7},{1,6},{2,5},{3,4},{4,3},{5,2},{6,1},{7,0},{8,15},{9,14},{10,... | collective-permute-start | bytes 196616 | tf_op jit(solution)/shard_map/ppermute | solution.py:17
  134.6 9.0 %collective-permute-start.30 = (bf16[256,128]{1,0:T(8,128)(2,1)S(1)}, bf16[256,128]{1,0:T(8,128)(2,1)S(1)}, u32[]{:S(2)}, u32[]{:S(2)}) collective-permute-start(bf16[256,128]{1,0:T(8,128)(2,1)S(1)} %get-tuple-element.91), channel_id=1, source_target_pairs={{0,5},{1,4},{2,7},{3,6},{4,1},{5,0},{6,3},{7,2},{8,13},{9,12},{10,... | collective-permute-start | bytes 196616 | tf_op jit(solution)/shard_map/ppermute | solution.py:17
  (32 other events, 343.3 us)

commit v6 on v5

--- a/solution.py
+++ b/solution.py
@@ -367,17 +367,17 @@
         parts_kv = from_owners(out_kv)
         parts_a = from_owners(out_a)
         own = functools.reduce(lambda a, b: a + b, parts_kv).astype(BF16)
-        far_b[1], own, cache = together(far_b[1], own, cache)
-        cache = [cache, swap(cache, "dp", n_dp, 1)]
+        far_b[1], own = together(far_b[1], own)
         group, _ = double(own[None], [0], "fsdp", n_fsdp, inner)
         near_b, layout_b = [(w_query, at_b, wide_b)], [(0, 0, share, wide_b, 0, 0)]
         (out_b,) = multiply(
             hidden, received, near_b, far_b, layout_b, d_order, n_fsdp, (wide_b,)
         )
-        group, cache[1], *tied = together(group, cache[1], *out_b, *parts_a[1:])
+        group, cache, *tied = together(group, cache, *out_b, *parts_a[1:])
         out_b, parts_a[1:] = tied[:inner], tied[inner:]
         parts_b = from_owners(out_b)
-        group, parts_b[1] = together(group, parts_b[1])
+        cache = [cache, swap(cache, "dp", n_dp, 1)]
+        group, parts_b[1], cache[1] = together(group, parts_b[1], cache[1])
         group = [group] + [swap(group, "fsdp", n_fsdp, k) for k in range(1, inner)]
         g_order = [o for k in range(inner) for o in (k, k ^ inner)]
         keep, give = attend(lengths, [parts_a, parts_b], d_attn, cache, group, g_order)

time: 153 us -> 149 us (0.974)
  waiting for transfers between devices: 76.6 us -> 73 us
    ppermute x35, waiting for transfers between devices: 76.6 us -> 73 us  [swap(): return lax.ppermute(value, axis, [(i, i ^ bit) for i in range(size)])]
  transfers between devices with their start and end apart: 35 -> 35, of which waited for: 22 -> 23; matrix products, arithmetic and copies ran while one was open for 1% -> 1% of each run, Pallas kernels for 7% -> 7%
where the time goes in v6:
time: 149 us
  waiting for transfers between devices  73 us (49%)
  starting transfers between devices  44.4 us (30%)
  Pallas kernels  26.2 us (18%)
  other arithmetic  3.34 us (2%)
    ppermute x35, waiting for transfers between devices, swap(): return lax.ppermute(value, axis, [(i, i ^ bit) for i in range(size)])  73 us
    ppermute x35, starting transfers between devices, swap(): return lax.ppermute(value, axis, [(i, i ^ bit) for i in range(size)])  44.4 us
    pallas_call x1, Pallas kernels, attend(): pl.pallas_call(body, in_specs=[pl.BlockSpec(memory_space=pltpu.SMEM)] + [...  12.7 us
    pallas_call x2, Pallas kernels, multiply(): pl.pallas_call(body, in_specs=[pl.BlockSpec(memory_space=pl.ANY)] * (1 +...  10.4 us
    pallas_call x1, Pallas kernels, prepare(): pl.pallas_call(body, in_specs=[pl.BlockSpec(memory_space=pl.ANY)] * 4, ou...  3.08 us
  transfers between devices with their start and end apart: 35, of which 23 were waited for; matrix products, arithmetic and copies ran while one was open for 1% of the time, Pallas kernels for 7%

profile of v6, /device:TPU:0, one launch (start us, length us, event | category | flops | bytes accessed | tf_op | source)
XLA Modules:
  0.0 148.8 jit_solution(11583162349839040470)
XLA Ops:
  0.6 3.1 %prepare.1 = (bf16[128,2048]{1,0:T(8,128)(2,1)}, bf16[128,2048]{1,0:T(8,128)(2,1)}, bf16[128,2048]{1,0:T(8,128)(2,1)}, bf16[640,512]{1,0:T(8,128)(2,1)}) custom-call(bf16[128,8192]{1,0:T(8,128)(2,1)} %hidden_ref.5, bf16[1024,1024]{1,0:T(8,128)(2,1)} %rest_3_.3, bf16[1024,128]{1,0:T(8,128)(2,1)} %rest_3_.2, bf16[1024,128]{1,0:T(8,128)(2,1)} %rest_4_.1), custom_call_target="tpu_custom_call" | custom-call | bytes 4456448 | tf_op jit(solution)/shard_map/prepare/pallas_call | solution.py:83
  3.7 4.1 %collective-permute-start = (bf16[640,512]{1,0:T(8,128)(2,1)}, bf16[640,512]{1,0:T(8,128)(2,1)S(1)}, u32[]{:S(2)}, u32[]{:S(2)}) collective-permute-start(bf16[640,512]{1,0:T(8,128)(2,1)} %get-tuple-element.44), channel_id=1, source_target_pairs={{0,4},{1,5},{2,6},{3,7},{4,0},{5,1},{6,2},{7,3},{8,12},{9,13},{10,... | collective-permute-start | bytes 1966088 | tf_op jit(solution)/shard_map/ppermute | solution.py:17
  11.3 25.6 %collective-permute-done = bf16[640,512]{1,0:T(8,128)(2,1)S(1)} collective-permute-done((bf16[640,512]{1,0:T(8,128)(2,1)}, bf16[640,512]{1,0:T(8,128)(2,1)S(1)}, u32[]{:S(2)}, u32[]{:S(2)}) %collective-permute-start) | collective-permute-done | bytes 655392 | tf_op jit(solution)/shard_map/ppermute | solution.py:17
  37.0 1.6 %collective-permute-start.3 = (bf16[1,384,512]{2,1,0:T(8,128)(2,1)S(1)}, bf16[1,384,512]{2,1,0:T(8,128)(2,1)S(1)}, u32[]{:S(2)}, u32[]{:S(2)}) collective-permute-start(bf16[1,384,512]{2,1,0:T(8,128)(2,1)S(1)} %slice_bitcast_fusion), channel_id=1, source_target_pairs={{0,16},{8,24},{16,0},{24,8},{1,17},{9,25},{17,1},{25,9},{2,18},{10... | collective-permute-start | bytes 1179656 | tf_op jit(solution)/shard_map/ppermute | solution.py:17
  38.7 7.3 %collective-permute-done.2 = bf16[1,256,128]{2,1,0:T(8,128)(2,1)S(1)} collective-permute-done((bf16[1,256,128]{2,1,0:T(8,128)(2,1)S(1)}, bf16[1,256,128]{2,1,0:T(8,128)(2,1)S(1)}, u32[]{:S(2)}, u32[]{:S(2)}) %collective-permute-start.2) | collective-permute-done | bytes 65568 | tf_op jit(solution)/shard_map/ppermute | solution.py:17
  50.6 4.8 %collective-permute-done.7 = bf16[2,256,128]{2,1,0:T(8,128)(2,1)S(1)} collective-permute-done((bf16[2,256,128]{2,1,0:T(8,128)(2,1)S(1)}, bf16[2,256,128]{2,1,0:T(8,128)(2,1)S(1)}, u32[]{:S(2)}, u32[]{:S(2)}) %collective-permute-start.7) | collective-permute-done | bytes 131104 | tf_op jit(solution)/shard_map/ppermute | solution.py:17
  55.4 1.6 %collective-permute-start.9 = (bf16[4,256,128]{2,1,0:T(8,128)(2,1)S(1)}, bf16[4,256,128]{2,1,0:T(8,128)(2,1)S(1)}, u32[]{:S(2)}, u32[]{:S(2)}) collective-permute-start(bf16[4,256,128]{2,1,0:T(8,128)(2,1)S(1)} %pad_maximum_fusion.3), channel_id=1, source_target_pairs={{0,1},{1,0},{2,3},{3,2},{4,5},{5,4},{6,7},{7,6},{8,9},{9,8},{10,11... | collective-permute-start | bytes 786440 | tf_op jit(solution)/shard_map/ppermute | solution.py:17
  57.2 5.9 %multiply.2 = (f32[128,256]{1,0:T(8,128)}, f32[128,256]{1,0:T(8,128)}, f32[128,256]{1,0:T(8,128)}, f32[128,256]{1,0:T(8,128)}, f32[128,512]{1,0:T(8,128)}, /*ind...) custom-call(bf16[128,8192]{1,0:T(8,128)(2,1)} %hidden_ref.5, bf16[128,2048]{1,0:T(8,128)(2,1)} %copy-done.2, ...), custom_call_target="tpu_custom_call" | custom-call | flops 1610612736 | bytes 6815744 | tf_op jit(solution)/shard_map/multiply/pallas_call | solution.py:154
  75.0 2.8 %collective-permute-start.14 = (bf16[1,128,256]{2,1,0:T(8,128)(2,1)S(1)}, bf16[1,128,256]{2,1,0:T(8,128)(2,1)S(1)}, u32[]{:S(2)}, u32[]{:S(2)}) collective-permute-start(bf16[1,128,256]{2,1,0:T(8,128)(2,1)S(1)} %bitcast.7), channel_id=1, source_target_pairs={{0,4},{1,5},{2,6},{3,7},{4,0},{5,1},{6,2},{7,3},{8,12},{9,13},{10,... | collective-permute-start | bytes 196616 | tf_op jit(solution)/shard_map/ppermute | solution.py:17
  77.7 4.6 %multiply.3 = (f32[128,512]{1,0:T(8,128)}, f32[128,512]{1,0:T(8,128)}, f32[128,512]{1,0:T(8,128)}, f32[128,512]{1,0:T(8,128)}) custom-call(bf16[128,8192]{1,0:T(8,128)(2,1)} %hidden_ref.5, bf16[128,2048]{1,0:T(8,128)(2,1)} %copy-done.2, bf16[128,2048]{1,0:T(8,128)(2,1)} %copy-done.3, bf16[128,2048]{1,0:T(8,128)(2,1)} %copy-done.4, ...), custom_call_target="tpu_custom_call" | custom-call | flops 1073741824 | bytes 5242880 | tf_op jit(solution)/shard_map/multiply/pallas_call | solution.py:154
  82.3 2.2 %collective-permute-done.14 = bf16[1,128,256]{2,1,0:T(8,128)(2,1)S(1)} collective-permute-done((bf16[1,128,256]{2,1,0:T(8,128)(2,1)S(1)}, bf16[1,128,256]{2,1,0:T(8,128)(2,1)S(1)}, u32[]{:S(2)}, u32[]{:S(2)}) %collective-permute-start.14) | collective-permute-done | bytes 65568 | tf_op jit(solution)/shard_map/ppermute | solution.py:17
  86.1 1.6 %collective-permute-start.18 = (f32[128,512]{1,0:T(8,128)}, f32[128,512]{1,0:T(8,128)S(1)}, u32[]{:S(2)}, u32[]{:S(2)}) collective-permute-start(f32[128,512]{1,0:T(8,128)} %get-tuple-element.73), channel_id=1, source_target_pairs={{0,1},{1,0},{2,3},{3,2},{4,5},{5,4},{6,7},{7,6},{8,9},{9,8},{10,11... | collective-permute-start | bytes 786440 | tf_op jit(solution)/shard_map/ppermute | solution.py:17
  87.7 1.9 %collective-permute-start.23 = (f32[128,512]{1,0:T(8,128)}, f32[128,512]{1,0:T(8,128)S(1)}, u32[]{:S(2)}, u32[]{:S(2)}) collective-permute-start(f32[128,512]{1,0:T(8,128)} %get-tuple-element.82), channel_id=1, source_target_pairs={{0,2},{1,3},{2,0},{3,1},{4,6},{5,7},{6,4},{7,5},{8,10},{9,11},{10,... | collective-permute-start | bytes 786440 | tf_op jit(solution)/shard_map/ppermute | solution.py:17
  90.5 4.5 %collective-permute-done.18.rest_11_ = f32[128,512]{1,0:T(8,128)S(1)} collective-permute-done((f32[128,512]{1,0:T(8,128)}, f32[128,512]{1,0:T(8,128)S(1)}, u32[]{:S(2)}, u32[]{:S(2)}) %collective-permute-start.18) | collective-permute-done | bytes 262176 | tf_op jit(solution)/shard_map/ppermute | solution.py:17
  95.0 2.9 %collective-permute-start.22 = (bf16[2,128,256]{2,1,0:T(8,128)(2,1)S(1)}, bf16[2,128,256]{2,1,0:T(8,128)(2,1)S(1)}, u32[]{:S(2)}, u32[]{:S(2)}) collective-permute-start(bf16[2,128,256]{2,1,0:T(8,128)(2,1)S(1)} %pad_maximum_fusion.5.rest_2_), channel_id=1, source_target_pairs={{0,3},{1,2},{2,1},{3,0},{4,7},{5,6},{6,5},{7,4},{8,11},{9,10},{10,... | collective-permute-start | bytes 393224 | tf_op jit(solution)/shard_map/ppermute | solution.py:17
  99.5 4.1 %collective-permute-done.24.rest_13_ = f32[128,512]{1,0:T(8,128)S(1)} collective-permute-done((f32[128,512]{1,0:T(8,128)}, f32[128,512]{1,0:T(8,128)S(1)}, u32[]{:S(2)}, u32[]{:S(2)}) %collective-permute-start.24) | collective-permute-done | bytes 262176 | tf_op jit(solution)/shard_map/ppermute | solution.py:17
  103.6 2.8 %collective-permute-done.22.rest_5_ = bf16[2,128,256]{2,1,0:T(8,128)(2,1)S(1)} collective-permute-done((bf16[2,128,256]{2,1,0:T(8,128)(2,1)S(1)}, bf16[2,128,256]{2,1,0:T(8,128)(2,1)S(1)}, u32[]{:S(2)}, u32[]{:S(2)}) %collective-permute-start.22) | collective-permute-done | bytes 131104 | tf_op jit(solution)/shard_map/ppermute | solution.py:17
  109.3 12.7 %attend.1 = (f32[2048,128]{1,0:T(8,128)}, f32[2048,128]{1,0:T(8,128)}) custom-call(s32[1,4]{1,0:T(1,128)} %len_ref.1, bf16[128,1024]{1,0:T(8,128)(2,1)} %d_ref.1, bf16[8,256,128]{2,1,0:T(8,128)(2,1)} %copy-done.6, bf16[8,256,128]{2,1,0:T(8,128)(2,1)} %copy-done.11, bf16[2,128,256]{2,1,0:T(8,128)(2,1)} %copy-done.8, bf16[2,128,256]{2,1,0:T(8,128)(2,1)} %copy-done.20, ...), custom_call_target="tpu_custom_call" | custom-call | flops 3221225472 | bytes 3145728 | tf_op jit(solution)/shard_map/attend/pallas_call | solution.py:299
  122.2 2.7 %collective-permute-done.25 = f32[2048,128]{1,0:T(8,128)S(1)} collective-permute-done((f32[2048,128]{1,0:T(8,128)}, f32[2048,128]{1,0:T(8,128)S(1)}, u32[]{:S(2)}, u32[]{:S(2)}) %collective-permute-start.25) | collective-permute-done | bytes 1048608 | tf_op jit(solution)/shard_map/ppermute | solution.py:17
  127.7 2.8 %collective-permute-start.32 = (bf16[256,128]{1,0:T(8,128)(2,1)S(1)}, bf16[256,128]{1,0:T(8,128)(2,1)S(1)}, u32[]{:S(2)}, u32[]{:S(2)}) collective-permute-start(bf16[256,128]{1,0:T(8,128)(2,1)S(1)} %get-tuple-element.89), channel_id=1, source_target_pairs={{0,7},{1,6},{2,5},{3,4},{4,3},{5,2},{6,1},{7,0},{8,15},{9,14},{10,... | collective-permute-start | bytes 196616 | tf_op jit(solution)/shard_map/ppermute | solution.py:17
  130.8 3.0 %collective-permute-start.30 = (bf16[256,128]{1,0:T(8,128)(2,1)S(1)}, bf16[256,128]{1,0:T(8,128)(2,1)S(1)}, u32[]{:S(2)}, u32[]{:S(2)}) collective-permute-start(bf16[256,128]{1,0:T(8,128)(2,1)S(1)} %get-tuple-element.91), channel_id=1, source_target_pairs={{0,5},{1,4},{2,7},{3,6},{4,1},{5,0},{6,3},{7,2},{8,13},{9,12},{10,... | collective-permute-start | bytes 196616 | tf_op jit(solution)/shard_map/ppermute | solution.py:17
  134.5 2.8 %collective-permute-start.28 = (bf16[256,128]{1,0:T(8,128)(2,1)S(1)}, bf16[256,128]{1,0:T(8,128)(2,1)S(1)}, u32[]{:S(2)}, u32[]{:S(2)}) collective-permute-start(bf16[256,128]{1,0:T(8,128)(2,1)S(1)} %get-tuple-element.93), channel_id=1, source_target_pairs={{0,6},{1,7},{2,4},{3,5},{4,2},{5,3},{6,0},{7,1},{8,14},{9,15},{10,... | collective-permute-start | bytes 196616 | tf_op jit(solution)/shard_map/ppermute | solution.py:17
  138.7 2.0 %collective-permute-done.28 = bf16[256,128]{1,0:T(8,128)(2,1)S(1)} collective-permute-done((bf16[256,128]{1,0:T(8,128)(2,1)S(1)}, bf16[256,128]{1,0:T(8,128)(2,1)S(1)}, u32[]{:S(2)}, u32[]{:S(2)}) %collective-permute-start.28) | collective-permute-done | bytes 65568 | tf_op jit(solution)/shard_map/ppermute | solution.py:17
  142.9 3.8 %collective-permute-done.33 = f32[256,128]{1,0:T(8,128)S(1)} collective-permute-done((f32[256,128]{1,0:T(8,128)S(1)}, f32[256,128]{1,0:T(8,128)S(1)}, u32[]{:S(2)}, u32[]{:S(2)}) %collective-permute-start.33) | collective-permute-done | bytes 131104 | tf_op jit(solution)/shard_map/ppermute | solution.py:17
  (107 shorter events, 36.8 us)
Async XLA Ops:
  3.7 33.2 %collective-permute-start = (bf16[640,512]{1,0:T(8,128)(2,1)}, bf16[640,512]{1,0:T(8,128)(2,1)S(1)}, u32[]{:S(2)}, u32[]{:S(2)}) collective-permute-start(bf16[640,512]{1,0:T(8,128)(2,1)} %get-tuple-element.44), channel_id=1, source_target_pairs={{0,4},{1,5},{2,6},{3,7},{4,0},{5,1},{6,2},{7,3},{8,12},{9,13},{10,... | collective-permute-start | bytes 1966088 | tf_op jit(solution)/shard_map/ppermute | solution.py:17
  7.8 39.5 %collective-permute-start.4 = (bf16[128,2048]{1,0:T(8,128)(2,1)}, bf16[128,2048]{1,0:T(8,128)(2,1)S(1)}, u32[]{:S(2)}, u32[]{:S(2)}) collective-permute-start(bf16[128,2048]{1,0:T(8,128)(2,1)} %get-tuple-element.45), channel_id=1, source_target_pairs={{0,1},{1,0},{2,3},{3,2},{4,5},{5,4},{6,7},{7,6},{8,9},{9,8},{10,11... | collective-permute-start | bytes 1572872 | tf_op jit(solution)/shard_map/ppermute | solution.py:17
  9.4 38.0 %collective-permute-start.5 = (bf16[128,2048]{1,0:T(8,128)(2,1)}, bf16[128,2048]{1,0:T(8,128)(2,1)S(1)}, u32[]{:S(2)}, u32[]{:S(2)}) collective-permute-start(bf16[128,2048]{1,0:T(8,128)(2,1)} %get-tuple-element.46), channel_id=1, source_target_pairs={{0,2},{1,3},{2,0},{3,1},{4,6},{5,7},{6,4},{7,5},{8,10},{9,11},{10,... | collective-permute-start | bytes 1572872 | tf_op jit(solution)/shard_map/ppermute | solution.py:17
  10.9 37.2 %collective-permute-start.6 = (bf16[128,2048]{1,0:T(8,128)(2,1)}, bf16[128,2048]{1,0:T(8,128)(2,1)S(1)}, u32[]{:S(2)}, u32[]{:S(2)}) collective-permute-start(bf16[128,2048]{1,0:T(8,128)(2,1)} %get-tuple-element.47), channel_id=1, source_target_pairs={{0,3},{1,2},{2,1},{3,0},{4,7},{5,6},{6,5},{7,4},{8,11},{9,10},{10,... | collective-permute-start | bytes 1572872 | tf_op jit(solution)/shard_map/ppermute | solution.py:17
  37.0 10.3 %collective-permute-start.3 = (bf16[1,384,512]{2,1,0:T(8,128)(2,1)S(1)}, bf16[1,384,512]{2,1,0:T(8,128)(2,1)S(1)}, u32[]{:S(2)}, u32[]{:S(2)}) collective-permute-start(bf16[1,384,512]{2,1,0:T(8,128)(2,1)S(1)} %slice_bitcast_fusion), channel_id=1, source_target_pairs={{0,16},{8,24},{16,0},{24,8},{1,17},{9,25},{17,1},{25,9},{2,18},{10... | collective-permute-start | bytes 1179656 | tf_op jit(solution)/shard_map/ppermute | solution.py:17
  38.6 7.4 %collective-permute-start.2 = (bf16[1,256,128]{2,1,0:T(8,128)(2,1)S(1)}, bf16[1,256,128]{2,1,0:T(8,128)(2,1)S(1)}, u32[]{:S(2)}, u32[]{:S(2)}) collective-permute-start(bf16[1,256,128]{2,1,0:T(8,128)(2,1)S(1)} %select_bitcast_fusion), channel_id=1, source_target_pairs={{0,4},{1,5},{2,6},{3,7},{4,0},{5,1},{6,2},{7,3},{8,12},{9,13},{10,... | collective-permute-start | bytes 196616 | tf_op jit(solution)/shard_map/ppermute | solution.py:17
  48.2 8.8 %collective-permute-start.1 = (bf16[1,256,512]{2,1,0:T(8,128)(2,1)S(1)}, bf16[1,256,512]{2,1,0:T(8,128)(2,1)S(1)}, u32[]{:S(2)}, u32[]{:S(2)}) collective-permute-start(bf16[1,256,512]{2,1,0:T(8,128)(2,1)S(1)} %slice_bitcast_fusion.1), channel_id=1, source_target_pairs={{0,16},{8,24},{16,0},{24,8},{1,17},{9,25},{17,1},{25,9},{2,18},{10... | collective-permute-start | bytes 786440 | tf_op jit(solution)/shard_map/ppermute | solution.py:17
  55.4 7.7 %collective-permute-start.9 = (bf16[4,256,128]{2,1,0:T(8,128)(2,1)S(1)}, bf16[4,256,128]{2,1,0:T(8,128)(2,1)S(1)}, u32[]{:S(2)}, u32[]{:S(2)}) collective-permute-start(bf16[4,256,128]{2,1,0:T(8,128)(2,1)S(1)} %pad_maximum_fusion.3), channel_id=1, source_target_pairs={{0,1},{1,0},{2,3},{3,2},{4,5},{5,4},{6,7},{7,6},{8,9},{9,8},{10,11... | collective-permute-start | bytes 786440 | tf_op jit(solution)/shard_map/ppermute | solution.py:17
  63.2 11.7 %collective-permute-start.10 = (bf16[2,256,512]{2,1,0:T(8,128)(2,1)S(1)}, bf16[2,256,512]{2,1,0:T(8,128)(2,1)S(1)}, u32[]{:S(2)}, u32[]{:S(2)}) collective-permute-start(bf16[2,256,512]{2,1,0:T(8,128)(2,1)S(1)} %pad_maximum_fusion.1.rest_4_), channel_id=1, source_target_pairs={{0,8},{8,0},{16,24},{24,16},{1,9},{9,1},{17,25},{25,17},{2,10},{10... | collective-permute-start | bytes 1572872 | tf_op jit(solution)/shard_map/ppermute | solution.py:17
  65.7 8.3 %collective-permute-start.13 = (f32[128,256]{1,0:T(8,128)}, f32[128,256]{1,0:T(8,128)S(1)}, u32[]{:S(2)}, u32[]{:S(2)}) collective-permute-start(f32[128,256]{1,0:T(8,128)} %get-tuple-element.60), channel_id=1, source_target_pairs={{0,3},{1,2},{2,1},{3,0},{4,7},{5,6},{6,5},{7,4},{8,11},{9,10},{10,... | collective-permute-start | bytes 393224 | tf_op jit(solution)/shard_map/ppermute | solution.py:17
  66.8 17.7 %collective-permute-start.15 = (f32[128,512]{1,0:T(8,128)}, f32[128,512]{1,0:T(8,128)S(1)}, u32[]{:S(2)}, u32[]{:S(2)}) collective-permute-start(f32[128,512]{1,0:T(8,128)} %get-tuple-element.68), channel_id=1, source_target_pairs={{0,1},{1,0},{2,3},{3,2},{4,5},{5,4},{6,7},{7,6},{8,9},{9,8},{10,11... | collective-permute-start | bytes 786440 | tf_op jit(solution)/shard_map/ppermute | solution.py:17
  69.5 15.1 %collective-permute-start.16 = (f32[128,512]{1,0:T(8,128)}, f32[128,512]{1,0:T(8,128)S(1)}, u32[]{:S(2)}, u32[]{:S(2)}) collective-permute-start(f32[128,512]{1,0:T(8,128)} %get-tuple-element.69), channel_id=1, source_target_pairs={{0,2},{1,3},{2,0},{3,1},{4,6},{5,7},{6,4},{7,5},{8,10},{9,11},{10,... | collective-permute-start | bytes 786440 | tf_op jit(solution)/shard_map/ppermute | solution.py:17
  71.4 14.7 %collective-permute-start.17 = (f32[128,512]{1,0:T(8,128)}, f32[128,512]{1,0:T(8,128)S(1)}, u32[]{:S(2)}, u32[]{:S(2)}) collective-permute-start(f32[128,512]{1,0:T(8,128)} %get-tuple-element.70), channel_id=1, source_target_pairs={{0,3},{1,2},{2,1},{3,0},{4,7},{5,6},{6,5},{7,4},{8,11},{9,10},{10,... | collective-permute-start | bytes 786440 | tf_op jit(solution)/shard_map/ppermute | solution.py:17
  75.0 9.5 %collective-permute-start.14 = (bf16[1,128,256]{2,1,0:T(8,128)(2,1)S(1)}, bf16[1,128,256]{2,1,0:T(8,128)(2,1)S(1)}, u32[]{:S(2)}, u32[]{:S(2)}) collective-permute-start(bf16[1,128,256]{2,1,0:T(8,128)(2,1)S(1)} %bitcast.7), channel_id=1, source_target_pairs={{0,4},{1,5},{2,6},{3,7},{4,0},{5,1},{6,2},{7,3},{8,12},{9,13},{10,... | collective-permute-start | bytes 196616 | tf_op jit(solution)/shard_map/ppermute | solution.py:17
  86.1 8.9 %collective-permute-start.19 = (bf16[8,256,128]{2,1,0:T(8,128)(2,1)S(1)}, bf16[8,256,128]{2,1,0:T(8,128)(2,1)S(1)}, u32[]{:S(2)}, u32[]{:S(2)}) collective-permute-start(bf16[8,256,128]{2,1,0:T(8,128)(2,1)S(1)} %pad_maximum_fusion.2.rest_0_), channel_id=1, source_target_pairs={{0,8},{8,0},{16,24},{24,16},{1,9},{9,1},{17,25},{25,17},{2,10},{10... | collective-permute-start | bytes 1572872 | tf_op jit(solution)/shard_map/ppermute | solution.py:17
  86.1 8.9 %collective-permute-start.18 = (f32[128,512]{1,0:T(8,128)}, f32[128,512]{1,0:T(8,128)S(1)}, u32[]{:S(2)}, u32[]{:S(2)}) collective-permute-start(f32[128,512]{1,0:T(8,128)} %get-tuple-element.73), channel_id=1, source_target_pairs={{0,1},{1,0},{2,3},{3,2},{4,5},{5,4},{6,7},{7,6},{8,9},{9,8},{10,11... | collective-permute-start | bytes 786440 | tf_op jit(solution)/shard_map/ppermute | solution.py:17
  87.7 11.8 %collective-permute-start.23 = (f32[128,512]{1,0:T(8,128)}, f32[128,512]{1,0:T(8,128)S(1)}, u32[]{:S(2)}, u32[]{:S(2)}) collective-permute-start(f32[128,512]{1,0:T(8,128)} %get-tuple-element.82), channel_id=1, source_target_pairs={{0,2},{1,3},{2,0},{3,1},{4,6},{5,7},{6,4},{7,5},{8,10},{9,11},{10,... | collective-permute-start | bytes 786440 | tf_op jit(solution)/shard_map/ppermute | solution.py:17
  89.6 14.0 %collective-permute-start.24 = (f32[128,512]{1,0:T(8,128)}, f32[128,512]{1,0:T(8,128)S(1)}, u32[]{:S(2)}, u32[]{:S(2)}) collective-permute-start(f32[128,512]{1,0:T(8,128)} %get-tuple-element.83), channel_id=1, source_target_pairs={{0,3},{1,2},{2,1},{3,0},{4,7},{5,6},{6,5},{7,4},{8,11},{9,10},{10,... | collective-permute-start | bytes 786440 | tf_op jit(solution)/shard_map/ppermute | solution.py:17
  95.0 11.3 %collective-permute-start.22 = (bf16[2,128,256]{2,1,0:T(8,128)(2,1)S(1)}, bf16[2,128,256]{2,1,0:T(8,128)(2,1)S(1)}, u32[]{:S(2)}, u32[]{:S(2)}) collective-permute-start(bf16[2,128,256]{2,1,0:T(8,128)(2,1)S(1)} %pad_maximum_fusion.5.rest_2_), channel_id=1, source_target_pairs={{0,3},{1,2},{2,1},{3,0},{4,7},{5,6},{6,5},{7,4},{8,11},{9,10},{10,... | collective-permute-start | bytes 393224 | tf_op jit(solution)/shard_map/ppermute | solution.py:17
  98.0 9.8 %collective-permute-start.21 = (bf16[2,128,256]{2,1,0:T(8,128)(2,1)S(1)}, bf16[2,128,256]{2,1,0:T(8,128)(2,1)S(1)}, u32[]{:S(2)}, u32[]{:S(2)}) collective-permute-start(bf16[2,128,256]{2,1,0:T(8,128)(2,1)S(1)} %pad_maximum_fusion.5.rest_2_), channel_id=1, source_target_pairs={{0,2},{1,3},{2,0},{3,1},{4,6},{5,7},{6,4},{7,5},{8,10},{9,11},{10,... | collective-permute-start | bytes 393224 | tf_op jit(solution)/shard_map/ppermute | solution.py:17
  98.1 10.5 %collective-permute-start.20 = (bf16[2,128,256]{2,1,0:T(8,128)(2,1)S(1)}, bf16[2,128,256]{2,1,0:T(8,128)(2,1)S(1)}, u32[]{:S(2)}, u32[]{:S(2)}) collective-permute-start(bf16[2,128,256]{2,1,0:T(8,128)(2,1)S(1)} %pad_maximum_fusion.5.rest_2_), channel_id=1, source_target_pairs={{0,1},{1,0},{2,3},{3,2},{4,5},{5,4},{6,7},{7,6},{8,9},{9,8},{10,11... | collective-permute-start | bytes 393224 | tf_op jit(solution)/shard_map/ppermute | solution.py:17
  126.3 8.2 %collective-permute-start.26 = (bf16[256,128]{1,0:T(8,128)(2,1)S(1)}, bf16[256,128]{1,0:T(8,128)(2,1)S(1)}, u32[]{:S(2)}, u32[]{:S(2)}) collective-permute-start(bf16[256,128]{1,0:T(8,128)(2,1)S(1)} %get-tuple-element.88), channel_id=1, source_target_pairs={{0,4},{1,5},{2,6},{3,7},{4,0},{5,1},{6,2},{7,3},{8,12},{9,13},{10,... | collective-permute-start | bytes 196616 | tf_op jit(solution)/shard_map/ppermute | solution.py:17
  127.7 9.5 %collective-permute-start.32 = (bf16[256,128]{1,0:T(8,128)(2,1)S(1)}, bf16[256,128]{1,0:T(8,128)(2,1)S(1)}, u32[]{:S(2)}, u32[]{:S(2)}) collective-permute-start(bf16[256,128]{1,0:T(8,128)(2,1)S(1)} %get-tuple-element.89), channel_id=1, source_target_pairs={{0,7},{1,6},{2,5},{3,4},{4,3},{5,2},{6,1},{7,0},{8,15},{9,14},{10,... | collective-permute-start | bytes 196616 | tf_op jit(solution)/shard_map/ppermute | solution.py:17
  130.8 7.5 %collective-permute-start.30 = (bf16[256,128]{1,0:T(8,128)(2,1)S(1)}, bf16[256,128]{1,0:T(8,128)(2,1)S(1)}, u32[]{:S(2)}, u32[]{:S(2)}) collective-permute-start(bf16[256,128]{1,0:T(8,128)(2,1)S(1)} %get-tuple-element.91), channel_id=1, source_target_pairs={{0,5},{1,4},{2,7},{3,6},{4,1},{5,0},{6,3},{7,2},{8,13},{9,12},{10,... | collective-permute-start | bytes 196616 | tf_op jit(solution)/shard_map/ppermute | solution.py:17
  (32 other events, 344.9 us)

commit v7 on v6

--- a/solution.py
+++ b/solution.py
@@ -182,7 +182,7 @@
     n_group = n_blocks * tokens
     slots = n_blocks // len(group)
     chunk = min(512, n_cache)
-    n_part = sum(len(terms) for terms in partials)
+    n_part = sum(len(terms) for terms, _ in partials)
     dims = (((1,), (1,)), ((), ()))
     spans = [(at, chunk) for at in range(0, n_cache, chunk)]
     spans += [(n_cache + i * slots * tokens, slots * tokens) for i in range(len(group))]
@@ -210,9 +210,9 @@
             pltpu.make_async_copy(cache_refs[0], cv_ref, sems.at[1]).start()
 
         h = 0
-        for terms in partials:
+        for terms, start in partials:
             refs, part_refs = part_refs[: len(terms)], part_refs[len(terms) :]
-            for at in range(0, terms[0].shape[1], head_dim):
+            for at in range(start, terms[0].shape[1], head_dim):
                 rows = pl.ds(h * tokens, tokens)
                 q = refs[0][:, at : at + head_dim]
                 for ref in refs[1:]:
@@ -293,7 +293,7 @@
             out_ref[odd, pl.ds(at, size)] = g
 
         for i, ref in enumerate((keep_ref, give_ref)):
-            ref[...] = out_ref[i]
+            ref[...] = out_ref[i].astype(ref.dtype)
 
     flops = 2 * lanes * head_dim * (5 * n_cache + 2 * n_group)
     return pl.pallas_call(
@@ -303,7 +303,7 @@
         + [pl.BlockSpec(memory_space=pl.ANY)] * 2
         + [pl.BlockSpec(memory_space=pltpu.VMEM)] * (len(group) + n_part),
         out_specs=[pl.BlockSpec(memory_space=pltpu.VMEM)] * 2,
-        out_shape=[jax.ShapeDtypeStruct((n_cache, head_dim), F32)] * 2,
+        out_shape=[jax.ShapeDtypeStruct((n_cache, head_dim), kind) for kind in (F32, BF16)],
         scratch_shapes=[
             pltpu.VMEM((2, n_cache, head_dim), F32),
             pltpu.VMEM((n_cache + n_group, lanes), F32),
@@ -321,7 +321,7 @@
             transcendentals=lanes * (n_cache + n_group),
         ),
         name="attend",
-    )(lengths, d_attn, *cache, *group, *[term for terms in partials for term in terms])
+    )(lengths, d_attn, *cache, *group, *[term for terms, _ in partials for term in terms])
 
 
 def make_on_device(n_dp, n_fsdp):
@@ -332,12 +332,11 @@
         head_dim = w_key.shape[1]
         q_width = w_query.shape[1]
         even = dp % 2 == 0
-        f_bits, d_bits = bits_down(n_fsdp), bits_down(n_dp)
+        d_bits = bits_down(n_dp)
 
         def from_owners(products):
             return [products[0]] + [swap(x, "fsdp", n_fsdp, k + 1) for k, x in enumerate(products[1:])]
 
-        cuts = [(0, q_width // 2), (q_width // 2, q_width // 2)]
         cuts = [(0, q_width // 2), (q_width // 2, q_width // 2)]
         sent, part = prepare(hidden, w_query, w_key, w_value, n_dp, n_fsdp)
         received = [swap(block, "fsdp", n_fsdp, k + 1) for k, block in enumerate(sent)]
@@ -347,49 +346,49 @@
         part_a, part_b = part[:cut], part[cut:]
         far_a, order = double(part_a[None], [0], "dp", n_dp, d_bits[0])
         cache = jnp.where(even, cache_keys, cache_values)[None]
-        cache, f_order = double(cache, [0], "fsdp", n_fsdp, f_bits[0])
+        cache, _ = double(cache, [0], "fsdp", n_fsdp, inner)
         cache, far_a, *received = together(cache, far_a, *received)
         far_b, _ = double(part_b[None], [0], "dp", n_dp, d_bits[0])
         far_a, d_order = finish(far_a, order, "dp", n_dp, d_bits[1:])
-        cache, f_order = double(cache, f_order, "fsdp", n_fsdp, f_bits[1])
-        cache, far_a[1] = together(cache, far_a[1])
+        cache = [cache] + [swap(cache, "fsdp", n_fsdp, k) for k in range(1, inner)]
+        far_a[1], far_b, *cache = together(far_a[1], far_b, *cache)
+        cache = jnp.concatenate(cache)
+        f_order = [o for k in range(inner) for o in (k, k ^ inner)]
+        cache = [cache, swap(cache, "dp", n_dp, 1)]
         kv, (at_a, wide_a), (at_b, wide_b) = 2 * head_dim, *cuts
         near_a = [(w_key, 0, head_dim), (w_value, 0, head_dim), (w_query, at_a, wide_a)]
         layout_a = [(0, 0, share, wide_a, 0, kv)]
         layout_a += [(share, i * kv, share // 2, kv, i * (share // 2), 0) for i in range(2)]
-        out_kv, out_a = multiply(
-            hidden, received, near_a, far_a, layout_a, d_order, n_fsdp, (kv, wide_a)
+        (out_a,) = multiply(
+            hidden, received, near_a, far_a, layout_a, d_order, n_fsdp, (kv + wide_a,)
         )
-        for bit in f_bits[2:]:
-            cache, f_order = double(cache, f_order, "fsdp", n_fsdp, bit)
-        far_b, cache, out_kv[0] = together(far_b, cache, out_kv[0])
+        far_b, cache[1], out_a[0] = together(far_b, cache[1], out_a[0])
         far_b, _ = finish(far_b, order, "dp", n_dp, d_bits[1:])
-        parts_kv = from_owners(out_kv)
         parts_a = from_owners(out_a)
-        own = functools.reduce(lambda a, b: a + b, parts_kv).astype(BF16)
-        far_b[1], own = together(far_b[1], own)
-        group, _ = double(own[None], [0], "fsdp", n_fsdp, inner)
         near_b, layout_b = [(w_query, at_b, wide_b)], [(0, 0, share, wide_b, 0, 0)]
         (out_b,) = multiply(
             hidden, received, near_b, far_b, layout_b, d_order, n_fsdp, (wide_b,)
         )
-        group, cache, *tied = together(group, cache, *out_b, *parts_a[1:])
-        out_b, parts_a[1:] = tied[:inner], tied[inner:]
         parts_b = from_owners(out_b)
-        cache = [cache, swap(cache, "dp", n_dp, 1)]
-        group, parts_b[1], cache[1] = together(group, parts_b[1], cache[1])
+        parts_b[0], parts_b[1], *parts_a = together(*parts_b[:2], *parts_a)
+        own = functools.reduce(lambda a, b: a + b, [x[:, :kv] for x in parts_a]).astype(BF16)
+        group, _ = double(own[None], [0], "fsdp", n_fsdp, inner)
+        group, *parts_b[2:] = together(group, *parts_b[2:])
         group = [group] + [swap(group, "fsdp", n_fsdp, k) for k in range(1, inner)]
-        g_order = [o for k in range(inner) for o in (k, k ^ inner)]
-        keep, give = attend(lengths, [parts_a, parts_b], d_attn, cache, group, g_order)
-
-        half = keep + swap(give, "dp", n_dp, 1)
+        partials = [(parts_a, kv), (parts_b, 0)]
+        keep, give = attend(lengths, partials, d_attn, cache, group, f_order)
+
+        half = keep + swap(give, "dp", n_dp, 1).astype(F32)
         size = half.shape[0] // n_fsdp
         mine = half[:size]
-        for slot in range(1, n_fsdp):
+        far = [slot for slot in range(n_fsdp) if f_order[slot] >= inner]
+        near = [slot for slot in range(1, n_fsdp) if f_order[slot] < inner]
+        for slot in far[:1] + near + far[:0:-1]:
             out = half[slot * size : (slot + 1) * size].astype(BF16)
             mine = mine + swap(out, "fsdp", n_fsdp, f_order[slot]).astype(F32)
         for bit in d_bits[:-1]:
-            mine = mine + swap(mine, "dp", n_dp, bit)
+            mine = mine.astype(BF16)
+            mine = mine.astype(F32) + swap(mine, "dp", n_dp, bit).astype(F32)
         other = swap(mine, "dp", n_dp, 1)
         return jnp.where(even, mine, other), jnp.where(even, other, mine)
 

time: 149 us -> 150 us (level)
  starting transfers between devices: 44.4 us -> 39.6 us
  waiting for transfers between devices: 73 us -> 76.3 us
  local copies, waits for them, and re-layouts: 0.73 us -> 2.9 us
    ppermute x35 -> x33, starting transfers between devices: 44.4 us -> 39.6 us  [swap(): return lax.ppermute(value, axis, [(i, i ^ bit) for i in range(size)])]
    ppermute x35 -> x33, waiting for transfers between devices: 73 us -> 76.3 us  [swap(): return lax.ppermute(value, axis, [(i, i ^ bit) for i in range(size)])]
    unnamed x42 -> x45, local copies, waits for them, and re-layouts: 0.66 us -> 2.81 us
  transfers between devices with their start and end apart: 35 -> 33, of which waited for: 23 -> 21; matrix products, arithmetic and copies ran while one was open for 1% -> 1% of each run, Pallas kernels for 7% -> 7%
where the time goes in v7:
time: 150 us; the launch traced here: 149 us
  waiting for transfers between devices  76.3 us (51%)
  starting transfers between devices  39.6 us (26%)
  Pallas kernels  26.2 us (17%)
  other arithmetic  3.36 us (2%)
  local copies, waits for them, and re-layouts  2.9 us (2%)
    ppermute x33, waiting for transfers between devices, swap(): return lax.ppermute(value, axis, [(i, i ^ bit) for i in range(size)])  76.3 us
    ppermute x33, starting transfers between devices, swap(): return lax.ppermute(value, axis, [(i, i ^ bit) for i in range(size)])  39.6 us
    pallas_call x1, Pallas kernels, attend(): pl.pallas_call(body, in_specs=[pl.BlockSpec(memory_space=pltpu.SMEM)] + [...  12.7 us
    pallas_call x2, Pallas kernels, multiply(): pl.pallas_call(body, in_specs=[pl.BlockSpec(memory_space=pl.ANY)] * (1 +...  10.4 us
    pallas_call x1, Pallas kernels, prepare(): pl.pallas_call(body, in_specs=[pl.BlockSpec(memory_space=pl.ANY)] * 4, ou...  3.08 us
  transfers between devices with their start and end apart: 33, of which 21 were waited for; matrix products, arithmetic and copies ran while one was open for 1% of the time, Pallas kernels for 7%

profile of v7, /device:TPU:0, one launch (start us, length us, event | category | flops | bytes accessed | tf_op | source)
XLA Modules:
  0.0 149.4 jit_solution(12024399928663714650)
XLA Ops:
  0.6 3.1 %prepare.1 = (bf16[128,2048]{1,0:T(8,128)(2,1)}, bf16[128,2048]{1,0:T(8,128)(2,1)}, bf16[128,2048]{1,0:T(8,128)(2,1)}, bf16[640,512]{1,0:T(8,128)(2,1)}) custom-call(bf16[128,8192]{1,0:T(8,128)(2,1)} %hidden_ref.5, bf16[1024,1024]{1,0:T(8,128)(2,1)} %rest_3_.3, bf16[1024,128]{1,0:T(8,128)(2,1)} %rest_3_.2, bf16[1024,128]{1,0:T(8,128)(2,1)} %rest_4_.1), custom_call_target="tpu_custom_call" | custom-call | bytes 4456448 | tf_op jit(solution)/shard_map/prepare/pallas_call | solution.py:83
  3.7 4.1 %collective-permute-start.1 = (bf16[640,512]{1,0:T(8,128)(2,1)}, bf16[640,512]{1,0:T(8,128)(2,1)S(1)}, u32[]{:S(2)}, u32[]{:S(2)}) collective-permute-start(bf16[640,512]{1,0:T(8,128)(2,1)} %get-tuple-element.39), channel_id=1, source_target_pairs={{0,4},{1,5},{2,6},{3,7},{4,0},{5,1},{6,2},{7,3},{8,12},{9,13},{10,... | collective-permute-start | bytes 1966088 | tf_op jit(solution)/shard_map/ppermute | solution.py:17
  11.3 25.6 %collective-permute-done.1 = bf16[640,512]{1,0:T(8,128)(2,1)S(1)} collective-permute-done((bf16[640,512]{1,0:T(8,128)(2,1)}, bf16[640,512]{1,0:T(8,128)(2,1)S(1)}, u32[]{:S(2)}, u32[]{:S(2)}) %collective-permute-start.1) | collective-permute-done | bytes 655392 | tf_op jit(solution)/shard_map/ppermute | solution.py:17
  38.7 7.3 %collective-permute-done = bf16[1,256,128]{2,1,0:T(8,128)(2,1)S(1)} collective-permute-done((bf16[1,256,128]{2,1,0:T(8,128)(2,1)S(1)}, bf16[1,256,128]{2,1,0:T(8,128)(2,1)S(1)}, u32[]{:S(2)}, u32[]{:S(2)}) %collective-permute-start) | collective-permute-done | bytes 65568 | tf_op jit(solution)/shard_map/ppermute | solution.py:17
  49.8 1.8 %collective-permute-start.10 = (bf16[2,256,128]{2,1,0:T(8,128)(2,1)S(1)}, bf16[2,256,128]{2,1,0:T(8,128)(2,1)S(1)}, u32[]{:S(2)}, u32[]{:S(2)}) collective-permute-start(bf16[2,256,128]{2,1,0:T(8,128)(2,1)S(1)} %pad_maximum_fusion.2), channel_id=1, source_target_pairs={{0,3},{1,2},{2,1},{3,0},{4,7},{5,6},{6,5},{7,4},{8,11},{9,10},{10,... | collective-permute-start | bytes 393224 | tf_op jit(solution)/shard_map/ppermute | solution.py:17
  53.3 3.7 %collective-permute-done.7 = bf16[1,256,512]{2,1,0:T(8,128)(2,1)S(1)} collective-permute-done((bf16[1,256,512]{2,1,0:T(8,128)(2,1)S(1)}, bf16[1,256,512]{2,1,0:T(8,128)(2,1)S(1)}, u32[]{:S(2)}, u32[]{:S(2)}) %collective-permute-start.7) | collective-permute-done | bytes 262176 | tf_op jit(solution)/shard_map/ppermute | solution.py:17
  57.1 2.1 %collective-permute-done.9 = bf16[2,256,128]{2,1,0:T(8,128)(2,1)S(1)} collective-permute-done((bf16[2,256,128]{2,1,0:T(8,128)(2,1)S(1)}, bf16[2,256,128]{2,1,0:T(8,128)(2,1)S(1)}, u32[]{:S(2)}, u32[]{:S(2)}) %collective-permute-start.9) | collective-permute-done | bytes 131104 | tf_op jit(solution)/shard_map/ppermute | solution.py:17
  60.1 5.9 %multiply.2 = (f32[128,768]{1,0:T(8,128)}, f32[128,768]{1,0:T(8,128)}, f32[128,768]{1,0:T(8,128)}, f32[128,768]{1,0:T(8,128)}) custom-call(bf16[128,8192]{1,0:T(8,128)(2,1)} %hidden_ref.5, bf16[128,2048]{1,0:T(8,128)(2,1)} %copy-done.2, bf16[128,2048]{1,0:T(8,128)(2,1)} %copy-done.3, bf16[128,2048]{1,0:T(8,128)(2,1)} %copy-done.4, ...), custom_call_target="tpu_custom_call" | custom-call | flops 1610612736 | bytes 6815744 | tf_op jit(solution)/shard_map/multiply/pallas_call | solution.py:154
  70.4 4.6 %multiply.3 = (f32[128,512]{1,0:T(8,128)}, f32[128,512]{1,0:T(8,128)}, f32[128,512]{1,0:T(8,128)}, f32[128,512]{1,0:T(8,128)}) custom-call(bf16[128,8192]{1,0:T(8,128)(2,1)} %hidden_ref.5, bf16[128,2048]{1,0:T(8,128)(2,1)} %copy-done.2, bf16[128,2048]{1,0:T(8,128)(2,1)} %copy-done.3, bf16[128,2048]{1,0:T(8,128)(2,1)} %copy-done.4, ...), custom_call_target="tpu_custom_call" | custom-call | flops 1073741824 | bytes 5242880 | tf_op jit(solution)/shard_map/multiply/pallas_call | solution.py:154
  78.0 1.8 %collective-permute-start.19 = (f32[128,512]{1,0:T(8,128)}, f32[128,512]{1,0:T(8,128)S(1)}, u32[]{:S(2)}, u32[]{:S(2)}) collective-permute-start(f32[128,512]{1,0:T(8,128)} %get-tuple-element.68), channel_id=1, source_target_pairs={{0,3},{1,2},{2,1},{3,0},{4,7},{5,6},{6,5},{7,4},{8,11},{9,10},{10,... | collective-permute-start | bytes 786440 | tf_op jit(solution)/shard_map/ppermute | solution.py:17
  79.8 8.4 %collective-permute-done.16.rest_9_ = f32[128,768]{1,0:T(8,128)S(1)} collective-permute-done((f32[128,768]{1,0:T(8,128)}, f32[128,768]{1,0:T(8,128)S(1)}, u32[]{:S(2)}, u32[]{:S(2)}) %collective-permute-start.16) | collective-permute-done | bytes 393248 | tf_op jit(solution)/shard_map/ppermute | solution.py:17
  88.2 3.6 %collective-permute-done.13.rest_11_ = f32[128,512]{1,0:T(8,128)S(1)} collective-permute-done((f32[128,512]{1,0:T(8,128)}, f32[128,512]{1,0:T(8,128)S(1)}, u32[]{:S(2)}, u32[]{:S(2)}) %collective-permute-start.13) | collective-permute-done | bytes 262176 | tf_op jit(solution)/shard_map/ppermute | solution.py:17
  92.9 2.4 %collective-permute-start.17 = (bf16[1,128,256]{2,1,0:T(8,128)(2,1)S(1)}, bf16[1,128,256]{2,1,0:T(8,128)(2,1)S(1)}, u32[]{:S(2)}, u32[]{:S(2)}) collective-permute-start(bf16[1,128,256]{2,1,0:T(8,128)(2,1)S(1)} %fusion.7), channel_id=1, source_target_pairs={{0,4},{1,5},{2,6},{3,7},{4,0},{5,1},{6,2},{7,3},{8,12},{9,13},{10,... | collective-permute-start | bytes 196616 | tf_op jit(solution)/shard_map/ppermute | solution.py:17
  95.3 3.1 %collective-permute-done.17 = bf16[1,128,256]{2,1,0:T(8,128)(2,1)S(1)} collective-permute-done((bf16[1,128,256]{2,1,0:T(8,128)(2,1)S(1)}, bf16[1,128,256]{2,1,0:T(8,128)(2,1)S(1)}, u32[]{:S(2)}, u32[]{:S(2)}) %collective-permute-start.17) | collective-permute-done | bytes 65568 | tf_op jit(solution)/shard_map/ppermute | solution.py:17
  100.1 2.6 %collective-permute-start.22 = (bf16[2,128,256]{2,1,0:T(8,128)(2,1)S(1)}, bf16[2,128,256]{2,1,0:T(8,128)(2,1)S(1)}, u32[]{:S(2)}, u32[]{:S(2)}) collective-permute-start(bf16[2,128,256]{2,1,0:T(8,128)(2,1)S(1)} %pad_maximum_fusion.3.rest_2_), channel_id=1, source_target_pairs={{0,3},{1,2},{2,1},{3,0},{4,7},{5,6},{6,5},{7,4},{8,11},{9,10},{10,... | collective-permute-start | bytes 393224 | tf_op jit(solution)/shard_map/ppermute | solution.py:17
  104.1 2.4 %collective-permute-done.22.rest_5_ = bf16[2,128,256]{2,1,0:T(8,128)(2,1)S(1)} collective-permute-done((bf16[2,128,256]{2,1,0:T(8,128)(2,1)S(1)}, bf16[2,128,256]{2,1,0:T(8,128)(2,1)S(1)}, u32[]{:S(2)}, u32[]{:S(2)}) %collective-permute-start.22) | collective-permute-done | bytes 131104 | tf_op jit(solution)/shard_map/ppermute | solution.py:17
  106.5 2.3 %collective-permute-done.21.rest_4_ = bf16[2,128,256]{2,1,0:T(8,128)(2,1)S(1)} collective-permute-done((bf16[2,128,256]{2,1,0:T(8,128)(2,1)S(1)}, bf16[2,128,256]{2,1,0:T(8,128)(2,1)S(1)}, u32[]{:S(2)}, u32[]{:S(2)}) %collective-permute-start.21) | collective-permute-done | bytes 131104 | tf_op jit(solution)/shard_map/ppermute | solution.py:17
  110.1 12.7 %attend.1 = (f32[2048,128]{1,0:T(8,128)}, bf16[2048,128]{1,0:T(8,128)(2,1)}) custom-call(s32[1,4]{1,0:T(1,128)} %len_ref.1, bf16[128,1024]{1,0:T(8,128)(2,1)} %d_ref.1, bf16[8,256,128]{2,1,0:T(8,128)(2,1)} %copy-done.13, bf16[8,256,128]{2,1,0:T(8,128)(2,1)} %copy-done.14, bf16[2,128,256]{2,1,0:T(8,128)(2,1)} %copy-done.7, bf16[2,128,256]{2,1,0:T(8,128)(2,1)} %copy-done.20, ...), custom_call_target="tpu_custom_call" | custom-call | flops 3221225472 | bytes 3145728 | tf_op jit(solution)/shard_map/attend/pallas_call | solution.py:299
  122.8 2.1 %collective-permute-done.23 = bf16[2048,128]{1,0:T(8,128)(2,1)S(1)} collective-permute-done((bf16[2048,128]{1,0:T(8,128)(2,1)}, bf16[2048,128]{1,0:T(8,128)(2,1)S(1)}, u32[]{:S(2)}, u32[]{:S(2)}) %collective-permute-start.23) | collective-permute-done | bytes 524320 | tf_op jit(solution)/shard_map/ppermute | solution.py:17
  126.3 1.7 %collective-permute-start.24 = (bf16[256,128]{1,0:T(8,128)(2,1)S(1)}, bf16[256,128]{1,0:T(8,128)(2,1)S(1)}, u32[]{:S(2)}, u32[]{:S(2)}) collective-permute-start(bf16[256,128]{1,0:T(8,128)(2,1)S(1)} %get-tuple-element.78), channel_id=1, source_target_pairs={{0,4},{1,5},{2,6},{3,7},{4,0},{5,1},{6,2},{7,3},{8,12},{9,13},{10,... | collective-permute-start | bytes 196616 | tf_op jit(solution)/shard_map/ppermute | solution.py:17
  128.0 1.7 %collective-permute-start.30 = (bf16[256,128]{1,0:T(8,128)(2,1)S(1)}, bf16[256,128]{1,0:T(8,128)(2,1)S(1)}, u32[]{:S(2)}, u32[]{:S(2)}) collective-permute-start(bf16[256,128]{1,0:T(8,128)(2,1)S(1)} %get-tuple-element.79), channel_id=1, source_target_pairs={{0,5},{1,4},{2,7},{3,6},{4,1},{5,0},{6,3},{7,2},{8,13},{9,12},{10,... | collective-permute-start | bytes 196616 | tf_op jit(solution)/shard_map/ppermute | solution.py:17
  129.7 3.3 %collective-permute-start.29 = (bf16[256,128]{1,0:T(8,128)(2,1)S(1)}, bf16[256,128]{1,0:T(8,128)(2,1)S(1)}, u32[]{:S(2)}, u32[]{:S(2)}) collective-permute-start(bf16[256,128]{1,0:T(8,128)(2,1)S(1)} %get-tuple-element.80), channel_id=1, source_target_pairs={{0,6},{1,7},{2,4},{3,5},{4,2},{5,3},{6,0},{7,1},{8,14},{9,15},{10,... | collective-permute-start | bytes 196616 | tf_op jit(solution)/shard_map/ppermute | solution.py:17
  136.4 2.1 %collective-permute-done.30 = bf16[256,128]{1,0:T(8,128)(2,1)S(1)} collective-permute-done((bf16[256,128]{1,0:T(8,128)(2,1)S(1)}, bf16[256,128]{1,0:T(8,128)(2,1)S(1)}, u32[]{:S(2)}, u32[]{:S(2)}) %collective-permute-start.30) | collective-permute-done | bytes 65568 | tf_op jit(solution)/shard_map/ppermute | solution.py:17
  143.5 3.7 %collective-permute-done.31 = bf16[256,128]{1,0:T(8,128)(2,1)S(1)} collective-permute-done((bf16[256,128]{1,0:T(8,128)(2,1)S(1)}, bf16[256,128]{1,0:T(8,128)(2,1)S(1)}, u32[]{:S(2)}, u32[]{:S(2)}) %collective-permute-start.31) | collective-permute-done | bytes 65568 | tf_op jit(solution)/shard_map/ppermute | solution.py:17
  (105 shorter events, 36.3 us)
Async XLA Ops:
  3.7 33.2 %collective-permute-start.1 = (bf16[640,512]{1,0:T(8,128)(2,1)}, bf16[640,512]{1,0:T(8,128)(2,1)S(1)}, u32[]{:S(2)}, u32[]{:S(2)}) collective-permute-start(bf16[640,512]{1,0:T(8,128)(2,1)} %get-tuple-element.39), channel_id=1, source_target_pairs={{0,4},{1,5},{2,6},{3,7},{4,0},{5,1},{6,2},{7,3},{8,12},{9,13},{10,... | collective-permute-start | bytes 1966088 | tf_op jit(solution)/shard_map/ppermute | solution.py:17
  7.8 39.5 %collective-permute-start.3 = (bf16[128,2048]{1,0:T(8,128)(2,1)}, bf16[128,2048]{1,0:T(8,128)(2,1)S(1)}, u32[]{:S(2)}, u32[]{:S(2)}) collective-permute-start(bf16[128,2048]{1,0:T(8,128)(2,1)} %get-tuple-element.40), channel_id=1, source_target_pairs={{0,1},{1,0},{2,3},{3,2},{4,5},{5,4},{6,7},{7,6},{8,9},{9,8},{10,11... | collective-permute-start | bytes 1572872 | tf_op jit(solution)/shard_map/ppermute | solution.py:17
  9.4 38.0 %collective-permute-start.4 = (bf16[128,2048]{1,0:T(8,128)(2,1)}, bf16[128,2048]{1,0:T(8,128)(2,1)S(1)}, u32[]{:S(2)}, u32[]{:S(2)}) collective-permute-start(bf16[128,2048]{1,0:T(8,128)(2,1)} %get-tuple-element.41), channel_id=1, source_target_pairs={{0,2},{1,3},{2,0},{3,1},{4,6},{5,7},{6,4},{7,5},{8,10},{9,11},{10,... | collective-permute-start | bytes 1572872 | tf_op jit(solution)/shard_map/ppermute | solution.py:17
  10.9 37.2 %collective-permute-start.5 = (bf16[128,2048]{1,0:T(8,128)(2,1)}, bf16[128,2048]{1,0:T(8,128)(2,1)S(1)}, u32[]{:S(2)}, u32[]{:S(2)}) collective-permute-start(bf16[128,2048]{1,0:T(8,128)(2,1)} %get-tuple-element.42), channel_id=1, source_target_pairs={{0,3},{1,2},{2,1},{3,0},{4,7},{5,6},{6,5},{7,4},{8,11},{9,10},{10,... | collective-permute-start | bytes 1572872 | tf_op jit(solution)/shard_map/ppermute | solution.py:17
  37.0 10.3 %collective-permute-start.2 = (bf16[1,384,512]{2,1,0:T(8,128)(2,1)S(1)}, bf16[1,384,512]{2,1,0:T(8,128)(2,1)S(1)}, u32[]{:S(2)}, u32[]{:S(2)}) collective-permute-start(bf16[1,384,512]{2,1,0:T(8,128)(2,1)S(1)} %slice_bitcast_fusion), channel_id=1, source_target_pairs={{0,16},{8,24},{16,0},{24,8},{1,17},{9,25},{17,1},{25,9},{2,18},{10... | collective-permute-start | bytes 1179656 | tf_op jit(solution)/shard_map/ppermute | solution.py:17
  38.6 7.4 %collective-permute-start = (bf16[1,256,128]{2,1,0:T(8,128)(2,1)S(1)}, bf16[1,256,128]{2,1,0:T(8,128)(2,1)S(1)}, u32[]{:S(2)}, u32[]{:S(2)}) collective-permute-start(bf16[1,256,128]{2,1,0:T(8,128)(2,1)S(1)} %select_bitcast_fusion), channel_id=1, source_target_pairs={{0,4},{1,5},{2,6},{3,7},{4,0},{5,1},{6,2},{7,3},{8,12},{9,13},{10,... | collective-permute-start | bytes 196616 | tf_op jit(solution)/shard_map/ppermute | solution.py:17
  48.2 11.0 %collective-permute-start.6 = (bf16[2,384,512]{2,1,0:T(8,128)(2,1)S(1)}, bf16[2,384,512]{2,1,0:T(8,128)(2,1)S(1)}, u32[]{:S(2)}, u32[]{:S(2)}) collective-permute-start(bf16[2,384,512]{2,1,0:T(8,128)(2,1)S(1)} %pad_maximum_fusion.rest_6_), channel_id=1, source_target_pairs={{0,8},{8,0},{16,24},{24,16},{1,9},{9,1},{17,25},{25,17},{2,10},{10... | collective-permute-start | bytes 2359304 | tf_op jit(solution)/shard_map/ppermute | solution.py:17
  48.2 8.8 %collective-permute-start.7 = (bf16[1,256,512]{2,1,0:T(8,128)(2,1)S(1)}, bf16[1,256,512]{2,1,0:T(8,128)(2,1)S(1)}, u32[]{:S(2)}, u32[]{:S(2)}) collective-permute-start(bf16[1,256,512]{2,1,0:T(8,128)(2,1)S(1)} %slice_bitcast_fusion.1), channel_id=1, source_target_pairs={{0,16},{8,24},{16,0},{24,8},{1,17},{9,25},{17,1},{25,9},{2,18},{10... | collective-permute-start | bytes 786440 | tf_op jit(solution)/shard_map/ppermute | solution.py:17
  49.8 7.3 %collective-permute-start.10 = (bf16[2,256,128]{2,1,0:T(8,128)(2,1)S(1)}, bf16[2,256,128]{2,1,0:T(8,128)(2,1)S(1)}, u32[]{:S(2)}, u32[]{:S(2)}) collective-permute-start(bf16[2,256,128]{2,1,0:T(8,128)(2,1)S(1)} %pad_maximum_fusion.2), channel_id=1, source_target_pairs={{0,3},{1,2},{2,1},{3,0},{4,7},{5,6},{6,5},{7,4},{8,11},{9,10},{10,... | collective-permute-start | bytes 393224 | tf_op jit(solution)/shard_map/ppermute | solution.py:17
  51.6 7.6 %collective-permute-start.9 = (bf16[2,256,128]{2,1,0:T(8,128)(2,1)S(1)}, bf16[2,256,128]{2,1,0:T(8,128)(2,1)S(1)}, u32[]{:S(2)}, u32[]{:S(2)}) collective-permute-start(bf16[2,256,128]{2,1,0:T(8,128)(2,1)S(1)} %pad_maximum_fusion.2), channel_id=1, source_target_pairs={{0,2},{1,3},{2,0},{3,1},{4,6},{5,7},{6,4},{7,5},{8,10},{9,11},{10,... | collective-permute-start | bytes 393224 | tf_op jit(solution)/shard_map/ppermute | solution.py:17
  52.8 6.4 %collective-permute-start.8 = (bf16[2,256,128]{2,1,0:T(8,128)(2,1)S(1)}, bf16[2,256,128]{2,1,0:T(8,128)(2,1)S(1)}, u32[]{:S(2)}, u32[]{:S(2)}) collective-permute-start(bf16[2,256,128]{2,1,0:T(8,128)(2,1)S(1)} %pad_maximum_fusion.2), channel_id=1, source_target_pairs={{0,1},{1,0},{2,3},{3,2},{4,5},{5,4},{6,7},{7,6},{8,9},{9,8},{10,11... | collective-permute-start | bytes 393224 | tf_op jit(solution)/shard_map/ppermute | solution.py:17
  59.3 6.6 %collective-permute-start.11 = (bf16[8,256,128]{2,1,0:T(8,128)(2,1)S(1)}, bf16[8,256,128]{2,1,0:T(8,128)(2,1)S(1)}, u32[]{:S(2)}, u32[]{:S(2)}) collective-permute-start(bf16[8,256,128]{2,1,0:T(8,128)(2,1)S(1)} %constant_dynamic-update-slice_fusion.rest_0_), channel_id=1, source_target_pairs={{0,8},{8,0},{16,24},{24,16},{1,9},{9,1},{17,25},{25,17},{2,10},{10... | collective-permute-start | bytes 1572872 | tf_op jit(solution)/shard_map/ppermute | solution.py:17
  66.1 12.0 %collective-permute-start.14 = (f32[128,768]{1,0:T(8,128)}, f32[128,768]{1,0:T(8,128)S(1)}, u32[]{:S(2)}, u32[]{:S(2)}) collective-permute-start(f32[128,768]{1,0:T(8,128)} %get-tuple-element.60), channel_id=1, source_target_pairs={{0,1},{1,0},{2,3},{3,2},{4,5},{5,4},{6,7},{7,6},{8,9},{9,8},{10,11... | collective-permute-start | bytes 1179656 | tf_op jit(solution)/shard_map/ppermute | solution.py:17
  67.6 12.2 %collective-permute-start.15 = (f32[128,768]{1,0:T(8,128)}, f32[128,768]{1,0:T(8,128)S(1)}, u32[]{:S(2)}, u32[]{:S(2)}) collective-permute-start(f32[128,768]{1,0:T(8,128)} %get-tuple-element.61), channel_id=1, source_target_pairs={{0,2},{1,3},{2,0},{3,1},{4,6},{5,7},{6,4},{7,5},{8,10},{9,11},{10,... | collective-permute-start | bytes 1179656 | tf_op jit(solution)/shard_map/ppermute | solution.py:17
  68.4 19.8 %collective-permute-start.16 = (f32[128,768]{1,0:T(8,128)}, f32[128,768]{1,0:T(8,128)S(1)}, u32[]{:S(2)}, u32[]{:S(2)}) collective-permute-start(f32[128,768]{1,0:T(8,128)} %get-tuple-element.62), channel_id=1, source_target_pairs={{0,3},{1,2},{2,1},{3,0},{4,7},{5,6},{6,5},{7,4},{8,11},{9,10},{10,... | collective-permute-start | bytes 1179656 | tf_op jit(solution)/shard_map/ppermute | solution.py:17
  75.0 16.8 %collective-permute-start.13 = (f32[128,512]{1,0:T(8,128)}, f32[128,512]{1,0:T(8,128)S(1)}, u32[]{:S(2)}, u32[]{:S(2)}) collective-permute-start(f32[128,512]{1,0:T(8,128)} %get-tuple-element.58), channel_id=1, source_target_pairs={{0,1},{1,0},{2,3},{3,2},{4,5},{5,4},{6,7},{7,6},{8,9},{9,8},{10,11... | collective-permute-start | bytes 786440 | tf_op jit(solution)/shard_map/ppermute | solution.py:17
  76.5 22.0 %collective-permute-start.18 = (f32[128,512]{1,0:T(8,128)}, f32[128,512]{1,0:T(8,128)S(1)}, u32[]{:S(2)}, u32[]{:S(2)}) collective-permute-start(f32[128,512]{1,0:T(8,128)} %get-tuple-element.67), channel_id=1, source_target_pairs={{0,2},{1,3},{2,0},{3,1},{4,6},{5,7},{6,4},{7,5},{8,10},{9,11},{10,... | collective-permute-start | bytes 786440 | tf_op jit(solution)/shard_map/ppermute | solution.py:17
  78.0 22.1 %collective-permute-start.19 = (f32[128,512]{1,0:T(8,128)}, f32[128,512]{1,0:T(8,128)S(1)}, u32[]{:S(2)}, u32[]{:S(2)}) collective-permute-start(f32[128,512]{1,0:T(8,128)} %get-tuple-element.68), channel_id=1, source_target_pairs={{0,3},{1,2},{2,1},{3,0},{4,7},{5,6},{6,5},{7,4},{8,11},{9,10},{10,... | collective-permute-start | bytes 786440 | tf_op jit(solution)/shard_map/ppermute | solution.py:17
  126.3 8.6 %collective-permute-start.24 = (bf16[256,128]{1,0:T(8,128)(2,1)S(1)}, bf16[256,128]{1,0:T(8,128)(2,1)S(1)}, u32[]{:S(2)}, u32[]{:S(2)}) collective-permute-start(bf16[256,128]{1,0:T(8,128)(2,1)S(1)} %get-tuple-element.78), channel_id=1, source_target_pairs={{0,4},{1,5},{2,6},{3,7},{4,0},{5,1},{6,2},{7,3},{8,12},{9,13},{10,... | collective-permute-start | bytes 196616 | tf_op jit(solution)/shard_map/ppermute | solution.py:17
  128.0 10.6 %collective-permute-start.30 = (bf16[256,128]{1,0:T(8,128)(2,1)S(1)}, bf16[256,128]{1,0:T(8,128)(2,1)S(1)}, u32[]{:S(2)}, u32[]{:S(2)}) collective-permute-start(bf16[256,128]{1,0:T(8,128)(2,1)S(1)} %get-tuple-element.79), channel_id=1, source_target_pairs={{0,5},{1,4},{2,7},{3,6},{4,1},{5,0},{6,3},{7,2},{8,13},{9,12},{10,... | collective-permute-start | bytes 196616 | tf_op jit(solution)/shard_map/ppermute | solution.py:17
  129.7 9.1 %collective-permute-start.29 = (bf16[256,128]{1,0:T(8,128)(2,1)S(1)}, bf16[256,128]{1,0:T(8,128)(2,1)S(1)}, u32[]{:S(2)}, u32[]{:S(2)}) collective-permute-start(bf16[256,128]{1,0:T(8,128)(2,1)S(1)} %get-tuple-element.80), channel_id=1, source_target_pairs={{0,6},{1,7},{2,4},{3,5},{4,2},{5,3},{6,0},{7,1},{8,14},{9,15},{10,... | collective-permute-start | bytes 196616 | tf_op jit(solution)/shard_map/ppermute | solution.py:17
  132.9 7.4 %collective-permute-start.28 = (bf16[256,128]{1,0:T(8,128)(2,1)S(1)}, bf16[256,128]{1,0:T(8,128)(2,1)S(1)}, u32[]{:S(2)}, u32[]{:S(2)}) collective-permute-start(bf16[256,128]{1,0:T(8,128)(2,1)S(1)} %get-tuple-element.81), channel_id=1, source_target_pairs={{0,7},{1,6},{2,5},{3,4},{4,3},{5,2},{6,1},{7,0},{8,15},{9,14},{10,... | collective-permute-start | bytes 196616 | tf_op jit(solution)/shard_map/ppermute | solution.py:17
  134.0 6.6 %collective-permute-start.27 = (bf16[256,128]{1,0:T(8,128)(2,1)S(1)}, bf16[256,128]{1,0:T(8,128)(2,1)S(1)}, u32[]{:S(2)}, u32[]{:S(2)}) collective-permute-start(bf16[256,128]{1,0:T(8,128)(2,1)S(1)} %get-tuple-element.82), channel_id=1, source_target_pairs={{0,3},{1,2},{2,1},{3,0},{4,7},{5,6},{6,5},{7,4},{8,11},{9,10},{10,... | collective-permute-start | bytes 196616 | tf_op jit(solution)/shard_map/ppermute | solution.py:17
  134.9 6.5 %collective-permute-start.26 = (bf16[256,128]{1,0:T(8,128)(2,1)S(1)}, bf16[256,128]{1,0:T(8,128)(2,1)S(1)}, u32[]{:S(2)}, u32[]{:S(2)}) collective-permute-start(bf16[256,128]{1,0:T(8,128)(2,1)S(1)} %get-tuple-element.83), channel_id=1, source_target_pairs={{0,2},{1,3},{2,0},{3,1},{4,6},{5,7},{6,4},{7,5},{8,10},{9,11},{10,... | collective-permute-start | bytes 196616 | tf_op jit(solution)/shard_map/ppermute | solution.py:17
  (30 other events, 353.1 us)

commit v8 on v4

--- a/solution.py
+++ b/solution.py
@@ -292,7 +292,8 @@
             out_ref[odd, pl.ds(at, size)] = g
 
         for i, ref in enumerate((keep_ref, give_ref)):
-            ref[...] = sum_refs[i][...] + out_ref[i] if n_sum else out_ref[i]
+            value = sum_refs[i][...] + out_ref[i] if n_sum else out_ref[i]
+            ref[...] = value.astype(ref.dtype)
 
     flops = 2 * lanes * head_dim * (5 * n_cache + 2 * n_group)
     return pl.pallas_call(
@@ -302,7 +303,10 @@
         + [pl.BlockSpec(memory_space=pl.ANY)] * 2
         + [pl.BlockSpec(memory_space=pltpu.VMEM)] * (len(group) + n_part + n_sum),
         out_specs=[pl.BlockSpec(memory_space=pltpu.VMEM)] * 2,
-        out_shape=[jax.ShapeDtypeStruct((n_cache, head_dim), F32)] * 2,
+        out_shape=[
+            jax.ShapeDtypeStruct((n_cache, head_dim), F32),
+            jax.ShapeDtypeStruct((n_cache, head_dim), BF16 if n_sum else F32),
+        ],
         scratch_shapes=[
             pltpu.VMEM((2, n_cache, head_dim), F32),
             pltpu.VMEM((n_cache + n_group, lanes), F32),
@@ -336,7 +340,6 @@
         def from_owners(products):
             return [products[0]] + [swap(x, "fsdp", n_fsdp, k + 1) for k, x in enumerate(products[1:])]
 
-        cuts = [(0, q_width // 2), (q_width // 2, q_width // 2)]
         cuts = [(0, q_width // 2), (q_width // 2, q_width // 2)]
         sent, part = prepare(hidden, w_query, w_key, w_value, n_dp, n_fsdp)
         received = [swap(block, "fsdp", n_fsdp, k + 1) for k, block in enumerate(sent)]
@@ -382,14 +385,17 @@
         sums = attend(lengths, parts_a, d_attn, 0, cache, group, g_order, ())
         keep, give = attend(lengths, parts_b, d_attn, first, cache, group, g_order, sums)
 
-        half = keep + swap(give, "dp", n_dp, 1)
+        half = keep + swap(give, "dp", n_dp, 1).astype(F32)
         size = half.shape[0] // n_fsdp
         mine = half[:size]
-        for slot in range(1, n_fsdp):
+        far = [slot for slot in range(n_fsdp) if f_order[slot] >= inner]
+        near = [slot for slot in range(1, n_fsdp) if f_order[slot] < inner]
+        for slot in far[:1] + near + far[:0:-1]:
             out = half[slot * size : (slot + 1) * size].astype(BF16)
             mine = mine + swap(out, "fsdp", n_fsdp, f_order[slot]).astype(F32)
         for bit in d_bits[:-1]:
-            mine = mine + swap(mine, "dp", n_dp, bit)
+            mine = mine.astype(BF16)
+            mine = mine.astype(F32) + swap(mine, "dp", n_dp, bit).astype(F32)
         other = swap(mine, "dp", n_dp, 1)
         return jnp.where(even, mine, other), jnp.where(even, other, mine)
 

time: 146 us -> 145 us (level)
  transfers between devices with their start and end apart: 35 -> 35, of which waited for: 18 -> 20; matrix products, arithmetic and copies ran while one was open for 1% -> 1% of each run, Pallas kernels for 13% -> 13%
where the time goes in v8:
time: 145 us; the launch traced here: 144 us
  waiting for transfers between devices  60.6 us (42%)
  starting transfers between devices  46.2 us (32%)
  Pallas kernels  31.3 us (22%)
  other arithmetic  3.35 us (2%)
  local copies, waits for them, and re-layouts  1.79 us (1%)
    ppermute x35, waiting for transfers between devices, swap(): return lax.ppermute(value, axis, [(i, i ^ bit) for i in range(size)])  60.6 us
    ppermute x35, starting transfers between devices, swap(): return lax.ppermute(value, axis, [(i, i ^ bit) for i in range(size)])  46.2 us
    pallas_call x2, Pallas kernels, attend(): pl.pallas_call(body, in_specs=[pl.BlockSpec(memory_space=pltpu.SMEM)] + [...  17.8 us
    pallas_call x2, Pallas kernels, multiply(): pl.pallas_call(body, in_specs=[pl.BlockSpec(memory_space=pl.ANY)] * (1 +...  10.4 us
    pallas_call x1, Pallas kernels, prepare(): pl.pallas_call(body, in_specs=[pl.BlockSpec(memory_space=pl.ANY)] * 4, ou...  3.12 us
  transfers between devices with their start and end apart: 35, of which 20 were waited for; matrix products, arithmetic and copies ran while one was open for 1% of the time, Pallas kernels for 13%

profile of v8, /device:TPU:0, one launch (start us, length us, event | category | flops | bytes accessed | tf_op | source)
XLA Modules:
  0.0 144.4 jit_solution(14315982079075371233)
XLA Ops:
  0.6 3.1 %prepare.1 = (bf16[128,2048]{1,0:T(8,128)(2,1)}, bf16[128,2048]{1,0:T(8,128)(2,1)}, bf16[128,2048]{1,0:T(8,128)(2,1)}, bf16[640,512]{1,0:T(8,128)(2,1)}) custom-call(bf16[128,8192]{1,0:T(8,128)(2,1)} %hidden_ref.5, bf16[1024,1024]{1,0:T(8,128)(2,1)} %rest_3_.3, bf16[1024,128]{1,0:T(8,128)(2,1)} %rest_3_.2, bf16[1024,128]{1,0:T(8,128)(2,1)} %rest_4_.1), custom_call_target="tpu_custom_call" | custom-call | bytes 4456448 | tf_op jit(solution)/shard_map/prepare/pallas_call | solution.py:83
  3.8 4.1 %collective-permute-start = (bf16[640,512]{1,0:T(8,128)(2,1)}, bf16[640,512]{1,0:T(8,128)(2,1)S(1)}, u32[]{:S(2)}, u32[]{:S(2)}) collective-permute-start(bf16[640,512]{1,0:T(8,128)(2,1)} %get-tuple-element.43), channel_id=1, source_target_pairs={{0,4},{1,5},{2,6},{3,7},{4,0},{5,1},{6,2},{7,3},{8,12},{9,13},{10,... | collective-permute-start | bytes 1966088 | tf_op jit(solution)/shard_map/ppermute | solution.py:17
  11.4 25.6 %collective-permute-done = bf16[640,512]{1,0:T(8,128)(2,1)S(1)} collective-permute-done((bf16[640,512]{1,0:T(8,128)(2,1)}, bf16[640,512]{1,0:T(8,128)(2,1)S(1)}, u32[]{:S(2)}, u32[]{:S(2)}) %collective-permute-start) | collective-permute-done | bytes 655392 | tf_op jit(solution)/shard_map/ppermute | solution.py:17
  37.0 1.6 %collective-permute-start.3 = (bf16[1,384,512]{2,1,0:T(8,128)(2,1)S(1)}, bf16[1,384,512]{2,1,0:T(8,128)(2,1)S(1)}, u32[]{:S(2)}, u32[]{:S(2)}) collective-permute-start(bf16[1,384,512]{2,1,0:T(8,128)(2,1)S(1)} %slice_bitcast_fusion), channel_id=1, source_target_pairs={{0,16},{8,24},{16,0},{24,8},{1,17},{9,25},{17,1},{25,9},{2,18},{10... | collective-permute-start | bytes 1179656 | tf_op jit(solution)/shard_map/ppermute | solution.py:17
  38.7 7.3 %collective-permute-done.2 = bf16[1,256,128]{2,1,0:T(8,128)(2,1)S(1)} collective-permute-done((bf16[1,256,128]{2,1,0:T(8,128)(2,1)S(1)}, bf16[1,256,128]{2,1,0:T(8,128)(2,1)S(1)}, u32[]{:S(2)}, u32[]{:S(2)}) %collective-permute-start.2) | collective-permute-done | bytes 65568 | tf_op jit(solution)/shard_map/ppermute | solution.py:17
  50.7 4.8 %collective-permute-done.7 = bf16[2,256,128]{2,1,0:T(8,128)(2,1)S(1)} collective-permute-done((bf16[2,256,128]{2,1,0:T(8,128)(2,1)S(1)}, bf16[2,256,128]{2,1,0:T(8,128)(2,1)S(1)}, u32[]{:S(2)}, u32[]{:S(2)}) %collective-permute-start.7) | collective-permute-done | bytes 131104 | tf_op jit(solution)/shard_map/ppermute | solution.py:17
  55.5 1.6 %collective-permute-start.9 = (bf16[4,256,128]{2,1,0:T(8,128)(2,1)S(1)}, bf16[4,256,128]{2,1,0:T(8,128)(2,1)S(1)}, u32[]{:S(2)}, u32[]{:S(2)}) collective-permute-start(bf16[4,256,128]{2,1,0:T(8,128)(2,1)S(1)} %pad_maximum_fusion.3), channel_id=1, source_target_pairs={{0,1},{1,0},{2,3},{3,2},{4,5},{5,4},{6,7},{7,6},{8,9},{9,8},{10,11... | collective-permute-start | bytes 786440 | tf_op jit(solution)/shard_map/ppermute | solution.py:17
  57.2 5.9 %multiply.2 = (f32[128,256]{1,0:T(8,128)}, f32[128,256]{1,0:T(8,128)}, f32[128,256]{1,0:T(8,128)}, f32[128,256]{1,0:T(8,128)}, f32[128,512]{1,0:T(8,128)}, /*ind...) custom-call(bf16[128,8192]{1,0:T(8,128)(2,1)} %hidden_ref.5, bf16[128,2048]{1,0:T(8,128)(2,1)} %copy-done.2, ...), custom_call_target="tpu_custom_call" | custom-call | flops 1610612736 | bytes 6815744 | tf_op jit(solution)/shard_map/multiply/pallas_call | solution.py:154
  75.0 2.8 %collective-permute-start.14 = (bf16[1,128,256]{2,1,0:T(8,128)(2,1)S(1)}, bf16[1,128,256]{2,1,0:T(8,128)(2,1)S(1)}, u32[]{:S(2)}, u32[]{:S(2)}) collective-permute-start(bf16[1,128,256]{2,1,0:T(8,128)(2,1)S(1)} %bitcast.7), channel_id=1, source_target_pairs={{0,4},{1,5},{2,6},{3,7},{4,0},{5,1},{6,2},{7,3},{8,12},{9,13},{10,... | collective-permute-start | bytes 196616 | tf_op jit(solution)/shard_map/ppermute | solution.py:17
  77.8 4.6 %multiply.3 = (f32[128,512]{1,0:T(8,128)}, f32[128,512]{1,0:T(8,128)}, f32[128,512]{1,0:T(8,128)}, f32[128,512]{1,0:T(8,128)}) custom-call(bf16[128,8192]{1,0:T(8,128)(2,1)} %hidden_ref.5, bf16[128,2048]{1,0:T(8,128)(2,1)} %copy-done.2, bf16[128,2048]{1,0:T(8,128)(2,1)} %copy-done.3, bf16[128,2048]{1,0:T(8,128)(2,1)} %copy-done.4, ...), custom_call_target="tpu_custom_call" | custom-call | flops 1073741824 | bytes 5242880 | tf_op jit(solution)/shard_map/multiply/pallas_call | solution.py:154
  82.3 2.2 %collective-permute-done.14 = bf16[1,128,256]{2,1,0:T(8,128)(2,1)S(1)} collective-permute-done((bf16[1,128,256]{2,1,0:T(8,128)(2,1)S(1)}, bf16[1,128,256]{2,1,0:T(8,128)(2,1)S(1)}, u32[]{:S(2)}, u32[]{:S(2)}) %collective-permute-start.14) | collective-permute-done | bytes 65568 | tf_op jit(solution)/shard_map/ppermute | solution.py:17
  86.1 2.9 %collective-permute-start.21 = (bf16[2,128,256]{2,1,0:T(8,128)(2,1)S(1)}, bf16[2,128,256]{2,1,0:T(8,128)(2,1)S(1)}, u32[]{:S(2)}, u32[]{:S(2)}) collective-permute-start(bf16[2,128,256]{2,1,0:T(8,128)(2,1)S(1)} %pad_maximum_fusion.5.rest_2_), channel_id=1, source_target_pairs={{0,3},{1,2},{2,1},{3,0},{4,7},{5,6},{6,5},{7,4},{8,11},{9,10},{10,... | collective-permute-start | bytes 393224 | tf_op jit(solution)/shard_map/ppermute | solution.py:17
  91.2 2.2 %collective-permute-done.21.rest_5_ = bf16[2,128,256]{2,1,0:T(8,128)(2,1)S(1)} collective-permute-done((bf16[2,128,256]{2,1,0:T(8,128)(2,1)S(1)}, bf16[2,128,256]{2,1,0:T(8,128)(2,1)S(1)}, u32[]{:S(2)}, u32[]{:S(2)}) %collective-permute-start.21) | collective-permute-done | bytes 131104 | tf_op jit(solution)/shard_map/ppermute | solution.py:17
  93.5 2.9 %collective-permute-start.23 = (f32[128,512]{1,0:T(8,128)}, f32[128,512]{1,0:T(8,128)S(1)}, u32[]{:S(2)}, u32[]{:S(2)}) collective-permute-start(f32[128,512]{1,0:T(8,128)} %get-tuple-element.74), channel_id=1, source_target_pairs={{0,2},{1,3},{2,0},{3,1},{4,6},{5,7},{6,4},{7,5},{8,10},{9,11},{10,... | collective-permute-start | bytes 786440 | tf_op jit(solution)/shard_map/ppermute | solution.py:17
  96.4 2.7 %collective-permute-start.24 = (f32[128,512]{1,0:T(8,128)}, f32[128,512]{1,0:T(8,128)S(1)}, u32[]{:S(2)}, u32[]{:S(2)}) collective-permute-start(f32[128,512]{1,0:T(8,128)} %get-tuple-element.75), channel_id=1, source_target_pairs={{0,3},{1,2},{2,1},{3,0},{4,7},{5,6},{6,5},{7,4},{8,11},{9,10},{10,... | collective-permute-start | bytes 786440 | tf_op jit(solution)/shard_map/ppermute | solution.py:17
  99.9 8.6 %attend.2 = (f32[2048,128]{1,0:T(8,128)}, f32[2048,128]{1,0:T(8,128)}) custom-call(s32[1,4]{1,0:T(1,128)} %len_ref.3, bf16[128,1024]{1,0:T(8,128)(2,1)} %d_ref.3, bf16[8,256,128]{2,1,0:T(8,128)(2,1)} %copy-done.6, bf16[8,256,128]{2,1,0:T(8,128)(2,1)} %copy-done.11, bf16[2,128,256]{2,1,0:T(8,128)(2,1)} %copy-done.8, bf16[2,128,256]{2,1,0:T(8,128)(2,1)} %copy-done.20, ...), custom_call_target="tpu_custom_call" | custom-call | flops 1610612736 | bytes 3145728 | tf_op jit(solution)/shard_map/attend/pallas_call | solution.py:299
  109.5 9.1 %attend.3 = (f32[2048,128]{1,0:T(8,128)}, bf16[2048,128]{1,0:T(8,128)(2,1)}) custom-call(s32[1,4]{1,0:T(1,128)} %len_ref.3, bf16[128,1024]{1,0:T(8,128)(2,1)} %d_ref.3, bf16[8,256,128]{2,1,0:T(8,128)(2,1)} %copy-done.6, bf16[8,256,128]{2,1,0:T(8,128)(2,1)} %copy-done.11, bf16[2,128,256]{2,1,0:T(8,128)(2,1)} %copy-done.8, bf16[2,128,256]{2,1,0:T(8,128)(2,1)} %copy-done.20, ...), custom_call_target="tpu_custom_call" | custom-call | flops 1610612736 | bytes 3145728 | tf_op jit(solution)/shard_map/attend/pallas_call | solution.py:299
  118.7 2.1 %collective-permute-done.25 = bf16[2048,128]{1,0:T(8,128)(2,1)S(1)} collective-permute-done((bf16[2048,128]{1,0:T(8,128)(2,1)}, bf16[2048,128]{1,0:T(8,128)(2,1)S(1)}, u32[]{:S(2)}, u32[]{:S(2)}) %collective-permute-start.25) | collective-permute-done | bytes 524320 | tf_op jit(solution)/shard_map/ppermute | solution.py:17
  123.5 2.3 %collective-permute-start.32 = (bf16[256,128]{1,0:T(8,128)(2,1)S(1)}, bf16[256,128]{1,0:T(8,128)(2,1)S(1)}, u32[]{:S(2)}, u32[]{:S(2)}) collective-permute-start(bf16[256,128]{1,0:T(8,128)(2,1)S(1)} %get-tuple-element.87), channel_id=1, source_target_pairs={{0,6},{1,7},{2,4},{3,5},{4,2},{5,3},{6,0},{7,1},{8,14},{9,15},{10,... | collective-permute-start | bytes 196616 | tf_op jit(solution)/shard_map/ppermute | solution.py:17
  127.1 2.0 %collective-permute-start.30 = (bf16[256,128]{1,0:T(8,128)(2,1)S(1)}, bf16[256,128]{1,0:T(8,128)(2,1)S(1)}, u32[]{:S(2)}, u32[]{:S(2)}) collective-permute-start(bf16[256,128]{1,0:T(8,128)(2,1)S(1)} %get-tuple-element.89), channel_id=1, source_target_pairs={{0,7},{1,6},{2,5},{3,4},{4,3},{5,2},{6,1},{7,0},{8,15},{9,14},{10,... | collective-permute-start | bytes 196616 | tf_op jit(solution)/shard_map/ppermute | solution.py:17
  129.0 1.7 %collective-permute-start.29 = (bf16[256,128]{1,0:T(8,128)(2,1)S(1)}, bf16[256,128]{1,0:T(8,128)(2,1)S(1)}, u32[]{:S(2)}, u32[]{:S(2)}) collective-permute-start(bf16[256,128]{1,0:T(8,128)(2,1)S(1)} %get-tuple-element.90), channel_id=1, source_target_pairs={{0,3},{1,2},{2,1},{3,0},{4,7},{5,6},{6,5},{7,4},{8,11},{9,10},{10,... | collective-permute-start | bytes 196616 | tf_op jit(solution)/shard_map/ppermute | solution.py:17
  130.8 2.2 %collective-permute-done.26 = bf16[256,128]{1,0:T(8,128)(2,1)S(1)} collective-permute-done((bf16[256,128]{1,0:T(8,128)(2,1)S(1)}, bf16[256,128]{1,0:T(8,128)(2,1)S(1)}, u32[]{:S(2)}, u32[]{:S(2)}) %collective-permute-start.26) | collective-permute-done | bytes 65568 | tf_op jit(solution)/shard_map/ppermute | solution.py:17
  133.2 2.4 %collective-permute-start.27 = (bf16[256,128]{1,0:T(8,128)(2,1)S(1)}, bf16[256,128]{1,0:T(8,128)(2,1)S(1)}, u32[]{:S(2)}, u32[]{:S(2)}) collective-permute-start(bf16[256,128]{1,0:T(8,128)(2,1)S(1)} %get-tuple-element.92), channel_id=1, source_target_pairs={{0,2},{1,3},{2,0},{3,1},{4,6},{5,7},{6,4},{7,5},{8,10},{9,11},{10,... | collective-permute-start | bytes 196616 | tf_op jit(solution)/shard_map/ppermute | solution.py:17
  139.0 3.2 %collective-permute-done.33 = bf16[256,128]{1,0:T(8,128)(2,1)S(1)} collective-permute-done((bf16[256,128]{1,0:T(8,128)(2,1)S(1)}, bf16[256,128]{1,0:T(8,128)(2,1)S(1)}, u32[]{:S(2)}, u32[]{:S(2)}) %collective-permute-start.33) | collective-permute-done | bytes 65568 | tf_op jit(solution)/shard_map/ppermute | solution.py:17
  (108 shorter events, 35.5 us)
Async XLA Ops:
  3.8 33.2 %collective-permute-start = (bf16[640,512]{1,0:T(8,128)(2,1)}, bf16[640,512]{1,0:T(8,128)(2,1)S(1)}, u32[]{:S(2)}, u32[]{:S(2)}) collective-permute-start(bf16[640,512]{1,0:T(8,128)(2,1)} %get-tuple-element.43), channel_id=1, source_target_pairs={{0,4},{1,5},{2,6},{3,7},{4,0},{5,1},{6,2},{7,3},{8,12},{9,13},{10,... | collective-permute-start | bytes 1966088 | tf_op jit(solution)/shard_map/ppermute | solution.py:17
  7.9 39.5 %collective-permute-start.4 = (bf16[128,2048]{1,0:T(8,128)(2,1)}, bf16[128,2048]{1,0:T(8,128)(2,1)S(1)}, u32[]{:S(2)}, u32[]{:S(2)}) collective-permute-start(bf16[128,2048]{1,0:T(8,128)(2,1)} %get-tuple-element.44), channel_id=1, source_target_pairs={{0,1},{1,0},{2,3},{3,2},{4,5},{5,4},{6,7},{7,6},{8,9},{9,8},{10,11... | collective-permute-start | bytes 1572872 | tf_op jit(solution)/shard_map/ppermute | solution.py:17
  9.4 38.0 %collective-permute-start.5 = (bf16[128,2048]{1,0:T(8,128)(2,1)}, bf16[128,2048]{1,0:T(8,128)(2,1)S(1)}, u32[]{:S(2)}, u32[]{:S(2)}) collective-permute-start(bf16[128,2048]{1,0:T(8,128)(2,1)} %get-tuple-element.45), channel_id=1, source_target_pairs={{0,2},{1,3},{2,0},{3,1},{4,6},{5,7},{6,4},{7,5},{8,10},{9,11},{10,... | collective-permute-start | bytes 1572872 | tf_op jit(solution)/shard_map/ppermute | solution.py:17
  11.0 37.2 %collective-permute-start.6 = (bf16[128,2048]{1,0:T(8,128)(2,1)}, bf16[128,2048]{1,0:T(8,128)(2,1)S(1)}, u32[]{:S(2)}, u32[]{:S(2)}) collective-permute-start(bf16[128,2048]{1,0:T(8,128)(2,1)} %get-tuple-element.46), channel_id=1, source_target_pairs={{0,3},{1,2},{2,1},{3,0},{4,7},{5,6},{6,5},{7,4},{8,11},{9,10},{10,... | collective-permute-start | bytes 1572872 | tf_op jit(solution)/shard_map/ppermute | solution.py:17
  37.0 10.3 %collective-permute-start.3 = (bf16[1,384,512]{2,1,0:T(8,128)(2,1)S(1)}, bf16[1,384,512]{2,1,0:T(8,128)(2,1)S(1)}, u32[]{:S(2)}, u32[]{:S(2)}) collective-permute-start(bf16[1,384,512]{2,1,0:T(8,128)(2,1)S(1)} %slice_bitcast_fusion), channel_id=1, source_target_pairs={{0,16},{8,24},{16,0},{24,8},{1,17},{9,25},{17,1},{25,9},{2,18},{10... | collective-permute-start | bytes 1179656 | tf_op jit(solution)/shard_map/ppermute | solution.py:17
  38.6 7.4 %collective-permute-start.2 = (bf16[1,256,128]{2,1,0:T(8,128)(2,1)S(1)}, bf16[1,256,128]{2,1,0:T(8,128)(2,1)S(1)}, u32[]{:S(2)}, u32[]{:S(2)}) collective-permute-start(bf16[1,256,128]{2,1,0:T(8,128)(2,1)S(1)} %select_bitcast_fusion), channel_id=1, source_target_pairs={{0,4},{1,5},{2,6},{3,7},{4,0},{5,1},{6,2},{7,3},{8,12},{9,13},{10,... | collective-permute-start | bytes 196616 | tf_op jit(solution)/shard_map/ppermute | solution.py:17
  48.2 8.8 %collective-permute-start.1 = (bf16[1,256,512]{2,1,0:T(8,128)(2,1)S(1)}, bf16[1,256,512]{2,1,0:T(8,128)(2,1)S(1)}, u32[]{:S(2)}, u32[]{:S(2)}) collective-permute-start(bf16[1,256,512]{2,1,0:T(8,128)(2,1)S(1)} %slice_bitcast_fusion.1), channel_id=1, source_target_pairs={{0,16},{8,24},{16,0},{24,8},{1,17},{9,25},{17,1},{25,9},{2,18},{10... | collective-permute-start | bytes 786440 | tf_op jit(solution)/shard_map/ppermute | solution.py:17
  55.5 7.7 %collective-permute-start.9 = (bf16[4,256,128]{2,1,0:T(8,128)(2,1)S(1)}, bf16[4,256,128]{2,1,0:T(8,128)(2,1)S(1)}, u32[]{:S(2)}, u32[]{:S(2)}) collective-permute-start(bf16[4,256,128]{2,1,0:T(8,128)(2,1)S(1)} %pad_maximum_fusion.3), channel_id=1, source_target_pairs={{0,1},{1,0},{2,3},{3,2},{4,5},{5,4},{6,7},{7,6},{8,9},{9,8},{10,11... | collective-permute-start | bytes 786440 | tf_op jit(solution)/shard_map/ppermute | solution.py:17
  63.2 11.7 %collective-permute-start.10 = (bf16[2,256,512]{2,1,0:T(8,128)(2,1)S(1)}, bf16[2,256,512]{2,1,0:T(8,128)(2,1)S(1)}, u32[]{:S(2)}, u32[]{:S(2)}) collective-permute-start(bf16[2,256,512]{2,1,0:T(8,128)(2,1)S(1)} %pad_maximum_fusion.1.rest_4_), channel_id=1, source_target_pairs={{0,8},{8,0},{16,24},{24,16},{1,9},{9,1},{17,25},{25,17},{2,10},{10... | collective-permute-start | bytes 1572872 | tf_op jit(solution)/shard_map/ppermute | solution.py:17
  65.7 8.3 %collective-permute-start.13 = (f32[128,256]{1,0:T(8,128)}, f32[128,256]{1,0:T(8,128)S(1)}, u32[]{:S(2)}, u32[]{:S(2)}) collective-permute-start(f32[128,256]{1,0:T(8,128)} %get-tuple-element.59), channel_id=1, source_target_pairs={{0,3},{1,2},{2,1},{3,0},{4,7},{5,6},{6,5},{7,4},{8,11},{9,10},{10,... | collective-permute-start | bytes 393224 | tf_op jit(solution)/shard_map/ppermute | solution.py:17
  66.9 17.7 %collective-permute-start.15 = (f32[128,512]{1,0:T(8,128)}, f32[128,512]{1,0:T(8,128)S(1)}, u32[]{:S(2)}, u32[]{:S(2)}) collective-permute-start(f32[128,512]{1,0:T(8,128)} %get-tuple-element.67), channel_id=1, source_target_pairs={{0,1},{1,0},{2,3},{3,2},{4,5},{5,4},{6,7},{7,6},{8,9},{9,8},{10,11... | collective-permute-start | bytes 786440 | tf_op jit(solution)/shard_map/ppermute | solution.py:17
  69.5 15.1 %collective-permute-start.16 = (f32[128,512]{1,0:T(8,128)}, f32[128,512]{1,0:T(8,128)S(1)}, u32[]{:S(2)}, u32[]{:S(2)}) collective-permute-start(f32[128,512]{1,0:T(8,128)} %get-tuple-element.68), channel_id=1, source_target_pairs={{0,2},{1,3},{2,0},{3,1},{4,6},{5,7},{6,4},{7,5},{8,10},{9,11},{10,... | collective-permute-start | bytes 786440 | tf_op jit(solution)/shard_map/ppermute | solution.py:17
  71.5 14.7 %collective-permute-start.17 = (f32[128,512]{1,0:T(8,128)}, f32[128,512]{1,0:T(8,128)S(1)}, u32[]{:S(2)}, u32[]{:S(2)}) collective-permute-start(f32[128,512]{1,0:T(8,128)} %get-tuple-element.69), channel_id=1, source_target_pairs={{0,3},{1,2},{2,1},{3,0},{4,7},{5,6},{6,5},{7,4},{8,11},{9,10},{10,... | collective-permute-start | bytes 786440 | tf_op jit(solution)/shard_map/ppermute | solution.py:17
  75.0 9.5 %collective-permute-start.14 = (bf16[1,128,256]{2,1,0:T(8,128)(2,1)S(1)}, bf16[1,128,256]{2,1,0:T(8,128)(2,1)S(1)}, u32[]{:S(2)}, u32[]{:S(2)}) collective-permute-start(bf16[1,128,256]{2,1,0:T(8,128)(2,1)S(1)} %bitcast.7), channel_id=1, source_target_pairs={{0,4},{1,5},{2,6},{3,7},{4,0},{5,1},{6,2},{7,3},{8,12},{9,13},{10,... | collective-permute-start | bytes 196616 | tf_op jit(solution)/shard_map/ppermute | solution.py:17
  86.1 13.0 %collective-permute-start.18 = (bf16[8,256,128]{2,1,0:T(8,128)(2,1)S(1)}, bf16[8,256,128]{2,1,0:T(8,128)(2,1)S(1)}, u32[]{:S(2)}, u32[]{:S(2)}) collective-permute-start(bf16[8,256,128]{2,1,0:T(8,128)(2,1)S(1)} %pad_maximum_fusion.2.rest_0_), channel_id=1, source_target_pairs={{0,8},{8,0},{16,24},{24,16},{1,9},{9,1},{17,25},{25,17},{2,10},{10... | collective-permute-start | bytes 1572872 | tf_op jit(solution)/shard_map/ppermute | solution.py:17
  89.2 9.9 %collective-permute-start.19 = (bf16[2,128,256]{2,1,0:T(8,128)(2,1)S(1)}, bf16[2,128,256]{2,1,0:T(8,128)(2,1)S(1)}, u32[]{:S(2)}, u32[]{:S(2)}) collective-permute-start(bf16[2,128,256]{2,1,0:T(8,128)(2,1)S(1)} %pad_maximum_fusion.5.rest_2_), channel_id=1, source_target_pairs={{0,1},{1,0},{2,3},{3,2},{4,5},{5,4},{6,7},{7,6},{8,9},{9,8},{10,11... | collective-permute-start | bytes 393224 | tf_op jit(solution)/shard_map/ppermute | solution.py:17
  90.6 18.0 %collective-permute-start.22 = (f32[128,512]{1,0:T(8,128)}, f32[128,512]{1,0:T(8,128)S(1)}, u32[]{:S(2)}, u32[]{:S(2)}) collective-permute-start(f32[128,512]{1,0:T(8,128)} %get-tuple-element.73), channel_id=1, source_target_pairs={{0,1},{1,0},{2,3},{3,2},{4,5},{5,4},{6,7},{7,6},{8,9},{9,8},{10,11... | collective-permute-start | bytes 786440 | tf_op jit(solution)/shard_map/ppermute | solution.py:17
  93.5 15.1 %collective-permute-start.23 = (f32[128,512]{1,0:T(8,128)}, f32[128,512]{1,0:T(8,128)S(1)}, u32[]{:S(2)}, u32[]{:S(2)}) collective-permute-start(f32[128,512]{1,0:T(8,128)} %get-tuple-element.74), channel_id=1, source_target_pairs={{0,2},{1,3},{2,0},{3,1},{4,6},{5,7},{6,4},{7,5},{8,10},{9,11},{10,... | collective-permute-start | bytes 786440 | tf_op jit(solution)/shard_map/ppermute | solution.py:17
  96.4 12.2 %collective-permute-start.24 = (f32[128,512]{1,0:T(8,128)}, f32[128,512]{1,0:T(8,128)S(1)}, u32[]{:S(2)}, u32[]{:S(2)}) collective-permute-start(f32[128,512]{1,0:T(8,128)} %get-tuple-element.75), channel_id=1, source_target_pairs={{0,3},{1,2},{2,1},{3,0},{4,7},{5,6},{6,5},{7,4},{8,11},{9,10},{10,... | collective-permute-start | bytes 786440 | tf_op jit(solution)/shard_map/ppermute | solution.py:17
  122.2 10.7 %collective-permute-start.26 = (bf16[256,128]{1,0:T(8,128)(2,1)S(1)}, bf16[256,128]{1,0:T(8,128)(2,1)S(1)}, u32[]{:S(2)}, u32[]{:S(2)}) collective-permute-start(bf16[256,128]{1,0:T(8,128)(2,1)S(1)} %get-tuple-element.86), channel_id=1, source_target_pairs={{0,4},{1,5},{2,6},{3,7},{4,0},{5,1},{6,2},{7,3},{8,12},{9,13},{10,... | collective-permute-start | bytes 196616 | tf_op jit(solution)/shard_map/ppermute | solution.py:17
  123.5 9.7 %collective-permute-start.32 = (bf16[256,128]{1,0:T(8,128)(2,1)S(1)}, bf16[256,128]{1,0:T(8,128)(2,1)S(1)}, u32[]{:S(2)}, u32[]{:S(2)}) collective-permute-start(bf16[256,128]{1,0:T(8,128)(2,1)S(1)} %get-tuple-element.87), channel_id=1, source_target_pairs={{0,6},{1,7},{2,4},{3,5},{4,2},{5,3},{6,0},{7,1},{8,14},{9,15},{10,... | collective-permute-start | bytes 196616 | tf_op jit(solution)/shard_map/ppermute | solution.py:17
  125.8 10.3 %collective-permute-start.31 = (bf16[256,128]{1,0:T(8,128)(2,1)S(1)}, bf16[256,128]{1,0:T(8,128)(2,1)S(1)}, u32[]{:S(2)}, u32[]{:S(2)}) collective-permute-start(bf16[256,128]{1,0:T(8,128)(2,1)S(1)} %get-tuple-element.88), channel_id=1, source_target_pairs={{0,5},{1,4},{2,7},{3,6},{4,1},{5,0},{6,3},{7,2},{8,13},{9,12},{10,... | collective-permute-start | bytes 196616 | tf_op jit(solution)/shard_map/ppermute | solution.py:17
  127.1 9.1 %collective-permute-start.30 = (bf16[256,128]{1,0:T(8,128)(2,1)S(1)}, bf16[256,128]{1,0:T(8,128)(2,1)S(1)}, u32[]{:S(2)}, u32[]{:S(2)}) collective-permute-start(bf16[256,128]{1,0:T(8,128)(2,1)S(1)} %get-tuple-element.89), channel_id=1, source_target_pairs={{0,7},{1,6},{2,5},{3,4},{4,3},{5,2},{6,1},{7,0},{8,15},{9,14},{10,... | collective-permute-start | bytes 196616 | tf_op jit(solution)/shard_map/ppermute | solution.py:17
  129.0 7.5 %collective-permute-start.29 = (bf16[256,128]{1,0:T(8,128)(2,1)S(1)}, bf16[256,128]{1,0:T(8,128)(2,1)S(1)}, u32[]{:S(2)}, u32[]{:S(2)}) collective-permute-start(bf16[256,128]{1,0:T(8,128)(2,1)S(1)} %get-tuple-element.90), channel_id=1, source_target_pairs={{0,3},{1,2},{2,1},{3,0},{4,7},{5,6},{6,5},{7,4},{8,11},{9,10},{10,... | collective-permute-start | bytes 196616 | tf_op jit(solution)/shard_map/ppermute | solution.py:17
  (32 other events, 273.6 us)

commit v9 on v8

--- a/solution.py
+++ b/solution.py
@@ -385,13 +385,14 @@
         sums = attend(lengths, parts_a, d_attn, 0, cache, group, g_order, ())
         keep, give = attend(lengths, parts_b, d_attn, first, cache, group, g_order, sums)
 
-        half = keep + swap(give, "dp", n_dp, 1).astype(F32)
-        size = half.shape[0] // n_fsdp
-        mine = half[:size]
+        given = swap(give, "dp", n_dp, 1)
+        size = keep.shape[0] // n_fsdp
+        mine = keep[:size] + given[:size].astype(F32)
         far = [slot for slot in range(n_fsdp) if f_order[slot] >= inner]
         near = [slot for slot in range(1, n_fsdp) if f_order[slot] < inner]
         for slot in far[:1] + near + far[:0:-1]:
-            out = half[slot * size : (slot + 1) * size].astype(BF16)
+            rows = slice(slot * size, (slot + 1) * size)
+            out = (keep[rows] + given[rows].astype(F32)).astype(BF16)
             mine = mine + swap(out, "fsdp", n_fsdp, f_order[slot]).astype(F32)
         for bit in d_bits[:-1]:
             mine = mine.astype(BF16)

time: 145 us -> 146 us (level)
  no operation moved by 1% of the time
where the time goes in v9:
time: 146 us; the launch traced here: 145 us
  waiting for transfers between devices  60.7 us (42%)
  starting transfers between devices  46.2 us (32%)
  Pallas kernels  31.3 us (21%)
  other arithmetic  4.24 us (3%)
  local copies, waits for them, and re-layouts  1.74 us (1%)
    ppermute x35, waiting for transfers between devices, swap(): return lax.ppermute(value, axis, [(i, i ^ bit) for i in range(size)])  60.7 us
    ppermute x35, starting transfers between devices, swap(): return lax.ppermute(value, axis, [(i, i ^ bit) for i in range(size)])  46.2 us
    pallas_call x2, Pallas kernels, attend(): pl.pallas_call(body, in_specs=[pl.BlockSpec(memory_space=pltpu.SMEM)] + [...  17.8 us
    pallas_call x2, Pallas kernels, multiply(): pl.pallas_call(body, in_specs=[pl.BlockSpec(memory_space=pl.ANY)] * (1 +...  10.4 us
    pallas_call x1, Pallas kernels, prepare(): pl.pallas_call(body, in_specs=[pl.BlockSpec(memory_space=pl.ANY)] * 4, ou...  3.1 us
  transfers between devices with their start and end apart: 35, of which 20 were waited for; matrix products, arithmetic and copies ran while one was open for 1% of the time, Pallas kernels for 13%

profile of v9, /device:TPU:0, one launch (start us, length us, event | category | flops | bytes accessed | tf_op | source)
XLA Modules:
  0.0 145.2 jit_solution(12224165071894853489)
XLA Ops:
  0.6 3.1 %prepare.1 = (bf16[128,2048]{1,0:T(8,128)(2,1)}, bf16[128,2048]{1,0:T(8,128)(2,1)}, bf16[128,2048]{1,0:T(8,128)(2,1)}, bf16[640,512]{1,0:T(8,128)(2,1)}) custom-call(bf16[128,8192]{1,0:T(8,128)(2,1)} %hidden_ref.5, bf16[1024,1024]{1,0:T(8,128)(2,1)} %rest_3_.3, bf16[1024,128]{1,0:T(8,128)(2,1)} %rest_3_.2, bf16[1024,128]{1,0:T(8,128)(2,1)} %rest_4_.1), custom_call_target="tpu_custom_call" | custom-call | bytes 4456448 | tf_op jit(solution)/shard_map/prepare/pallas_call | solution.py:83
  3.8 4.1 %collective-permute-start = (bf16[640,512]{1,0:T(8,128)(2,1)}, bf16[640,512]{1,0:T(8,128)(2,1)S(1)}, u32[]{:S(2)}, u32[]{:S(2)}) collective-permute-start(bf16[640,512]{1,0:T(8,128)(2,1)} %get-tuple-element.43), channel_id=1, source_target_pairs={{0,4},{1,5},{2,6},{3,7},{4,0},{5,1},{6,2},{7,3},{8,12},{9,13},{10,... | collective-permute-start | bytes 1966088 | tf_op jit(solution)/shard_map/ppermute | solution.py:17
  11.3 25.6 %collective-permute-done = bf16[640,512]{1,0:T(8,128)(2,1)S(1)} collective-permute-done((bf16[640,512]{1,0:T(8,128)(2,1)}, bf16[640,512]{1,0:T(8,128)(2,1)S(1)}, u32[]{:S(2)}, u32[]{:S(2)}) %collective-permute-start) | collective-permute-done | bytes 655392 | tf_op jit(solution)/shard_map/ppermute | solution.py:17
  37.0 1.6 %collective-permute-start.3 = (bf16[1,384,512]{2,1,0:T(8,128)(2,1)S(1)}, bf16[1,384,512]{2,1,0:T(8,128)(2,1)S(1)}, u32[]{:S(2)}, u32[]{:S(2)}) collective-permute-start(bf16[1,384,512]{2,1,0:T(8,128)(2,1)S(1)} %slice_bitcast_fusion), channel_id=1, source_target_pairs={{0,16},{8,24},{16,0},{24,8},{1,17},{9,25},{17,1},{25,9},{2,18},{10... | collective-permute-start | bytes 1179656 | tf_op jit(solution)/shard_map/ppermute | solution.py:17
  38.7 7.3 %collective-permute-done.2 = bf16[1,256,128]{2,1,0:T(8,128)(2,1)S(1)} collective-permute-done((bf16[1,256,128]{2,1,0:T(8,128)(2,1)S(1)}, bf16[1,256,128]{2,1,0:T(8,128)(2,1)S(1)}, u32[]{:S(2)}, u32[]{:S(2)}) %collective-permute-start.2) | collective-permute-done | bytes 65568 | tf_op jit(solution)/shard_map/ppermute | solution.py:17
  50.7 4.8 %collective-permute-done.7 = bf16[2,256,128]{2,1,0:T(8,128)(2,1)S(1)} collective-permute-done((bf16[2,256,128]{2,1,0:T(8,128)(2,1)S(1)}, bf16[2,256,128]{2,1,0:T(8,128)(2,1)S(1)}, u32[]{:S(2)}, u32[]{:S(2)}) %collective-permute-start.7) | collective-permute-done | bytes 131104 | tf_op jit(solution)/shard_map/ppermute | solution.py:17
  55.5 1.6 %collective-permute-start.9 = (bf16[4,256,128]{2,1,0:T(8,128)(2,1)S(1)}, bf16[4,256,128]{2,1,0:T(8,128)(2,1)S(1)}, u32[]{:S(2)}, u32[]{:S(2)}) collective-permute-start(bf16[4,256,128]{2,1,0:T(8,128)(2,1)S(1)} %pad_maximum_fusion.3), channel_id=1, source_target_pairs={{0,1},{1,0},{2,3},{3,2},{4,5},{5,4},{6,7},{7,6},{8,9},{9,8},{10,11... | collective-permute-start | bytes 786440 | tf_op jit(solution)/shard_map/ppermute | solution.py:17
  57.2 5.9 %multiply.2 = (f32[128,256]{1,0:T(8,128)}, f32[128,256]{1,0:T(8,128)}, f32[128,256]{1,0:T(8,128)}, f32[128,256]{1,0:T(8,128)}, f32[128,512]{1,0:T(8,128)}, /*ind...) custom-call(bf16[128,8192]{1,0:T(8,128)(2,1)} %hidden_ref.5, bf16[128,2048]{1,0:T(8,128)(2,1)} %copy-done.2, ...), custom_call_target="tpu_custom_call" | custom-call | flops 1610612736 | bytes 6815744 | tf_op jit(solution)/shard_map/multiply/pallas_call | solution.py:154
  75.0 2.8 %collective-permute-start.14 = (bf16[1,128,256]{2,1,0:T(8,128)(2,1)S(1)}, bf16[1,128,256]{2,1,0:T(8,128)(2,1)S(1)}, u32[]{:S(2)}, u32[]{:S(2)}) collective-permute-start(bf16[1,128,256]{2,1,0:T(8,128)(2,1)S(1)} %bitcast.7), channel_id=1, source_target_pairs={{0,4},{1,5},{2,6},{3,7},{4,0},{5,1},{6,2},{7,3},{8,12},{9,13},{10,... | collective-permute-start | bytes 196616 | tf_op jit(solution)/shard_map/ppermute | solution.py:17
  77.7 4.6 %multiply.3 = (f32[128,512]{1,0:T(8,128)}, f32[128,512]{1,0:T(8,128)}, f32[128,512]{1,0:T(8,128)}, f32[128,512]{1,0:T(8,128)}) custom-call(bf16[128,8192]{1,0:T(8,128)(2,1)} %hidden_ref.5, bf16[128,2048]{1,0:T(8,128)(2,1)} %copy-done.2, bf16[128,2048]{1,0:T(8,128)(2,1)} %copy-done.3, bf16[128,2048]{1,0:T(8,128)(2,1)} %copy-done.4, ...), custom_call_target="tpu_custom_call" | custom-call | flops 1073741824 | bytes 5242880 | tf_op jit(solution)/shard_map/multiply/pallas_call | solution.py:154
  82.3 2.2 %collective-permute-done.14 = bf16[1,128,256]{2,1,0:T(8,128)(2,1)S(1)} collective-permute-done((bf16[1,128,256]{2,1,0:T(8,128)(2,1)S(1)}, bf16[1,128,256]{2,1,0:T(8,128)(2,1)S(1)}, u32[]{:S(2)}, u32[]{:S(2)}) %collective-permute-start.14) | collective-permute-done | bytes 65568 | tf_op jit(solution)/shard_map/ppermute | solution.py:17
  86.1 2.9 %collective-permute-start.21 = (bf16[2,128,256]{2,1,0:T(8,128)(2,1)S(1)}, bf16[2,128,256]{2,1,0:T(8,128)(2,1)S(1)}, u32[]{:S(2)}, u32[]{:S(2)}) collective-permute-start(bf16[2,128,256]{2,1,0:T(8,128)(2,1)S(1)} %pad_maximum_fusion.5.rest_2_), channel_id=1, source_target_pairs={{0,3},{1,2},{2,1},{3,0},{4,7},{5,6},{6,5},{7,4},{8,11},{9,10},{10,... | collective-permute-start | bytes 393224 | tf_op jit(solution)/shard_map/ppermute | solution.py:17
  91.2 2.2 %collective-permute-done.21.rest_5_ = bf16[2,128,256]{2,1,0:T(8,128)(2,1)S(1)} collective-permute-done((bf16[2,128,256]{2,1,0:T(8,128)(2,1)S(1)}, bf16[2,128,256]{2,1,0:T(8,128)(2,1)S(1)}, u32[]{:S(2)}, u32[]{:S(2)}) %collective-permute-start.21) | collective-permute-done | bytes 131104 | tf_op jit(solution)/shard_map/ppermute | solution.py:17
  93.5 2.9 %collective-permute-start.23 = (f32[128,512]{1,0:T(8,128)}, f32[128,512]{1,0:T(8,128)S(1)}, u32[]{:S(2)}, u32[]{:S(2)}) collective-permute-start(f32[128,512]{1,0:T(8,128)} %get-tuple-element.74), channel_id=1, source_target_pairs={{0,2},{1,3},{2,0},{3,1},{4,6},{5,7},{6,4},{7,5},{8,10},{9,11},{10,... | collective-permute-start | bytes 786440 | tf_op jit(solution)/shard_map/ppermute | solution.py:17
  96.3 2.7 %collective-permute-start.24 = (f32[128,512]{1,0:T(8,128)}, f32[128,512]{1,0:T(8,128)S(1)}, u32[]{:S(2)}, u32[]{:S(2)}) collective-permute-start(f32[128,512]{1,0:T(8,128)} %get-tuple-element.75), channel_id=1, source_target_pairs={{0,3},{1,2},{2,1},{3,0},{4,7},{5,6},{6,5},{7,4},{8,11},{9,10},{10,... | collective-permute-start | bytes 786440 | tf_op jit(solution)/shard_map/ppermute | solution.py:17
  99.9 8.6 %attend.2 = (f32[2048,128]{1,0:T(8,128)}, f32[2048,128]{1,0:T(8,128)}) custom-call(s32[1,4]{1,0:T(1,128)} %len_ref.3, bf16[128,1024]{1,0:T(8,128)(2,1)} %d_ref.3, bf16[8,256,128]{2,1,0:T(8,128)(2,1)} %copy-done.6, bf16[8,256,128]{2,1,0:T(8,128)(2,1)} %copy-done.11, bf16[2,128,256]{2,1,0:T(8,128)(2,1)} %copy-done.8, bf16[2,128,256]{2,1,0:T(8,128)(2,1)} %copy-done.20, ...), custom_call_target="tpu_custom_call" | custom-call | flops 1610612736 | bytes 3145728 | tf_op jit(solution)/shard_map/attend/pallas_call | solution.py:299
  109.4 9.1 %attend.3 = (f32[2048,128]{1,0:T(8,128)}, bf16[2048,128]{1,0:T(8,128)(2,1)}) custom-call(s32[1,4]{1,0:T(1,128)} %len_ref.3, bf16[128,1024]{1,0:T(8,128)(2,1)} %d_ref.3, bf16[8,256,128]{2,1,0:T(8,128)(2,1)} %copy-done.6, bf16[8,256,128]{2,1,0:T(8,128)(2,1)} %copy-done.11, bf16[2,128,256]{2,1,0:T(8,128)(2,1)} %copy-done.8, bf16[2,128,256]{2,1,0:T(8,128)(2,1)} %copy-done.20, ...), custom_call_target="tpu_custom_call" | custom-call | flops 1610612736 | bytes 3145728 | tf_op jit(solution)/shard_map/attend/pallas_call | solution.py:299
  118.7 2.1 %collective-permute-done.25 = bf16[2048,128]{1,0:T(8,128)(2,1)S(1)} collective-permute-done((bf16[2048,128]{1,0:T(8,128)(2,1)}, bf16[2048,128]{1,0:T(8,128)(2,1)S(1)}, u32[]{:S(2)}, u32[]{:S(2)}) %collective-permute-start.25) | collective-permute-done | bytes 524320 | tf_op jit(solution)/shard_map/ppermute | solution.py:17
  123.4 2.3 %collective-permute-start.32 = (bf16[256,128]{1,0:T(8,128)(2,1)S(1)}, bf16[256,128]{1,0:T(8,128)(2,1)S(1)}, u32[]{:S(2)}, u32[]{:S(2)}) collective-permute-start(bf16[256,128]{1,0:T(8,128)(2,1)S(1)} %get-tuple-element.85), channel_id=1, source_target_pairs={{0,6},{1,7},{2,4},{3,5},{4,2},{5,3},{6,0},{7,1},{8,14},{9,15},{10,... | collective-permute-start | bytes 196616 | tf_op jit(solution)/shard_map/ppermute | solution.py:17
  127.0 2.0 %collective-permute-start.30 = (bf16[256,128]{1,0:T(8,128)(2,1)S(1)}, bf16[256,128]{1,0:T(8,128)(2,1)S(1)}, u32[]{:S(2)}, u32[]{:S(2)}) collective-permute-start(bf16[256,128]{1,0:T(8,128)(2,1)S(1)} %get-tuple-element.87), channel_id=1, source_target_pairs={{0,7},{1,6},{2,5},{3,4},{4,3},{5,2},{6,1},{7,0},{8,15},{9,14},{10,... | collective-permute-start | bytes 196616 | tf_op jit(solution)/shard_map/ppermute | solution.py:17
  128.9 1.7 %collective-permute-start.29 = (bf16[256,128]{1,0:T(8,128)(2,1)S(1)}, bf16[256,128]{1,0:T(8,128)(2,1)S(1)}, u32[]{:S(2)}, u32[]{:S(2)}) collective-permute-start(bf16[256,128]{1,0:T(8,128)(2,1)S(1)} %get-tuple-element.88), channel_id=1, source_target_pairs={{0,3},{1,2},{2,1},{3,0},{4,7},{5,6},{6,5},{7,4},{8,11},{9,10},{10,... | collective-permute-start | bytes 196616 | tf_op jit(solution)/shard_map/ppermute | solution.py:17
  130.7 2.2 %collective-permute-done.26 = bf16[256,128]{1,0:T(8,128)(2,1)S(1)} collective-permute-done((bf16[256,128]{1,0:T(8,128)(2,1)S(1)}, bf16[256,128]{1,0:T(8,128)(2,1)S(1)}, u32[]{:S(2)}, u32[]{:S(2)}) %collective-permute-start.26) | collective-permute-done | bytes 65568 | tf_op jit(solution)/shard_map/ppermute | solution.py:17
  133.1 2.4 %collective-permute-start.27 = (bf16[256,128]{1,0:T(8,128)(2,1)S(1)}, bf16[256,128]{1,0:T(8,128)(2,1)S(1)}, u32[]{:S(2)}, u32[]{:S(2)}) collective-permute-start(bf16[256,128]{1,0:T(8,128)(2,1)S(1)} %get-tuple-element.90), channel_id=1, source_target_pairs={{0,2},{1,3},{2,0},{3,1},{4,6},{5,7},{6,4},{7,5},{8,10},{9,11},{10,... | collective-permute-start | bytes 196616 | tf_op jit(solution)/shard_map/ppermute | solution.py:17
  139.8 3.2 %collective-permute-done.33 = bf16[256,128]{1,0:T(8,128)(2,1)S(1)} collective-permute-done((bf16[256,128]{1,0:T(8,128)(2,1)S(1)}, bf16[256,128]{1,0:T(8,128)(2,1)S(1)}, u32[]{:S(2)}, u32[]{:S(2)}) %collective-permute-start.33) | collective-permute-done | bytes 65568 | tf_op jit(solution)/shard_map/ppermute | solution.py:17
  (107 shorter events, 36.3 us)
Async XLA Ops:
  3.8 33.2 %collective-permute-start = (bf16[640,512]{1,0:T(8,128)(2,1)}, bf16[640,512]{1,0:T(8,128)(2,1)S(1)}, u32[]{:S(2)}, u32[]{:S(2)}) collective-permute-start(bf16[640,512]{1,0:T(8,128)(2,1)} %get-tuple-element.43), channel_id=1, source_target_pairs={{0,4},{1,5},{2,6},{3,7},{4,0},{5,1},{6,2},{7,3},{8,12},{9,13},{10,... | collective-permute-start | bytes 1966088 | tf_op jit(solution)/shard_map/ppermute | solution.py:17
  7.9 39.5 %collective-permute-start.4 = (bf16[128,2048]{1,0:T(8,128)(2,1)}, bf16[128,2048]{1,0:T(8,128)(2,1)S(1)}, u32[]{:S(2)}, u32[]{:S(2)}) collective-permute-start(bf16[128,2048]{1,0:T(8,128)(2,1)} %get-tuple-element.44), channel_id=1, source_target_pairs={{0,1},{1,0},{2,3},{3,2},{4,5},{5,4},{6,7},{7,6},{8,9},{9,8},{10,11... | collective-permute-start | bytes 1572872 | tf_op jit(solution)/shard_map/ppermute | solution.py:17
  9.4 38.0 %collective-permute-start.5 = (bf16[128,2048]{1,0:T(8,128)(2,1)}, bf16[128,2048]{1,0:T(8,128)(2,1)S(1)}, u32[]{:S(2)}, u32[]{:S(2)}) collective-permute-start(bf16[128,2048]{1,0:T(8,128)(2,1)} %get-tuple-element.45), channel_id=1, source_target_pairs={{0,2},{1,3},{2,0},{3,1},{4,6},{5,7},{6,4},{7,5},{8,10},{9,11},{10,... | collective-permute-start | bytes 1572872 | tf_op jit(solution)/shard_map/ppermute | solution.py:17
  11.0 37.2 %collective-permute-start.6 = (bf16[128,2048]{1,0:T(8,128)(2,1)}, bf16[128,2048]{1,0:T(8,128)(2,1)S(1)}, u32[]{:S(2)}, u32[]{:S(2)}) collective-permute-start(bf16[128,2048]{1,0:T(8,128)(2,1)} %get-tuple-element.46), channel_id=1, source_target_pairs={{0,3},{1,2},{2,1},{3,0},{4,7},{5,6},{6,5},{7,4},{8,11},{9,10},{10,... | collective-permute-start | bytes 1572872 | tf_op jit(solution)/shard_map/ppermute | solution.py:17
  37.0 10.3 %collective-permute-start.3 = (bf16[1,384,512]{2,1,0:T(8,128)(2,1)S(1)}, bf16[1,384,512]{2,1,0:T(8,128)(2,1)S(1)}, u32[]{:S(2)}, u32[]{:S(2)}) collective-permute-start(bf16[1,384,512]{2,1,0:T(8,128)(2,1)S(1)} %slice_bitcast_fusion), channel_id=1, source_target_pairs={{0,16},{8,24},{16,0},{24,8},{1,17},{9,25},{17,1},{25,9},{2,18},{10... | collective-permute-start | bytes 1179656 | tf_op jit(solution)/shard_map/ppermute | solution.py:17
  38.6 7.4 %collective-permute-start.2 = (bf16[1,256,128]{2,1,0:T(8,128)(2,1)S(1)}, bf16[1,256,128]{2,1,0:T(8,128)(2,1)S(1)}, u32[]{:S(2)}, u32[]{:S(2)}) collective-permute-start(bf16[1,256,128]{2,1,0:T(8,128)(2,1)S(1)} %select_bitcast_fusion), channel_id=1, source_target_pairs={{0,4},{1,5},{2,6},{3,7},{4,0},{5,1},{6,2},{7,3},{8,12},{9,13},{10,... | collective-permute-start | bytes 196616 | tf_op jit(solution)/shard_map/ppermute | solution.py:17
  48.2 8.8 %collective-permute-start.1 = (bf16[1,256,512]{2,1,0:T(8,128)(2,1)S(1)}, bf16[1,256,512]{2,1,0:T(8,128)(2,1)S(1)}, u32[]{:S(2)}, u32[]{:S(2)}) collective-permute-start(bf16[1,256,512]{2,1,0:T(8,128)(2,1)S(1)} %slice_bitcast_fusion.1), channel_id=1, source_target_pairs={{0,16},{8,24},{16,0},{24,8},{1,17},{9,25},{17,1},{25,9},{2,18},{10... | collective-permute-start | bytes 786440 | tf_op jit(solution)/shard_map/ppermute | solution.py:17
  55.5 7.7 %collective-permute-start.9 = (bf16[4,256,128]{2,1,0:T(8,128)(2,1)S(1)}, bf16[4,256,128]{2,1,0:T(8,128)(2,1)S(1)}, u32[]{:S(2)}, u32[]{:S(2)}) collective-permute-start(bf16[4,256,128]{2,1,0:T(8,128)(2,1)S(1)} %pad_maximum_fusion.3), channel_id=1, source_target_pairs={{0,1},{1,0},{2,3},{3,2},{4,5},{5,4},{6,7},{7,6},{8,9},{9,8},{10,11... | collective-permute-start | bytes 786440 | tf_op jit(solution)/shard_map/ppermute | solution.py:17
  63.2 11.7 %collective-permute-start.10 = (bf16[2,256,512]{2,1,0:T(8,128)(2,1)S(1)}, bf16[2,256,512]{2,1,0:T(8,128)(2,1)S(1)}, u32[]{:S(2)}, u32[]{:S(2)}) collective-permute-start(bf16[2,256,512]{2,1,0:T(8,128)(2,1)S(1)} %pad_maximum_fusion.1.rest_4_), channel_id=1, source_target_pairs={{0,8},{8,0},{16,24},{24,16},{1,9},{9,1},{17,25},{25,17},{2,10},{10... | collective-permute-start | bytes 1572872 | tf_op jit(solution)/shard_map/ppermute | solution.py:17
  65.7 8.3 %collective-permute-start.13 = (f32[128,256]{1,0:T(8,128)}, f32[128,256]{1,0:T(8,128)S(1)}, u32[]{:S(2)}, u32[]{:S(2)}) collective-permute-start(f32[128,256]{1,0:T(8,128)} %get-tuple-element.59), channel_id=1, source_target_pairs={{0,3},{1,2},{2,1},{3,0},{4,7},{5,6},{6,5},{7,4},{8,11},{9,10},{10,... | collective-permute-start | bytes 393224 | tf_op jit(solution)/shard_map/ppermute | solution.py:17
  66.9 17.7 %collective-permute-start.15 = (f32[128,512]{1,0:T(8,128)}, f32[128,512]{1,0:T(8,128)S(1)}, u32[]{:S(2)}, u32[]{:S(2)}) collective-permute-start(f32[128,512]{1,0:T(8,128)} %get-tuple-element.67), channel_id=1, source_target_pairs={{0,1},{1,0},{2,3},{3,2},{4,5},{5,4},{6,7},{7,6},{8,9},{9,8},{10,11... | collective-permute-start | bytes 786440 | tf_op jit(solution)/shard_map/ppermute | solution.py:17
  69.5 15.1 %collective-permute-start.16 = (f32[128,512]{1,0:T(8,128)}, f32[128,512]{1,0:T(8,128)S(1)}, u32[]{:S(2)}, u32[]{:S(2)}) collective-permute-start(f32[128,512]{1,0:T(8,128)} %get-tuple-element.68), channel_id=1, source_target_pairs={{0,2},{1,3},{2,0},{3,1},{4,6},{5,7},{6,4},{7,5},{8,10},{9,11},{10,... | collective-permute-start | bytes 786440 | tf_op jit(solution)/shard_map/ppermute | solution.py:17
  71.4 14.7 %collective-permute-start.17 = (f32[128,512]{1,0:T(8,128)}, f32[128,512]{1,0:T(8,128)S(1)}, u32[]{:S(2)}, u32[]{:S(2)}) collective-permute-start(f32[128,512]{1,0:T(8,128)} %get-tuple-element.69), channel_id=1, source_target_pairs={{0,3},{1,2},{2,1},{3,0},{4,7},{5,6},{6,5},{7,4},{8,11},{9,10},{10,... | collective-permute-start | bytes 786440 | tf_op jit(solution)/shard_map/ppermute | solution.py:17
  75.0 9.5 %collective-permute-start.14 = (bf16[1,128,256]{2,1,0:T(8,128)(2,1)S(1)}, bf16[1,128,256]{2,1,0:T(8,128)(2,1)S(1)}, u32[]{:S(2)}, u32[]{:S(2)}) collective-permute-start(bf16[1,128,256]{2,1,0:T(8,128)(2,1)S(1)} %bitcast.7), channel_id=1, source_target_pairs={{0,4},{1,5},{2,6},{3,7},{4,0},{5,1},{6,2},{7,3},{8,12},{9,13},{10,... | collective-permute-start | bytes 196616 | tf_op jit(solution)/shard_map/ppermute | solution.py:17
  86.1 13.0 %collective-permute-start.18 = (bf16[8,256,128]{2,1,0:T(8,128)(2,1)S(1)}, bf16[8,256,128]{2,1,0:T(8,128)(2,1)S(1)}, u32[]{:S(2)}, u32[]{:S(2)}) collective-permute-start(bf16[8,256,128]{2,1,0:T(8,128)(2,1)S(1)} %pad_maximum_fusion.2.rest_0_), channel_id=1, source_target_pairs={{0,8},{8,0},{16,24},{24,16},{1,9},{9,1},{17,25},{25,17},{2,10},{10... | collective-permute-start | bytes 1572872 | tf_op jit(solution)/shard_map/ppermute | solution.py:17
  89.2 9.9 %collective-permute-start.19 = (bf16[2,128,256]{2,1,0:T(8,128)(2,1)S(1)}, bf16[2,128,256]{2,1,0:T(8,128)(2,1)S(1)}, u32[]{:S(2)}, u32[]{:S(2)}) collective-permute-start(bf16[2,128,256]{2,1,0:T(8,128)(2,1)S(1)} %pad_maximum_fusion.5.rest_2_), channel_id=1, source_target_pairs={{0,1},{1,0},{2,3},{3,2},{4,5},{5,4},{6,7},{7,6},{8,9},{9,8},{10,11... | collective-permute-start | bytes 393224 | tf_op jit(solution)/shard_map/ppermute | solution.py:17
  90.6 18.0 %collective-permute-start.22 = (f32[128,512]{1,0:T(8,128)}, f32[128,512]{1,0:T(8,128)S(1)}, u32[]{:S(2)}, u32[]{:S(2)}) collective-permute-start(f32[128,512]{1,0:T(8,128)} %get-tuple-element.73), channel_id=1, source_target_pairs={{0,1},{1,0},{2,3},{3,2},{4,5},{5,4},{6,7},{7,6},{8,9},{9,8},{10,11... | collective-permute-start | bytes 786440 | tf_op jit(solution)/shard_map/ppermute | solution.py:17
  93.5 15.1 %collective-permute-start.23 = (f32[128,512]{1,0:T(8,128)}, f32[128,512]{1,0:T(8,128)S(1)}, u32[]{:S(2)}, u32[]{:S(2)}) collective-permute-start(f32[128,512]{1,0:T(8,128)} %get-tuple-element.74), channel_id=1, source_target_pairs={{0,2},{1,3},{2,0},{3,1},{4,6},{5,7},{6,4},{7,5},{8,10},{9,11},{10,... | collective-permute-start | bytes 786440 | tf_op jit(solution)/shard_map/ppermute | solution.py:17
  96.3 12.2 %collective-permute-start.24 = (f32[128,512]{1,0:T(8,128)}, f32[128,512]{1,0:T(8,128)S(1)}, u32[]{:S(2)}, u32[]{:S(2)}) collective-permute-start(f32[128,512]{1,0:T(8,128)} %get-tuple-element.75), channel_id=1, source_target_pairs={{0,3},{1,2},{2,1},{3,0},{4,7},{5,6},{6,5},{7,4},{8,11},{9,10},{10,... | collective-permute-start | bytes 786440 | tf_op jit(solution)/shard_map/ppermute | solution.py:17
  122.1 10.7 %collective-permute-start.26 = (bf16[256,128]{1,0:T(8,128)(2,1)S(1)}, bf16[256,128]{1,0:T(8,128)(2,1)S(1)}, u32[]{:S(2)}, u32[]{:S(2)}) collective-permute-start(bf16[256,128]{1,0:T(8,128)(2,1)S(1)} %get-tuple-element.84), channel_id=1, source_target_pairs={{0,4},{1,5},{2,6},{3,7},{4,0},{5,1},{6,2},{7,3},{8,12},{9,13},{10,... | collective-permute-start | bytes 196616 | tf_op jit(solution)/shard_map/ppermute | solution.py:17
  123.4 9.7 %collective-permute-start.32 = (bf16[256,128]{1,0:T(8,128)(2,1)S(1)}, bf16[256,128]{1,0:T(8,128)(2,1)S(1)}, u32[]{:S(2)}, u32[]{:S(2)}) collective-permute-start(bf16[256,128]{1,0:T(8,128)(2,1)S(1)} %get-tuple-element.85), channel_id=1, source_target_pairs={{0,6},{1,7},{2,4},{3,5},{4,2},{5,3},{6,0},{7,1},{8,14},{9,15},{10,... | collective-permute-start | bytes 196616 | tf_op jit(solution)/shard_map/ppermute | solution.py:17
  125.7 10.3 %collective-permute-start.31 = (bf16[256,128]{1,0:T(8,128)(2,1)S(1)}, bf16[256,128]{1,0:T(8,128)(2,1)S(1)}, u32[]{:S(2)}, u32[]{:S(2)}) collective-permute-start(bf16[256,128]{1,0:T(8,128)(2,1)S(1)} %get-tuple-element.86), channel_id=1, source_target_pairs={{0,5},{1,4},{2,7},{3,6},{4,1},{5,0},{6,3},{7,2},{8,13},{9,12},{10,... | collective-permute-start | bytes 196616 | tf_op jit(solution)/shard_map/ppermute | solution.py:17
  127.0 9.1 %collective-permute-start.30 = (bf16[256,128]{1,0:T(8,128)(2,1)S(1)}, bf16[256,128]{1,0:T(8,128)(2,1)S(1)}, u32[]{:S(2)}, u32[]{:S(2)}) collective-permute-start(bf16[256,128]{1,0:T(8,128)(2,1)S(1)} %get-tuple-element.87), channel_id=1, source_target_pairs={{0,7},{1,6},{2,5},{3,4},{4,3},{5,2},{6,1},{7,0},{8,15},{9,14},{10,... | collective-permute-start | bytes 196616 | tf_op jit(solution)/shard_map/ppermute | solution.py:17
  128.9 7.5 %collective-permute-start.29 = (bf16[256,128]{1,0:T(8,128)(2,1)S(1)}, bf16[256,128]{1,0:T(8,128)(2,1)S(1)}, u32[]{:S(2)}, u32[]{:S(2)}) collective-permute-start(bf16[256,128]{1,0:T(8,128)(2,1)S(1)} %get-tuple-element.88), channel_id=1, source_target_pairs={{0,3},{1,2},{2,1},{3,0},{4,7},{5,6},{6,5},{7,4},{8,11},{9,10},{10,... | collective-permute-start | bytes 196616 | tf_op jit(solution)/shard_map/ppermute | solution.py:17
  (32 other events, 273.6 us)
